TPU v7x, 128 devices: a whole 4x4x4 slice. The times are simulated.
128 devices in a mesh: batch: 8 (over y_hi, z), feat: 16 (over x, y_lo, core).
Axes of the slice: x: 4, y: 4 (y_hi: 2, y_lo: 2; y = y_hi * 2 + y_lo), z: 4, core: 2. Of those that a mesh axis runs over, the one named last changes fastest.
Arguments:
- view_a: bfloat16 [4096, 8192], P('batch', 'feat'), may hold values from -100 to 100
- view_b: bfloat16 [4096, 8192], P('batch', 'feat'), may hold values from -100 to 100
Outputs:
- grad_a: bfloat16 [4096, 8192], P('batch', 'feat')
- grad_b: bfloat16 [4096, 8192], P('batch', 'feat')
- loss: float32 [], replicated
All inputs are finite; a program needn't handle non-finite values.
Results may differ from a plain program's by a relative error of at most 0.0069.
Values may be sent and summed in bfloat16 or wider, within the bound.
No kernel may reach another device: no remote copies, remote signals or barrier semaphores. Data moves between devices by JAX's collectives and lax.ppermute only.
A program may use at most 128 MiB of HBM per device.

v0:
```python
import jax
import jax.numpy as jnp
from jax import lax
from jax.sharding import PartitionSpec as P

D = 8192


def body(view_a, view_b):
    rows_dev = view_a.shape[0]
    groups = lax.axis_size("batch")
    samples_all = rows_dev * groups
    divisor = float(samples_all - 1)
    first = view_a.astype(jnp.float32)
    second = view_b.astype(jnp.float32)
    sum_a, sum_b = lax.psum((jnp.sum(first, axis=0), jnp.sum(second, axis=0)), "batch")
    cent_a = first - sum_a / samples_all
    cent_b = second - sum_b / samples_all
    square_a, square_b = lax.psum(
        (jnp.sum(cent_a * cent_a, axis=0), jnp.sum(cent_b * cent_b, axis=0)), "batch"
    )
    var_a = square_a / divisor
    var_b = square_b / divisor
    std_a = jnp.sqrt(var_a + 0.0001)
    std_b = jnp.sqrt(var_b + 0.0001)
    stacked = jnp.stack([cent_a.astype(jnp.bfloat16), cent_b.astype(jnp.bfloat16)])
    gathered = lax.all_gather(stacked, "batch", axis=1, tiled=True)
    partial_value = jnp.einsum(
        "vnc,vmc->vnm", stacked, gathered, preferred_element_type=jnp.float32
    )
    share_cols = samples_all // lax.axis_size("feat")
    gram = lax.psum(partial_value, "feat")
    own_part = lax.dynamic_slice_in_dim(gram, lax.axis_index("feat") * share_cols, share_cols, 2)
    frobenius = jnp.sum(own_part * own_part)
    gram_low = gram.astype(jnp.bfloat16)
    inner = (
        jnp.einsum("vnm,vmc->vnc", gram_low, gathered, preferred_element_type=jnp.float32) / divisor
    )
    ratio = samples_all / divisor
    term_a = (
        ratio * (inner[0] - cent_a * var_a)
        - 3.125 * ratio * jnp.where(std_a < 1.0, 1.0 / std_a, 0.0) * cent_a
    )
    term_b = (
        ratio * (inner[1] - cent_b * var_b)
        - 3.125 * ratio * jnp.where(std_b < 1.0, 1.0 / std_b, 0.0) * cent_b
    )
    diff = first - second
    column_part = (
        12.5 * (jnp.sum(jax.nn.relu(1.0 - std_a)) + jnp.sum(jax.nn.relu(1.0 - std_b)))
        - jnp.sum(var_a * var_a)
        - jnp.sum(var_b * var_b)
    )
    local_loss = (
        25.0 * jnp.sum(diff * diff) / (samples_all * D)
        + column_part / (D * groups)
        + frobenius / (divisor * divisor * D)
    )
    loss = lax.psum(local_loss, ("batch", "feat"))
    grad_a = (term_a + 12.5 * diff).astype(jnp.bfloat16)
    grad_b = (term_b - 12.5 * diff).astype(jnp.bfloat16)
    return (grad_a, grad_b, loss)


def solution(mesh):
    return jax.shard_map(
        body,
        mesh=mesh,
        in_specs=(P("batch", "feat"), P("batch", "feat")),
        out_specs=(P("batch", "feat"), P("batch", "feat"), P()),
        check_vma=False,
    )
```

profile of v0, /device:TPU:1, one launch (start us, length us, event | category | flops | bytes accessed | tf_op | source)
XLA Modules:
  0.0 602.2 jit_solution(12294598400748726420)
XLA Ops:
  7.2 0.0 all-gather.2.cloned.1.call-start
  7.2 1.2 convert_reduce_fusion
  8.4 1.2 convert_reduce_fusion.1
  9.5 22.7 %all-reduce.1 = (f32[512]{0:T(512)S(1)}, f32[512]{0:T(512)S(1)}) all-reduce(f32[512]{0:T(512)S(1)} %convert_reduce_fusion, f32[512]{0:T(512)S(1)} %convert_reduce_fusion.1), channel_id=1, replica_groups=mesh['batch'=8,'feat'=16] {'batch'}, use_global_device_ids=true, to_apply=%region_3.0 | all-reduce | flops 1024 | bytes 8192 | tf_op jit(solution)/shard_map/psum | solution.py:16
  32.2 2.2 multiply_reduce_fusion.1
  34.4 1.1 pad_maximum_fusion
  35.5 0.0 all-gather.2.cloned.1.call-update
  35.5 0.0 all-reduce.4.cloned.1.call-start
  35.6 107.5 %all-gather.2.cloned.1.call-done = bf16[2,4096,512]{2,1,0:T(8,128)(2,1)} async-done(((bf16[2,512,512]{2,1,0:T(8,128)(2,1)}), bf16[2,4096,512]{2,1,0:T(8,128)(2,1)}) %all-gather.2.cloned.1.call-update) | async-done | bytes 8388624 | tf_op jit(solution)/shard_map/all_gather | solution.py:27
  143.1 11.5 %fusion.30 = f32[2,512,4096]{2,1,0:T(8,128)} fusion(bf16[2,4096,512]{2,1,0:T(8,128)(2,1)} %all-gather.2.cloned.1.call-done, bf16[1,512,512]{2,1,0:T(8,128)(2,1)S(1)} %get-tuple-element.17, bf16[1,512,512]{2,1,0:T(8,128)(2,1)S(1)} %get-tuple-element.16), kind=kOutput, calls=%fused_computation.50 | convolution fusion | flops 4295491584 | bytes 26214400 | tf_op jit(solution)/shard_map/vnc,vmc->vnm/dot_general | solution.py:28
  154.6 0.0 all-reduce.4.cloned.1.call-update
  155.3 26.9 %all-reduce = (f32[512]{0:T(512)S(1)}, f32[512]{0:T(512)S(1)}) all-reduce(f32[512]{0:T(512)S(1)} %get-tuple-element.4, f32[512]{0:T(512)S(1)} %get-tuple-element.5), channel_id=1, replica_groups=mesh['batch'=8,'feat'=16] {'batch'}, use_global_device_ids=true, to_apply=%region_6.0 | all-reduce | flops 1024 | bytes 8192 | tf_op jit(solution)/shard_map/psum | solution.py:19
  182.1 0.6 multiply_reduce_fusion.2
  182.7 0.6 multiply_reduce_fusion.3
  185.8 329.2 %all-reduce.4.cloned.1.call-done = f32[2,512,4096]{2,1,0:T(8,128)} async-done(((f32[2,512,4096]{2,1,0:T(8,128)}), f32[2,512,4096]{2,1,0:T(8,128)}) %all-reduce.4.cloned.1.call-update) | async-done | bytes 16777232 | tf_op jit(solution)/shard_map/psum | solution.py:32
  515.0 2.1 multiply_reduce_fusion
  517.8 65.3 %psum.47 = f32[]{:T(128)} all-reduce(f32[]{:T(128)S(6)} %add.39), channel_id=1, replica_groups=mesh['batch'=8,'feat'=16] {'batch','feat'}, use_global_device_ids=true, to_apply=%region_15.16 | all-reduce | flops 1 | bytes 8 | tf_op jit(solution)/shard_map/psum | solution.py:59
  583.1 0.0 copy-start
  583.1 0.0 copy-start.1
  583.1 10.6 %fusion.2 = f32[2,512,512]{2,1,0:T(8,128)S(1)} fusion(bf16[2,4096,512]{2,1,0:T(8,128)(2,1)} %all-gather.2.cloned.1.call-done, f32[2,512,4096]{2,1,0:T(8,128)} %all-reduce.4.cloned.1.call-done), kind=kOutput, calls=%fused_computation.2 | convolution fusion | flops 4299685888 | bytes 27262976 | tf_op jit(solution)/shard_map/vnm,vmc->vnc/dot_general | solution.py:37
  593.7 0.0 copy-done
  593.7 0.0 copy-done.1
  593.7 1.6 fusion.24
  (1 shorter events, 0.0 us)
Async XLA Ops:
  7.2 135.9 %all-gather.2.cloned.1.call-start = ((), (), s32[]{:S(2)}) async-start(), calls=%async_computation | async-start | bytes 9437184 | tf_op jit(solution)/shard_map/all_gather | solution.py:27
  35.5 479.5 %all-reduce.4.cloned.1.call-start = ((), (), s32[]{:S(2)}) async-start(), calls=%async_computation.1 | async-start | bytes 33554432 | tf_op jit(solution)/shard_map/psum | solution.py:32
  583.1 10.6 %copy-start = (bf16[512,512]{1,0:T(8,128)(2,1)S(1)}, bf16[512,512]{1,0:T(8,128)(2,1)}, u32[]{:S(2)}) copy-start(bf16[512,512]{1,0:T(8,128)(2,1)} %param.3) | copy-start | bytes 1572868
  583.1 10.6 %copy-start.1 = (bf16[512,512]{1,0:T(8,128)(2,1)S(1)}, bf16[512,512]{1,0:T(8,128)(2,1)}, u32[]{:S(2)}) copy-start(bf16[512,512]{1,0:T(8,128)(2,1)} %param.2) | copy-start | bytes 1572868
Sparse Core Ops, SparseCore 0:
  35.7 107.3 all-gather.1
  154.7 360.2 all-reduce.3
where the time goes:
time: 603 us; the launch traced here: 602 us
  waiting for transfers between devices  437 us (72%)
  blocking collectives  115 us (19%)
  matrix products  22.1 us (4%)
  between operations  17.9 us (3%)
  other arithmetic  10.6 us (2%)
    psum x1, waiting for transfers between devices, body(): gram = lax.psum(partial_value, 'feat')  329 us
    all_gather x1, waiting for transfers between devices, body(): gathered = lax.all_gather(stacked, 'batch', axis=1, tiled=True)  108 us
    psum x1, blocking collectives, body(): loss = lax.psum(local_loss, ('batch', 'feat'))  65.3 us
    psum x1, blocking collectives, body(): lax.psum((jnp.sum(cent_a * cent_a, axis=0), jnp.sum(cent_b * cent_b, axis...  26.9 us
    psum x1, blocking collectives, body(): lax.psum((jnp.sum(first, axis=0), jnp.sum(second, axis=0)), 'batch')  22.7 us
  transfers between devices with their start and end apart: 2, of which 2 were waited for; matrix products, arithmetic and copies ran while one was open for 0% of the time, Pallas kernels for 0%

commit v1 on v0

v1 whole, which is shorter than its diff:
```python
import jax
import jax.numpy as jnp
from jax import lax
from jax.sharding import Mesh, PartitionSpec as P

D = 8192
F32 = jnp.float32
BF16 = jnp.bfloat16
AXES = ("yh", "z", "x", "yl", "c")
SIZES = (2, 4, 4, 2, 2)
COUNT = dict(zip(AXES, SIZES, strict=True))


def shift(value, axis, step):
    size = COUNT[axis]
    return lax.ppermute(value, axis, [(i, (i + step) % size) for i in range(size)])


def gather_small(value, axes, size):
    return lax.all_to_all(jnp.broadcast_to(value, (size,) + value.shape), axes, 0, 0)


def nt(lhs, rhs):
    return lax.dot_general(lhs, rhs, (((1,), (1,)), ((), ())), preferred_element_type=F32)


def reduce_gram(part):
    n = part.shape[1]
    pieces = part.astype(BF16).reshape(4, 2, 64, n)
    got = lax.all_to_all(pieces, "x", 0, 0)
    total = jnp.sum(got.astype(F32), axis=0)
    yl = lax.axis_index("yl")
    keep = jnp.where(yl == 0, total[0], total[1])
    send = jnp.where(yl == 0, total[1], total[0]).astype(BF16)
    return keep + shift(send, "yl", 1).astype(F32)


def gather_gram(low):
    n = low.shape[1]
    other = shift(low, "yl", 1)
    first = lax.axis_index("yl") == 0
    pair = jnp.stack([jnp.where(first, low, other), jnp.where(first, other, low)])
    return gather_small(pair, "x", 4).reshape(512, n)


def body(view_a, view_b):
    rows = view_a.shape[0]
    samples = 4096
    divisor = float(samples - 1)
    core0 = lax.axis_index("c") == 0

    got_a = shift(view_a, "c", 1)
    got_b = shift(view_b, "c", 1)
    mine = jnp.concatenate(
        [jnp.where(core0, view_a, view_b), jnp.where(core0, got_a, got_b)], axis=1
    )
    other = jnp.concatenate(
        [jnp.where(core0, view_b, view_a), jnp.where(core0, got_b, got_a)], axis=1
    )

    mine32 = mine.astype(F32)
    local_sum = jnp.sum(mine32, axis=0)
    local_dev = mine32 - local_sum / rows
    local_square = jnp.sum(local_dev * local_dev, axis=0)
    stats = gather_small(jnp.stack([local_sum, local_square]), ("yh", "z"), 8)
    mean = jnp.sum(stats[:, 0], axis=0) / samples
    apart = stats[:, 0] / rows - mean
    square = jnp.sum(stats[:, 1], axis=0) + rows * jnp.sum(apart * apart, axis=0)
    var = square / divisor
    std = jnp.sqrt(var + 0.0001)

    left = shift(mine, "z", 1)
    right = shift(mine, "z", 3)
    partner = shift(mine, "yh", 1)
    far0 = shift(left[:256], "z", 1)
    far1 = shift(right[256:], "z", 3)

    def centre(value):
        return (value.astype(F32) - mean).astype(BF16)

    cent = mine32 - mean
    own = cent.astype(BF16)
    pair = centre(partner)
    half = jnp.concatenate([own, centre(left), centre(right), centre(far0), centre(far1)])

    red_pair = reduce_gram(nt(pair, half))
    red_own = reduce_gram(nt(own, half))
    frobenius = jnp.sum(red_pair * red_pair) + jnp.sum(red_own * red_own)

    gram_pair = gather_gram(red_pair.astype(BF16))
    inner_pair = jnp.dot(gram_pair, half, preferred_element_type=F32)
    from_pair = shift(inner_pair.astype(BF16), "yh", 1)
    gram_own = gather_gram(red_own.astype(BF16))
    inner = jnp.dot(gram_own, half, preferred_element_type=F32)
    inner = (inner + from_pair.astype(F32)) / divisor

    ratio = samples / divisor
    term = (
        ratio * (inner - cent * var)
        - 3.125 * ratio * jnp.where(std < 1.0, 1.0 / std, 0.0) * cent
    )
    grad = (term + 12.5 * (mine32 - other.astype(F32))).astype(BF16)
    cols = view_a.shape[1]
    back = shift(grad[:, cols:], "c", 1)
    grad_a = jnp.where(core0, grad[:, :cols], back)
    grad_b = jnp.where(core0, back, grad[:, :cols])

    diff = view_a.astype(F32) - view_b.astype(F32)
    column_part = 12.5 * jnp.sum(jax.nn.relu(1.0 - std)) - jnp.sum(var * var)
    local_loss = (
        25.0 * jnp.sum(diff * diff) / (samples * D)
        + column_part / (D * 8)
        + frobenius / (divisor * divisor * D)
    )
    tile = jnp.full((8, 128), local_loss, F32)
    tile = jnp.sum(gather_small(tile, ("x", "yl", "c"), 16), axis=0)
    tile = jnp.sum(gather_small(tile, ("yh", "z"), 8), axis=0)
    return grad_a, grad_b, tile[0, 0]


def solution(mesh):
    fine = Mesh(mesh.devices.reshape(SIZES), AXES)
    spec = P(("yh", "z"), ("x", "yl", "c"))
    return jax.shard_map(
        body, mesh=fine, in_specs=(spec, spec), out_specs=(spec, spec, P()), check_vma=False
    )
```

time: 603 us -> 218 us (0.36)
  waiting for transfers between devices: 437 us -> 101 us
  blocking collectives: 115 us -> 35.1 us
  starting transfers between devices: 0.08 us -> 33.6 us
  between operations: 17.9 us -> 4.08 us
  local copies, waits for them, and re-layouts: 0.01 us -> 6.22 us
    psum x1 -> x0, waiting for transfers between devices: 329 us -> none  [body(): gram = lax.psum(partial_value, 'feat')]
    psum x3 -> x0, blocking collectives: 115 us -> none  [the longest x1 65.3 us: body(): loss = lax.psum(local_loss, ('batch', 'feat'))]
    all_gather x1 -> x0, waiting for transfers between devices: 108 us -> none  [body(): gathered = lax.all_gather(stacked, 'batch', axis=1, tiled=True)]
    ppermute x0 -> x13, waiting for transfers between devices: none -> 53.8 us  [shift(): lax.ppermute(value, axis, [(i, (i + step) % size) for i in range(size)])]
    all_to_all x0 -> x4, waiting for transfers between devices: none -> 47.2 us  [the longest x2 29.4 us: reduce_gram(): got = lax.all_to_all(pieces, 'x', 0, 0)]
    all_to_all x0 -> x3, blocking collectives: none -> 35.1 us  [gather_small(): lax.all_to_all(jnp.broadcast_to(value, (size,) + value.shape), axes, 0, 0)]
    ppermute x0 -> x13, starting transfers between devices: none -> 17.6 us  [shift(): lax.ppermute(value, axis, [(i, (i + step) % size) for i in range(size)])]
    all_to_all x0 -> x4, starting transfers between devices: none -> 16 us  [the longest x2 8.36 us: gather_small(): lax.all_to_all(jnp.broadcast_to(value, (size,) + value.shape), axes, 0, 0)]
  transfers between devices with their start and end apart: 2 -> 17, of which waited for: 2 -> 11; matrix products, arithmetic and copies ran while one was open for 0% -> 10% of each run, Pallas kernels for 0% -> 0%
where the time goes in v1:
time: 218 us; the launch traced here: 216 us
  waiting for transfers between devices  101 us (46%)
  blocking collectives  35.1 us (16%)
  starting transfers between devices  33.6 us (15%)
  matrix products  21.7 us (10%)
  other arithmetic  14.7 us (7%)
  local copies, waits for them, and re-layouts  6.22 us (3%)
  between operations  4.08 us (2%)
    ppermute x13, waiting for transfers between devices, shift(): lax.ppermute(value, axis, [(i, (i + step) % size) for i in range(size)])  53.8 us
    all_to_all x3, blocking collectives, gather_small(): lax.all_to_all(jnp.broadcast_to(value, (size,) + value.shape), axes, 0, 0)  35.1 us
    all_to_all x2, waiting for transfers between devices, reduce_gram(): got = lax.all_to_all(pieces, 'x', 0, 0)  29.4 us
    all_to_all x2, waiting for transfers between devices, gather_small(): lax.all_to_all(jnp.broadcast_to(value, (size,) + value.shape), axes, 0, 0)  17.8 us
    ppermute x13, starting transfers between devices, shift(): lax.ppermute(value, axis, [(i, (i + step) % size) for i in range(size)])  17.6 us
    dot_general x2, matrix products, nt(): lax.dot_general(lhs, rhs, (((1,), (1,)), ((), ())), preferred_element_typ...  9.65 us
    all_to_all x2, starting transfers between devices, gather_small(): lax.all_to_all(jnp.broadcast_to(value, (size,) + value.shape), axes, 0, 0)  8.36 us
    all_to_all x2, starting transfers between devices, reduce_gram(): got = lax.all_to_all(pieces, 'x', 0, 0)  7.62 us
  transfers between devices with their start and end apart: 17, of which 11 were waited for; matrix products, arithmetic and copies ran while one was open for 10% of the time, Pallas kernels for 0%

profile of v1, /device:TPU:1, one launch (start us, length us, event | category | flops | bytes accessed | tf_op | source)
XLA Modules:
  0.0 216.4 jit_solution(800729299813178189)
XLA Ops:
  6.0 14.2 %all_to_all.35 = f32[8,2,1024]{2,1,0:T(2,128)S(1)} all-to-all(f32[8,2,1024]{2,1,0:T(2,128)S(1)} %broadcast_in_dim.11), channel_id=1, replica_groups=mesh['yh'=2,'z'=4,'x'=4,'yl'=2,'c'=2] {'yh','z'}, dimensions={0} | all-to-all | bytes 131072 | tf_op jit(solution)/shard_map/all_to_all | solution.py:20
  21.1 2.4 %collective-permute-start.3 = (bf16[512,1024]{1,0:T(8,128)(2,1)S(1)}, bf16[512,1024]{1,0:T(8,128)(2,1)S(1)}, u32[]{:S(2)}, u32[]{:S(2)}) collective-permute-start(bf16[512,1024]{1,0:T(8,128)(2,1)S(1)} %get-tuple-element.18), channel_id=1, source_target_pairs={{0,48},{16,0},{32,16},{48,32},{1,49},{17,1},{33,17},{49,33},{2,50}... | collective-permute-start | bytes 3145736 | tf_op jit(solution)/shard_map/ppermute | solution.py:16
  23.9 21.0 %collective-permute-done.2 = bf16[512,1024]{1,0:T(8,128)(2,1)S(1)} collective-permute-done((bf16[512,1024]{1,0:T(8,128)(2,1)S(1)}, bf16[512,1024]{1,0:T(8,128)(2,1)S(1)}, u32[]{:S(2)}, u32[]{:S(2)}) %collective-permute-start.2) | collective-permute-done | bytes 1048608 | tf_op jit(solution)/shard_map/ppermute | solution.py:16
  45.0 2.7 %collective-permute-start.5 = (bf16[256,1024]{1,0:T(8,128)(2,1)S(1)}, bf16[256,1024]{1,0:T(8,128)(2,1)S(1)}, u32[]{:S(2)}, u32[]{:S(2)}) collective-permute-start(bf16[256,1024]{1,0:T(8,128)(2,1)S(1)} %slice.52), channel_id=1, source_target_pairs={{0,48},{16,0},{32,16},{48,32},{1,49},{17,1},{33,17},{49,33},{2,50}... | collective-permute-start | bytes 1572872 | tf_op jit(solution)/shard_map/ppermute | solution.py:16
  48.3 8.6 %collective-permute-done.4 = bf16[256,1024]{1,0:T(8,128)(2,1)S(1)} collective-permute-done((bf16[256,1024]{1,0:T(8,128)(2,1)S(1)}, bf16[256,1024]{1,0:T(8,128)(2,1)S(1)}, u32[]{:S(2)}, u32[]{:S(2)}) %collective-permute-start.4) | collective-permute-done | bytes 524320 | tf_op jit(solution)/shard_map/ppermute | solution.py:16
  57.1 3.8 %convolution_convert_fusion = bf16[512,2048]{1,0:T(8,128)(2,1)} fusion(bf16[2048,1024]{1,0:T(8,128)(2,1)S(1)} %fusion.17, bf16[512,1024]{1,0:T(8,128)(2,1)S(1)} %collective-permute-done.8, f32[1024]{0:T(1024)S(1)} %broadcast_multiply_fusion), kind=kOutput, calls=%fused_computation.6 | convolution fusion | flops 2150105088 | bytes 7344128 | tf_op jit(solution)/shard_map/dot_general | solution.py:24
  60.9 4.0 %all-to-all-start.3 = ((bf16[4,2,64,2048]{3,2,1,0:T(8,128)(2,1)}), bf16[4,2,64,2048]{3,2,1,0:T(8,128)(2,1)S(1)}, u32[]{:S(2)}, u32[]{:S(2)}) async-start(bf16[4,2,64,2048]{3,2,1,0:T(8,128)(2,1)} %bitcast.45), calls=%async_computation.3 | async-start | bytes 4194304 | tf_op jit(solution)/shard_map/all_to_all | solution.py:30
  64.9 5.9 %convolution_convert_fusion.1 = bf16[512,2048]{1,0:T(8,128)(2,1)} fusion(bf16[2048,1024]{1,0:T(8,128)(2,1)} %copy-done.5, f32[1024]{0:T(1024)S(1)} %broadcast_multiply_fusion, bf16[512,512]{1,0:T(8,128)(2,1)S(1)} %get-tuple-element.17, bf16[512,512]{1,0:T(8,128)(2,1)S(1)} %get-tuple-element.15), kind=kOutput, calls=%fused_computation.7 | convolution fusion | flops 2151677952 | bytes 7344128 | tf_op jit(solution)/shard_map/dot_general | solution.py:24
  70.8 16.5 %all-to-all-done.3 = bf16[4,2,64,2048]{3,2,1,0:T(8,128)(2,1)S(1)} async-done(((bf16[4,2,64,2048]{3,2,1,0:T(8,128)(2,1)}), bf16[4,2,64,2048]{3,2,1,0:T(8,128)(2,1)S(1)}, u32[]{:S(2)}, u32[]{:S(2)}) %all-to-all-start.3) | async-done | bytes 2097184 | tf_op jit(solution)/shard_map/all_to_all | solution.py:30
  88.7 3.6 %all-to-all-start.1 = ((bf16[4,2,64,2048]{3,2,1,0:T(8,128)(2,1)}), bf16[4,2,64,2048]{3,2,1,0:T(8,128)(2,1)S(1)}, u32[]{:S(2)}, u32[]{:S(2)}) async-start(bf16[4,2,64,2048]{3,2,1,0:T(8,128)(2,1)} %bitcast.43), calls=%async_computation.1 | async-start | bytes 4194304 | tf_op jit(solution)/shard_map/all_to_all | solution.py:30
  94.9 4.8 %collective-permute-done.9 = bf16[64,2048]{1,0:T(8,128)(2,1)S(1)} collective-permute-done((bf16[64,2048]{1,0:T(8,128)(2,1)S(1)}, bf16[64,2048]{1,0:T(8,128)(2,1)S(1)}, u32[]{:S(2)}, u32[]{:S(2)}) %collective-permute-start.9) | collective-permute-done | bytes 262176 | tf_op jit(solution)/shard_map/ppermute | solution.py:16
  100.9 12.8 %all-to-all-done.1 = bf16[4,2,64,2048]{3,2,1,0:T(8,128)(2,1)S(1)} async-done(((bf16[4,2,64,2048]{3,2,1,0:T(8,128)(2,1)}), bf16[4,2,64,2048]{3,2,1,0:T(8,128)(2,1)S(1)}, u32[]{:S(2)}, u32[]{:S(2)}) %all-to-all-start.1) | async-done | bytes 2097184 | tf_op jit(solution)/shard_map/all_to_all | solution.py:30
  117.9 4.6 %all-to-all-start.4 = ((bf16[4,2,64,2048]{3,2,1,0:T(8,128)(2,1)}), bf16[4,2,64,2048]{3,2,1,0:T(8,128)(2,1)}, u32[]{:S(2)}, u32[]{:S(2)}) async-start(bf16[4,2,64,2048]{3,2,1,0:T(8,128)(2,1)} %broadcast_in_dim.14), calls=%async_computation.4 | async-start | bytes 4194304 | tf_op jit(solution)/shard_map/all_to_all | solution.py:20
  123.0 4.8 %collective-permute-done.6 = bf16[64,2048]{1,0:T(8,128)(2,1)S(1)} collective-permute-done((bf16[64,2048]{1,0:T(8,128)(2,1)S(1)}, bf16[64,2048]{1,0:T(8,128)(2,1)S(1)}, u32[]{:S(2)}, u32[]{:S(2)}) %collective-permute-start.6) | collective-permute-done | bytes 262176 | tf_op jit(solution)/shard_map/ppermute | solution.py:16
  129.0 7.8 %collective-permute-done.7 = bf16[64,2048]{1,0:T(8,128)(2,1)S(1)} collective-permute-done((bf16[64,2048]{1,0:T(8,128)(2,1)S(1)}, bf16[64,2048]{1,0:T(8,128)(2,1)S(1)}, u32[]{:S(2)}, u32[]{:S(2)}) %collective-permute-start.7) | collective-permute-done | bytes 262176 | tf_op jit(solution)/shard_map/ppermute | solution.py:16
  137.0 5.9 %all-to-all-done.4 = bf16[4,2,64,2048]{3,2,1,0:T(8,128)(2,1)} async-done(((bf16[4,2,64,2048]{3,2,1,0:T(8,128)(2,1)}), bf16[4,2,64,2048]{3,2,1,0:T(8,128)(2,1)}, u32[]{:S(2)}, u32[]{:S(2)}) %all-to-all-start.4) | async-done | bytes 2097184 | tf_op jit(solution)/shard_map/all_to_all | solution.py:20
  144.4 3.8 %all-to-all-start.2 = ((bf16[4,2,64,2048]{3,2,1,0:T(8,128)(2,1)}), bf16[4,2,64,2048]{3,2,1,0:T(8,128)(2,1)S(1)}, u32[]{:S(2)}, u32[]{:S(2)}) async-start(bf16[4,2,64,2048]{3,2,1,0:T(8,128)(2,1)} %broadcast_in_dim.12), calls=%async_computation.2 | async-start | bytes 4194304 | tf_op jit(solution)/shard_map/all_to_all | solution.py:20
  148.2 6.2 %convolution_convert_fusion.2 = bf16[512,1024]{1,0:T(8,128)(2,1)} fusion(bf16[512,2048]{1,0:T(8,128)(2,1)} %bitcast.13, bf16[2048,1024]{1,0:T(8,128)(2,1)} %copy-done.5), kind=kOutput, calls=%fused_computation.22 | convolution fusion | flops 2148007936 | bytes 7340032 | tf_op jit(solution)/shard_map/dot_general | solution.py:91
  155.6 12.0 %all-to-all-done.2 = bf16[4,2,64,2048]{3,2,1,0:T(8,128)(2,1)S(1)} async-done(((bf16[4,2,64,2048]{3,2,1,0:T(8,128)(2,1)}), bf16[4,2,64,2048]{3,2,1,0:T(8,128)(2,1)S(1)}, u32[]{:S(2)}, u32[]{:S(2)}) %all-to-all-start.2) | async-done | bytes 2097184 | tf_op jit(solution)/shard_map/all_to_all | solution.py:20
  167.5 6.4 %collective-permute-done.11 = bf16[512,1024]{1,0:T(8,128)(2,1)} collective-permute-done((bf16[512,1024]{1,0:T(8,128)(2,1)}, bf16[512,1024]{1,0:T(8,128)(2,1)}, u32[]{:S(2)}, u32[]{:S(2)}) %collective-permute-start.11) | collective-permute-done | bytes 1048608 | tf_op jit(solution)/shard_map/ppermute | solution.py:16
  174.0 5.8 %fusion.7 = bf16[512,1024]{1,0:T(8,128)(2,1)S(1)} fusion(bf16[512,1024]{1,0:T(8,128)(2,1)} %collective-permute-done.11, bf16[512,512]{1,0:T(8,128)(2,1)} %get-tuple-element.16, bf16[512,512]{1,0:T(8,128)(2,1)} %get-tuple-element.14, f32[1024]{0:T(1024)S(1)} %select_multiply_fusion, f32[1024]{0:T(1024)S(1)} %get-tuple-element.7, ...), kind=kOutput, calls=%fused_computation.15 | convolution fusion | flops 2158493696 | bytes 10498048 | tf_op jit(solution)/shard_map/dot_general | solution.py:94
  180.8 8.0 %collective-permute-start.12 = (bf16[512,512]{1,0:T(8,128)(2,1)S(1)}, bf16[512,512]{1,0:T(8,128)(2,1)S(1)}, u32[]{:S(2)}, u32[]{:S(2)}) collective-permute-start(bf16[512,512]{1,0:T(8,128)(2,1)S(1)} %slice.59), channel_id=1, source_target_pairs={{0,1},{1,0},{2,3},{3,2},{4,5},{5,4},{6,7},{7,6},{8,9},{9,8},{10,11... | collective-permute-start | bytes 1572872 | tf_op jit(solution)/shard_map/ppermute | solution.py:16
  192.9 10.2 %all_to_all.36 = f32[16,8,128]{2,1,0:T(8,128)S(1)} all-to-all(f32[16,8,128]{2,1,0:T(8,128)S(1)} %broadcast_in_dim_broadcast_in_dim.3), channel_id=1, replica_groups=mesh['yh'=2,'z'=4,'x'=4,'yl'=2,'c'=2] {'x','yl','c'}, dimensions={0} | all-to-all | bytes 131072 | tf_op jit(solution)/shard_map/all_to_all | solution.py:20
  203.1 10.6 %all_to_all.37 = f32[8,8,128]{2,1,0:T(8,128)S(1)} all-to-all(f32[8,8,128]{2,1,0:T(8,128)S(1)} %broadcast_in_dim.30), channel_id=1, replica_groups=mesh['yh'=2,'z'=4,'x'=4,'yl'=2,'c'=2] {'yh','z'}, dimensions={0} | all-to-all | bytes 65536 | tf_op jit(solution)/shard_map/all_to_all | solution.py:20
  (68 shorter events, 25.7 us)
Async XLA Ops:
  0.6 3.7 %collective-permute-start = (bf16[512,512]{1,0:T(8,128)(2,1)}, bf16[512,512]{1,0:T(8,128)(2,1)S(1)}, u32[]{:S(2)}, u32[]{:S(2)}) collective-permute-start(bf16[512,512]{1,0:T(8,128)(2,1)} %param.2), channel_id=1, source_target_pairs={{0,1},{1,0},{2,3},{3,2},{4,5},{5,4},{6,7},{7,6},{8,9},{9,8},{10,11... | collective-permute-start | bytes 1572872 | tf_op jit(solution)/shard_map/ppermute | solution.py:16
  2.1 2.5 %collective-permute-start.1 = (bf16[512,512]{1,0:T(8,128)(2,1)}, bf16[512,512]{1,0:T(8,128)(2,1)S(1)}, u32[]{:S(2)}, u32[]{:S(2)}) collective-permute-start(bf16[512,512]{1,0:T(8,128)(2,1)} %param.3), channel_id=1, source_target_pairs={{0,1},{1,0},{2,3},{3,2},{4,5},{5,4},{6,7},{7,6},{8,9},{9,8},{10,11... | collective-permute-start | bytes 1572872 | tf_op jit(solution)/shard_map/ppermute | solution.py:16
  20.7 24.1 %collective-permute-start.2 = (bf16[512,1024]{1,0:T(8,128)(2,1)S(1)}, bf16[512,1024]{1,0:T(8,128)(2,1)S(1)}, u32[]{:S(2)}, u32[]{:S(2)}) collective-permute-start(bf16[512,1024]{1,0:T(8,128)(2,1)S(1)} %get-tuple-element.18), channel_id=1, source_target_pairs={{0,16},{16,32},{32,48},{48,0},{1,17},{17,33},{33,49},{49,1},{2,18}... | collective-permute-start | bytes 3145736 | tf_op jit(solution)/shard_map/ppermute | solution.py:16
  21.1 23.9 %collective-permute-start.3 = (bf16[512,1024]{1,0:T(8,128)(2,1)S(1)}, bf16[512,1024]{1,0:T(8,128)(2,1)S(1)}, u32[]{:S(2)}, u32[]{:S(2)}) collective-permute-start(bf16[512,1024]{1,0:T(8,128)(2,1)S(1)} %get-tuple-element.18), channel_id=1, source_target_pairs={{0,48},{16,0},{32,16},{48,32},{1,49},{17,1},{33,17},{49,33},{2,50}... | collective-permute-start | bytes 3145736 | tf_op jit(solution)/shard_map/ppermute | solution.py:16
  23.5 33.6 %collective-permute-start.8 = (bf16[512,1024]{1,0:T(8,128)(2,1)S(1)}, bf16[512,1024]{1,0:T(8,128)(2,1)S(1)}, u32[]{:S(2)}, u32[]{:S(2)}) collective-permute-start(bf16[512,1024]{1,0:T(8,128)(2,1)S(1)} %get-tuple-element.18), channel_id=1, source_target_pairs={{0,64},{64,0},{1,65},{65,1},{2,66},{66,2},{3,67},{67,3},{4,68},{68... | collective-permute-start | bytes 3145736 | tf_op jit(solution)/shard_map/ppermute | solution.py:16
  44.9 12.0 %collective-permute-start.4 = (bf16[256,1024]{1,0:T(8,128)(2,1)S(1)}, bf16[256,1024]{1,0:T(8,128)(2,1)S(1)}, u32[]{:S(2)}, u32[]{:S(2)}) collective-permute-start(bf16[256,1024]{1,0:T(8,128)(2,1)S(1)} %slice.51), channel_id=1, source_target_pairs={{0,16},{16,32},{32,48},{48,0},{1,17},{17,33},{33,49},{49,1},{2,18}... | collective-permute-start | bytes 1572872 | tf_op jit(solution)/shard_map/ppermute | solution.py:16
  45.0 11.9 %collective-permute-start.5 = (bf16[256,1024]{1,0:T(8,128)(2,1)S(1)}, bf16[256,1024]{1,0:T(8,128)(2,1)S(1)}, u32[]{:S(2)}, u32[]{:S(2)}) collective-permute-start(bf16[256,1024]{1,0:T(8,128)(2,1)S(1)} %slice.52), channel_id=1, source_target_pairs={{0,48},{16,0},{32,16},{48,32},{1,49},{17,1},{33,17},{49,33},{2,50}... | collective-permute-start | bytes 1572872 | tf_op jit(solution)/shard_map/ppermute | solution.py:16
  57.1 3.8 %copy-start.5 = (bf16[2048,1024]{1,0:T(8,128)(2,1)}, bf16[2048,1024]{1,0:T(8,128)(2,1)S(1)}, u32[]{:S(2)}) copy-start(bf16[2048,1024]{1,0:T(8,128)(2,1)S(1)} %fusion.17) | copy-start | bytes 12582916
  60.9 26.5 %all-to-all-start.3 = ((bf16[4,2,64,2048]{3,2,1,0:T(8,128)(2,1)}), bf16[4,2,64,2048]{3,2,1,0:T(8,128)(2,1)S(1)}, u32[]{:S(2)}, u32[]{:S(2)}) async-start(bf16[4,2,64,2048]{3,2,1,0:T(8,128)(2,1)} %bitcast.45), calls=%async_computation.3 | async-start | bytes 4194304 | tf_op jit(solution)/shard_map/all_to_all | solution.py:30
  87.3 1.3 copy-start
  88.7 25.1 %all-to-all-start.1 = ((bf16[4,2,64,2048]{3,2,1,0:T(8,128)(2,1)}), bf16[4,2,64,2048]{3,2,1,0:T(8,128)(2,1)S(1)}, u32[]{:S(2)}, u32[]{:S(2)}) async-start(bf16[4,2,64,2048]{3,2,1,0:T(8,128)(2,1)} %bitcast.43), calls=%async_computation.1 | async-start | bytes 4194304 | tf_op jit(solution)/shard_map/all_to_all | solution.py:30
  94.5 5.3 %collective-permute-start.9 = (bf16[64,2048]{1,0:T(8,128)(2,1)S(1)}, bf16[64,2048]{1,0:T(8,128)(2,1)S(1)}, u32[]{:S(2)}, u32[]{:S(2)}) collective-permute-start(bf16[64,2048]{1,0:T(8,128)(2,1)S(1)} %fusion.19), channel_id=1, source_target_pairs={{0,2},{2,0},{1,3},{3,1},{4,6},{6,4},{5,7},{7,5},{8,10},{10,8},{9,1... | collective-permute-start | bytes 786440 | tf_op jit(solution)/shard_map/ppermute | solution.py:16
  100.5 14.7 %collective-permute-start.10 = (bf16[64,2048]{1,0:T(8,128)(2,1)S(1)}, bf16[64,2048]{1,0:T(8,128)(2,1)}, u32[]{:S(2)}, u32[]{:S(2)}) collective-permute-start(bf16[64,2048]{1,0:T(8,128)(2,1)S(1)} %get-tuple-element.13), channel_id=1, source_target_pairs={{0,2},{2,0},{1,3},{3,1},{4,6},{6,4},{5,7},{7,5},{8,10},{10,8},{9,1... | collective-permute-start | bytes 786440 | tf_op jit(solution)/shard_map/ppermute | solution.py:16
  117.9 4.6 %copy-start.1 = (f32[2,64,2048]{2,1,0:T(8,128)S(1)}, f32[2,64,2048]{2,1,0:T(8,128)}, u32[]{:S(2)}) copy-start(f32[2,64,2048]{2,1,0:T(8,128)} %convert_reduce_fusion.1) | copy-start | bytes 3145732
  117.9 24.9 %all-to-all-start.4 = ((bf16[4,2,64,2048]{3,2,1,0:T(8,128)(2,1)}), bf16[4,2,64,2048]{3,2,1,0:T(8,128)(2,1)}, u32[]{:S(2)}, u32[]{:S(2)}) async-start(bf16[4,2,64,2048]{3,2,1,0:T(8,128)(2,1)} %broadcast_in_dim.14), calls=%async_computation.4 | async-start | bytes 4194304 | tf_op jit(solution)/shard_map/all_to_all | solution.py:20
  122.5 5.3 %collective-permute-start.6 = (bf16[64,2048]{1,0:T(8,128)(2,1)S(1)}, bf16[64,2048]{1,0:T(8,128)(2,1)S(1)}, u32[]{:S(2)}, u32[]{:S(2)}) collective-permute-start(bf16[64,2048]{1,0:T(8,128)(2,1)S(1)} %fusion.18), channel_id=1, source_target_pairs={{0,2},{2,0},{1,3},{3,1},{4,6},{6,4},{5,7},{7,5},{8,10},{10,8},{9,1... | collective-permute-start | bytes 786440 | tf_op jit(solution)/shard_map/ppermute | solution.py:16
  128.6 8.2 %collective-permute-start.7 = (bf16[64,2048]{1,0:T(8,128)(2,1)S(1)}, bf16[64,2048]{1,0:T(8,128)(2,1)S(1)}, u32[]{:S(2)}, u32[]{:S(2)}) collective-permute-start(bf16[64,2048]{1,0:T(8,128)(2,1)S(1)} %get-tuple-element.11), channel_id=1, source_target_pairs={{0,2},{2,0},{1,3},{3,1},{4,6},{6,4},{5,7},{7,5},{8,10},{10,8},{9,1... | collective-permute-start | bytes 786440 | tf_op jit(solution)/shard_map/ppermute | solution.py:16
  144.4 23.1 %all-to-all-start.2 = ((bf16[4,2,64,2048]{3,2,1,0:T(8,128)(2,1)}), bf16[4,2,64,2048]{3,2,1,0:T(8,128)(2,1)S(1)}, u32[]{:S(2)}, u32[]{:S(2)}) async-start(bf16[4,2,64,2048]{3,2,1,0:T(8,128)(2,1)} %broadcast_in_dim.12), calls=%async_computation.2 | async-start | bytes 4194304 | tf_op jit(solution)/shard_map/all_to_all | solution.py:20
  154.5 19.5 %collective-permute-start.11 = (bf16[512,1024]{1,0:T(8,128)(2,1)}, bf16[512,1024]{1,0:T(8,128)(2,1)}, u32[]{:S(2)}, u32[]{:S(2)}) collective-permute-start(bf16[512,1024]{1,0:T(8,128)(2,1)} %convolution_convert_fusion.2), channel_id=1, source_target_pairs={{0,64},{64,0},{1,65},{65,1},{2,66},{66,2},{3,67},{67,3},{4,68},{68... | collective-permute-start | bytes 3145736 | tf_op jit(solution)/shard_map/ppermute | solution.py:16
  174.0 14.9 %copy-start.2 = (bf16[512,512]{1,0:T(8,128)(2,1)S(1)}, bf16[512,512]{1,0:T(8,128)(2,1)}, u32[]{:S(2)}) copy-start(bf16[512,512]{1,0:T(8,128)(2,1)} %param.3) | copy-start | bytes 1572868
  174.0 14.9 %copy-start.3 = (bf16[512,512]{1,0:T(8,128)(2,1)S(1)}, bf16[512,512]{1,0:T(8,128)(2,1)}, u32[]{:S(2)}) copy-start(bf16[512,512]{1,0:T(8,128)(2,1)} %param.2) | copy-start | bytes 1572868
  179.8 1.0 copy-start.4
  180.8 33.5 %collective-permute-start.12 = (bf16[512,512]{1,0:T(8,128)(2,1)S(1)}, bf16[512,512]{1,0:T(8,128)(2,1)S(1)}, u32[]{:S(2)}, u32[]{:S(2)}) collective-permute-start(bf16[512,512]{1,0:T(8,128)(2,1)S(1)} %slice.59), channel_id=1, source_target_pairs={{0,1},{1,0},{2,3},{3,2},{4,5},{5,4},{6,7},{7,6},{8,9},{9,8},{10,11... | collective-permute-start | bytes 1572872 | tf_op jit(solution)/shard_map/ppermute | solution.py:16

commit v2 on v1

v2 whole, which is shorter than its diff:
```python
import jax
import jax.numpy as jnp
from jax import lax
from jax.sharding import Mesh, PartitionSpec as P

D = 8192
F32 = jnp.float32
BF16 = jnp.bfloat16
AXES = ("yh", "z", "x", "yl", "c")
SIZES = (2, 4, 4, 2, 2)
COUNT = dict(zip(AXES, SIZES, strict=True))


def shift(value, axis, step):
    size = COUNT[axis]
    return lax.ppermute(value, axis, [(i, (i + step) % size) for i in range(size)])


def gather_small(value, axes, size):
    return lax.all_to_all(jnp.broadcast_to(value, (size,) + value.shape), axes, 0, 0)


def swap(value, axis, mask):
    return lax.ppermute(value, axis, [(i, i ^ mask) for i in range(COUNT[axis])])


def batch_shift(value, half, step):
    pairs = [(4 * y + z, 4 * (y ^ half) + (z + step) % 4) for y in range(2) for z in range(4)]
    return lax.ppermute(value, ("yh", "z"), pairs)


def nt(lhs, rhs):
    return lax.dot_general(lhs, rhs, (((1,), (1,)), ((), ())), preferred_element_type=F32)


def send_gram(part):
    pieces = part.reshape(8, part.shape[0] // 8, part.shape[1])
    return lax.all_to_all(pieces, ("x", "yl"), 0, 0)


def sum_gram(got):
    return jnp.sum(got.astype(F32), axis=0)


def spread_gram(low):
    other = shift(low, "yl", 1)
    first = lax.axis_index("yl") == 0
    return jnp.stack([jnp.where(first, low, other), jnp.where(first, other, low)])


def gather_gram(both):
    n = both.shape[2]
    prev = shift(both, "x", 1)
    succ = shift(both, "x", 3)
    far0 = shift(prev[0], "x", 1)
    far1 = shift(succ[1], "x", 3)
    x = lax.axis_index("x")
    rows = jnp.zeros((4, 2, 64, n), BF16)
    for step, block in ((0, both), (3, prev), (1, succ), (2, jnp.stack([far0, far1]))):
        rows = lax.dynamic_update_slice_in_dim(rows, block[None], (x + step) % 4, 0)
    return rows.reshape(512, n), prev


def merge(stats, axis, mask, held):
    apart = swap(stats, axis, mask)
    gap = (stats[0] - apart[0]) / held
    return jnp.stack([stats[0] + apart[0], stats[1] + apart[1] + gap * gap * (held / 2)])


def body(view_a, view_b):
    rows = view_a.shape[0]
    samples = 4096
    divisor = float(samples - 1)
    core0 = lax.axis_index("c") == 0

    got_a = shift(view_a, "c", 1)
    got_b = shift(view_b, "c", 1)
    mine = jnp.concatenate(
        [jnp.where(core0, view_a, view_b), jnp.where(core0, got_a, got_b)], axis=1
    )
    other = jnp.concatenate(
        [jnp.where(core0, view_b, view_a), jnp.where(core0, got_b, got_a)], axis=1
    )

    mine32 = mine.astype(F32)
    local_sum = jnp.sum(mine32, axis=0)
    local_dev = mine32 - local_sum / rows
    local_square = jnp.sum(local_dev * local_dev, axis=0)
    stats = jnp.stack([local_sum, local_square])
    stats = merge(merge(stats, "z", 1, 512.0), "z", 3, 1024.0)
    ring, stats = lax.optimization_barrier((mine, stats))
    stats = merge(stats, "yh", 1, 2048.0)
    sent, stats = lax.optimization_barrier((mine, stats))
    mean = stats[0] / samples
    var = stats[1] / divisor
    std = jnp.sqrt(var + 0.0001)

    left = shift(ring, "z", 1)
    right = shift(ring, "z", 3)
    partner = shift(sent, "yh", 1)
    far0 = shift(left[:256], "z", 1)
    far1 = shift(right[256:], "z", 3)

    def centre(value, mean):
        return (value.astype(F32) - mean).astype(BF16)

    cent = mine32 - mean
    own = cent.astype(BF16)
    pair = centre(partner, mean)
    near = jnp.concatenate([own, centre(right, mean)])
    far0, far1, mean1 = lax.optimization_barrier((far0, far1, mean))
    far = jnp.concatenate([centre(far0, mean1), centre(far1, mean1)])

    got_near = send_gram(nt(pair, near).astype(BF16))
    rows = jnp.stack([pair.reshape(8, 64, 1024), own.reshape(8, 64, 1024)], axis=1)
    part_far = nt(rows.reshape(1024, 1024), far).astype(BF16)
    part_own, got_near, mean2, left = lax.optimization_barrier(
        (nt(own, near).astype(BF16), got_near, mean1, left)
    )
    got_own = send_gram(part_own)
    part_far, got_own = lax.optimization_barrier((part_far, got_own))
    got_far = send_gram(part_far)
    before = centre(left, mean2)

    red_near = sum_gram(got_near)
    low_near = red_near.astype(BF16)
    turned_near = batch_shift(low_near[:, 512:], 1, 1)
    got_far, turned_near = lax.optimization_barrier((got_far, turned_near))
    red_far = sum_gram(got_far)
    low_far = red_far.astype(BF16)
    low_pair = jnp.concatenate([low_near, low_far[:64], turned_near], axis=1)
    both_pair = spread_gram(low_pair)
    red_own = sum_gram(got_own)
    low_own = red_own.astype(BF16)
    turned_own = batch_shift(low_own[:, 512:], 0, 1)
    low_own = jnp.concatenate([low_own, low_far[64:], turned_own], axis=1)

    def lanes(value):
        return jnp.sum(value.reshape(-1, 128), axis=0)

    def rows_of(value):
        return lanes(jnp.sum(value, axis=0))

    frobenius = rows_of(red_far * red_far) + sum(
        rows_of(red[:, :512] * red[:, :512]) + 2.0 * rows_of(red[:, 512:] * red[:, 512:])
        for red in (red_near, red_own)
    )
    diff = view_a.astype(F32) - view_b.astype(F32)
    column_part = lanes(12.5 * jax.nn.relu(1.0 - std) - var * var)
    loss = (
        rows_of(diff * diff) * (25.0 / (samples * D))
        + column_part * (1.0 / (D * 8))
        + frobenius * (1.0 / (divisor * divisor * D))
    )
    high = lax.reduce_precision(loss, 8, 7)
    middle = lax.reduce_precision(loss - high, 8, 7)
    low = loss - high - middle
    line = lax.broadcasted_iota(jnp.int32, (64, 128), 0)
    loss = jnp.where(line == 0, high, jnp.where(line == 1, middle, jnp.where(line == 2, low, 0.0)))
    low_own = jnp.concatenate([low_own, loss.astype(BF16)], axis=1)

    def times(gram):
        return (
            jnp.dot(gram[:, :1024], near, preferred_element_type=F32)
            + jnp.dot(gram[:, 1024:1536], far, preferred_element_type=F32)
            + lax.dot_general(
                gram[:, 1536:2048], before, (((0,), (0,)), ((), ())), preferred_element_type=F32
            )
        )

    gram_pair, came = gather_gram(both_pair)
    inner_pair = times(gram_pair).astype(BF16)
    from_pair = shift(inner_pair, "yh", 1)
    both_own, _ = lax.optimization_barrier((spread_gram(low_own), came))
    gram_own, _ = gather_gram(both_own)
    loss = jnp.sum(gram_own.reshape(8, 64, 2176)[:, :3, 2048:].astype(F32), axis=(0, 1))
    loss = jnp.broadcast_to(loss, (8, 128))
    for axis, mask in (("z", 1), ("z", 3), ("c", 1)):
        loss = loss + swap(loss, axis, mask)
    from_pair, loss = lax.optimization_barrier((from_pair, loss))
    loss = loss + swap(loss, "yh", 1)
    inner = (times(gram_own) + from_pair.astype(F32)) / divisor

    ratio = samples / divisor
    term = (
        ratio * (inner - cent * var)
        - 3.125 * ratio * jnp.where(std < 1.0, 1.0 / std, 0.0) * cent
    )
    grad = (term + 12.5 * (mine32 - other.astype(F32))).astype(BF16)
    cols = view_a.shape[1]
    back = shift(grad[:, cols:], "c", 1)
    grad_a = jnp.where(core0, grad[:, :cols], back)
    grad_b = jnp.where(core0, back, grad[:, :cols])

    return grad_a, grad_b, jnp.sum(loss[0])


def solution(mesh):
    fine = Mesh(mesh.devices.reshape(SIZES), AXES)
    spec = P(("yh", "z"), ("x", "yl", "c"))
    return jax.shard_map(
        body, mesh=fine, in_specs=(spec, spec), out_specs=(spec, spec, P()), check_vma=False
    )
```

time: 218 us -> 174 us (0.80)
  blocking collectives: 35.1 us -> 0 us
  starting transfers between devices: 33.6 us -> 61 us
  waiting for transfers between devices: 101 us -> 78.4 us
  matrix products: 21.7 us -> 12.3 us
  between operations: 4.08 us -> 1.27 us
    all_to_all x4 -> x3, waiting for transfers between devices: 47.2 us -> 12 us  [send_gram(): return lax.all_to_all(pieces, ('x', 'yl'), 0, 0)]
    all_to_all x3 -> x0, blocking collectives: 35.1 us -> none  [gather_small(): lax.all_to_all(jnp.broadcast_to(value, (size,) + value.shape), axes, 0, 0)]
    ppermute x0 -> x9, starting transfers between devices: none -> 25.6 us  [the longest x7 25.5 us: swap(): lax.ppermute(value, axis, [(i, i ^ mask) for i in range(COUNT[axis])])]
    ppermute x0 -> x9, waiting for transfers between devices: none -> 11.9 us  [the longest x7 6.9 us: swap(): lax.ppermute(value, axis, [(i, i ^ mask) for i in range(COUNT[axis])])]
    dot_general x2 -> x6, matrix products: 12.1 us -> 5.46 us  [the longest x2 2.51 us: times(): jnp.dot(gram[:, :1024], near, preferred_element_type=F32)]
    convert_element_type x2 -> x7, other arithmetic: 0.1 us -> 3.66 us  [the longest x2 2.11 us: centre(): return (value.astype(F32) - mean).astype(BF16)]
    dot_general x2 -> x3, matrix products: 9.65 us -> 6.84 us  [nt(): lax.dot_general(lhs, rhs, (((1,), (1,)), ((), ())), preferred_element_typ...]
    reduce_sum x10 -> x14, other arithmetic: 6.77 us -> 4.02 us  [the longest x3 2.98 us: sum_gram(): return jnp.sum(got.astype(F32), axis=0)]
  transfers between devices with their start and end apart: 17 -> 31, of which waited for: 11 -> 18; matrix products, arithmetic and copies ran while one was open for 10% -> 15% of each run, Pallas kernels for 0% -> 0%
where the time goes in v2:
time: 174 us; the launch traced here: 173 us
  waiting for transfers between devices  78.4 us (45%)
  starting transfers between devices  61 us (35%)
  other arithmetic  14.2 us (8%)
  matrix products  12.3 us (7%)
  local copies, waits for them, and re-layouts  5.68 us (3%)
    ppermute x19, waiting for transfers between devices, shift(): lax.ppermute(value, axis, [(i, (i + step) % size) for i in range(size)])  54.4 us
    ppermute x7, starting transfers between devices, swap(): lax.ppermute(value, axis, [(i, i ^ mask) for i in range(COUNT[axis])])  25.5 us
    ppermute x19, starting transfers between devices, shift(): lax.ppermute(value, axis, [(i, (i + step) % size) for i in range(size)])  19.7 us
    all_to_all x3, starting transfers between devices, send_gram(): return lax.all_to_all(pieces, ('x', 'yl'), 0, 0)  15.6 us
    all_to_all x3, waiting for transfers between devices, send_gram(): return lax.all_to_all(pieces, ('x', 'yl'), 0, 0)  12 us
    ppermute x7, waiting for transfers between devices, swap(): lax.ppermute(value, axis, [(i, i ^ mask) for i in range(COUNT[axis])])  6.9 us
    dot_general x3, matrix products, nt(): lax.dot_general(lhs, rhs, (((1,), (1,)), ((), ())), preferred_element_typ...  6.84 us
    ppermute x2, waiting for transfers between devices, batch_shift(): return lax.ppermute(value, ('yh', 'z'), pairs)  5.05 us
  transfers between devices with their start and end apart: 31, of which 18 were waited for; matrix products, arithmetic and copies ran while one was open for 15% of the time, Pallas kernels for 0%

profile of v2, /device:TPU:1, one launch (start us, length us, event | category | flops | bytes accessed | tf_op | source)
XLA Modules:
  0.0 172.8 jit_solution(9761436131192130059)
XLA Ops:
  8.9 3.7 %collective-permute-start.3 = (f32[2,1024]{1,0:T(2,128)S(1)}, f32[2,1024]{1,0:T(2,128)S(1)}, u32[]{:S(2)}, u32[]{:S(2)}) collective-permute-start(f32[2,1024]{1,0:T(2,128)S(1)} %pad_maximum_fusion.16), channel_id=1, source_target_pairs={{0,48},{16,32},{32,16},{48,0},{1,49},{17,33},{33,17},{49,1},{2,50}... | collective-permute-start | bytes 24584 | tf_op jit(solution)/shard_map/ppermute | solution.py:24
  13.7 3.0 %collective-permute-start.4 = (f32[2,1024]{1,0:T(2,128)S(1)}, f32[2,1024]{1,0:T(2,128)S(1)}, u32[]{:S(2)}, u32[]{:S(2)}) collective-permute-start(f32[2,1024]{1,0:T(2,128)S(1)} %pad_maximum_fusion.17), channel_id=1, source_target_pairs={{0,64},{64,0},{1,65},{65,1},{2,66},{66,2},{3,67},{67,3},{4,68},{68... | collective-permute-start | bytes 24584 | tf_op jit(solution)/shard_map/ppermute | solution.py:24
  16.7 2.6 %collective-permute-start.8 = (bf16[512,1024]{1,0:T(8,128)(2,1)}, bf16[512,1024]{1,0:T(8,128)(2,1)S(1)}, u32[]{:S(2)}, u32[]{:S(2)}) collective-permute-start(bf16[512,1024]{1,0:T(8,128)(2,1)} %pad_maximum_fusion.2), channel_id=1, source_target_pairs={{0,48},{16,0},{32,16},{48,32},{1,49},{17,1},{33,17},{49,33},{2,50}... | collective-permute-start | bytes 3145736 | tf_op jit(solution)/shard_map/ppermute | solution.py:16
  20.9 18.2 %collective-permute-done.8 = bf16[512,1024]{1,0:T(8,128)(2,1)S(1)} collective-permute-done((bf16[512,1024]{1,0:T(8,128)(2,1)}, bf16[512,1024]{1,0:T(8,128)(2,1)S(1)}, u32[]{:S(2)}, u32[]{:S(2)}) %collective-permute-start.8) | collective-permute-done | bytes 1048608 | tf_op jit(solution)/shard_map/ppermute | solution.py:16
  39.1 3.4 %collective-permute-done.5 = bf16[512,1024]{1,0:T(8,128)(2,1)S(1)} collective-permute-done((bf16[512,1024]{1,0:T(8,128)(2,1)}, bf16[512,1024]{1,0:T(8,128)(2,1)S(1)}, u32[]{:S(2)}, u32[]{:S(2)}) %collective-permute-start.5) | collective-permute-done | bytes 1048608 | tf_op jit(solution)/shard_map/ppermute | solution.py:16
  43.4 2.3 %convolution_convert_fusion = bf16[512,1024]{1,0:T(8,128)(2,1)} fusion(bf16[512,1024]{1,0:T(8,128)(2,1)S(1)} %get-tuple-element.71, bf16[512,1024]{1,0:T(8,128)(2,1)S(1)} %get-tuple-element.69, bf16[512,1024]{1,0:T(8,128)(2,1)S(1)} %get-tuple-element.70), kind=kOutput, calls=%fused_computation.25 | convolution fusion | flops 1078460416 | bytes 4194304 | tf_op jit(solution)/shard_map/dot_general | solution.py:33
  45.7 4.1 %all-to-all-start = ((bf16[8,64,1024]{2,1,0:T(8,128)(2,1)}), bf16[8,64,1024]{2,1,0:T(8,128)(2,1)S(1)}, u32[]{:S(2)}, u32[]{:S(2)}) async-start(bf16[8,64,1024]{2,1,0:T(8,128)(2,1)} %bitcast.89), calls=%async_computation | async-start | bytes 2097152 | tf_op jit(solution)/shard_map/all_to_all | solution.py:38
  56.4 3.9 %collective-permute-done.7 = bf16[256,1024]{1,0:T(8,128)(2,1)S(1)} collective-permute-done((bf16[256,1024]{1,0:T(8,128)(2,1)S(1)}, bf16[256,1024]{1,0:T(8,128)(2,1)S(1)}, u32[]{:S(2)}, u32[]{:S(2)}) %collective-permute-start.7) | collective-permute-done | bytes 524320 | tf_op jit(solution)/shard_map/ppermute | solution.py:16
  61.5 5.8 %all-to-all-start.1 = ((bf16[8,64,1024]{2,1,0:T(8,128)(2,1)}), bf16[8,64,1024]{2,1,0:T(8,128)(2,1)}, u32[]{:S(2)}, u32[]{:S(2)}) async-start(bf16[8,64,1024]{2,1,0:T(8,128)(2,1)} %bitcast.90), calls=%async_computation.1 | async-start | bytes 2097152 | tf_op jit(solution)/shard_map/all_to_all | solution.py:38
  70.9 2.3 %convolution_convert_fusion.2 = bf16[1024,512]{1,0:T(8,128)(2,1)} fusion(bf16[1024,1024]{1,0:T(8,128)(2,1)S(1)} %bitcast.87, bf16[256,1024]{1,0:T(8,128)(2,1)S(1)} %get-tuple-element.73, bf16[256,1024]{1,0:T(8,128)(2,1)S(1)} %get-tuple-element.72), kind=kOutput, calls=%fused_computation.27 | convolution fusion | flops 1076363264 | bytes 4194304 | tf_op jit(solution)/shard_map/dot_general | solution.py:33
  73.2 5.9 %all-to-all-done.1 = bf16[8,64,1024]{2,1,0:T(8,128)(2,1)} async-done(((bf16[8,64,1024]{2,1,0:T(8,128)(2,1)}), bf16[8,64,1024]{2,1,0:T(8,128)(2,1)}, u32[]{:S(2)}, u32[]{:S(2)}) %all-to-all-start.1) | async-done | bytes 1048608 | tf_op jit(solution)/shard_map/all_to_all | solution.py:38
  79.1 5.7 %all-to-all-start.2 = ((bf16[8,128,512]{2,1,0:T(8,128)(2,1)}), bf16[8,128,512]{2,1,0:T(8,128)(2,1)}, u32[]{:S(2)}, u32[]{:S(2)}) async-start(bf16[8,128,512]{2,1,0:T(8,128)(2,1)} %bitcast.88), calls=%async_computation.2 | async-start | bytes 2097152 | tf_op jit(solution)/shard_map/all_to_all | solution.py:38
  86.8 5.0 %collective-permute-done.10 = bf16[64,512]{1,0:T(8,128)(2,1)S(1)} collective-permute-done((bf16[64,512]{1,0:T(8,128)(2,1)S(1)}, bf16[64,512]{1,0:T(8,128)(2,1)S(1)}, u32[]{:S(2)}, u32[]{:S(2)}) %collective-permute-start.10) | collective-permute-done | bytes 65568 | tf_op jit(solution)/shard_map/ppermute | solution.py:29
  91.9 5.6 %all-to-all-done.2 = bf16[8,128,512]{2,1,0:T(8,128)(2,1)} async-done(((bf16[8,128,512]{2,1,0:T(8,128)(2,1)}), bf16[8,128,512]{2,1,0:T(8,128)(2,1)}, u32[]{:S(2)}, u32[]{:S(2)}) %all-to-all-start.2) | async-done | bytes 1048608 | tf_op jit(solution)/shard_map/all_to_all | solution.py:38
  101.0 3.3 %collective-permute-done.13 = bf16[64,2048]{1,0:T(8,128)(2,1)S(1)} collective-permute-done((bf16[64,2048]{1,0:T(8,128)(2,1)S(1)}, bf16[64,2048]{1,0:T(8,128)(2,1)S(1)}, u32[]{:S(2)}, u32[]{:S(2)}) %collective-permute-start.13) | collective-permute-done | bytes 262176 | tf_op jit(solution)/shard_map/ppermute | solution.py:16
  104.9 2.3 %collective-permute-start.19 = (bf16[2,64,2048]{2,1,0:T(8,128)(2,1)S(1)}, bf16[2,64,2048]{2,1,0:T(8,128)(2,1)S(1)}, u32[]{:S(2)}, u32[]{:S(2)}) collective-permute-start(bf16[2,64,2048]{2,1,0:T(8,128)(2,1)S(1)} %pad_maximum_fusion.5), channel_id=1, source_target_pairs={{0,12},{4,0},{8,4},{12,8},{1,13},{5,1},{9,5},{13,9},{2,14},{6,2},{... | collective-permute-start | bytes 1572872 | tf_op jit(solution)/shard_map/ppermute | solution.py:16
  109.1 4.7 %collective-permute-done.14 = bf16[2,64,2048]{2,1,0:T(8,128)(2,1)S(1)} collective-permute-done((bf16[2,64,2048]{2,1,0:T(8,128)(2,1)S(1)}, bf16[2,64,2048]{2,1,0:T(8,128)(2,1)S(1)}, u32[]{:S(2)}, u32[]{:S(2)}) %collective-permute-start.14) | collective-permute-done | bytes 524320 | tf_op jit(solution)/shard_map/ppermute | solution.py:16
  113.8 2.6 %collective-permute-start.16 = (bf16[2,64,2176]{2,1,0:T(8,128)(2,1)S(1)}, bf16[2,64,2176]{2,1,0:T(8,128)(2,1)S(1)}, u32[]{:S(2)}, u32[]{:S(2)}) collective-permute-start(bf16[2,64,2176]{2,1,0:T(8,128)(2,1)S(1)} %pad_maximum_fusion.4), channel_id=1, source_target_pairs={{0,12},{4,0},{8,4},{12,8},{1,13},{5,1},{9,5},{13,9},{2,14},{6,2},{... | collective-permute-start | bytes 1671176 | tf_op jit(solution)/shard_map/ppermute | solution.py:16
  118.6 12.7 %collective-permute-done.21 = bf16[64,2048]{1,0:T(8,128)(2,1)S(1)} collective-permute-done((bf16[64,2048]{1,0:T(8,128)(2,1)S(1)}, bf16[64,2048]{1,0:T(8,128)(2,1)S(1)}, u32[]{:S(2)}, u32[]{:S(2)}) %collective-permute-start.21) | collective-permute-done | bytes 262176 | tf_op jit(solution)/shard_map/ppermute | solution.py:16
  137.2 4.6 %collective-permute-done.18 = bf16[64,2176]{1,0:T(8,128)(2,1)S(1)} collective-permute-done((bf16[64,2176]{1,0:T(8,128)(2,1)S(1)}, bf16[64,2176]{1,0:T(8,128)(2,1)S(1)}, u32[]{:S(2)}, u32[]{:S(2)}) %collective-permute-start.18) | collective-permute-done | bytes 278560 | tf_op jit(solution)/shard_map/ppermute | solution.py:16
  143.8 8.4 %collective-permute-start.23 = (f32[8,128]{1,0:T(8,128)S(1)}, f32[8,128]{1,0:T(8,128)S(1)}, u32[]{:S(2)}, u32[]{:S(2)}) collective-permute-start(f32[8,128]{1,0:T(8,128)S(1)} %broadcast_in_dim.73), channel_id=1, source_target_pairs={{0,16},{16,0},{32,48},{48,32},{1,17},{17,1},{33,49},{49,33},{2,18}... | collective-permute-start | bytes 12296 | tf_op jit(solution)/shard_map/ppermute | solution.py:24
  154.3 3.2 %collective-permute-done.24 = f32[8,128]{1,0:T(8,128)S(1)} collective-permute-done((f32[8,128]{1,0:T(8,128)S(1)}, f32[8,128]{1,0:T(8,128)S(1)}, u32[]{:S(2)}, u32[]{:S(2)}) %collective-permute-start.24) | collective-permute-done | bytes 4128 | tf_op jit(solution)/shard_map/ppermute | solution.py:24
  157.6 7.1 %collective-permute-start.25 = (f32[8,128]{1,0:T(8,128)S(1)}, f32[8,128]{1,0:T(8,128)S(1)}, u32[]{:S(2)}, u32[]{:S(2)}) collective-permute-start(f32[8,128]{1,0:T(8,128)S(1)} %fusion.44), channel_id=1, source_target_pairs={{0,1},{1,0},{2,3},{3,2},{4,5},{5,4},{6,7},{7,6},{8,9},{9,8},{10,11... | collective-permute-start | bytes 12296 | tf_op jit(solution)/shard_map/ppermute | solution.py:24
  168.6 2.5 %collective-permute-done.27 = f32[8,128]{1,0:T(8,128)S(1)} collective-permute-done((f32[8,128]{1,0:T(8,128)S(1)}, f32[8,128]{1,0:T(8,128)S(1)}, u32[]{:S(2)}, u32[]{:S(2)}) %collective-permute-start.27) | collective-permute-done | bytes 4128 | tf_op jit(solution)/shard_map/ppermute | solution.py:24
  (154 shorter events, 48.5 us)
Async XLA Ops:
  13.7 5.6 %collective-permute-start.4 = (f32[2,1024]{1,0:T(2,128)S(1)}, f32[2,1024]{1,0:T(2,128)S(1)}, u32[]{:S(2)}, u32[]{:S(2)}) collective-permute-start(f32[2,1024]{1,0:T(2,128)S(1)} %pad_maximum_fusion.17), channel_id=1, source_target_pairs={{0,64},{64,0},{1,65},{65,1},{2,66},{66,2},{3,67},{67,3},{4,68},{68... | collective-permute-start | bytes 24584 | tf_op jit(solution)/shard_map/ppermute | solution.py:24
  16.7 22.4 %collective-permute-start.8 = (bf16[512,1024]{1,0:T(8,128)(2,1)}, bf16[512,1024]{1,0:T(8,128)(2,1)S(1)}, u32[]{:S(2)}, u32[]{:S(2)}) collective-permute-start(bf16[512,1024]{1,0:T(8,128)(2,1)} %pad_maximum_fusion.2), channel_id=1, source_target_pairs={{0,48},{16,0},{32,16},{48,32},{1,49},{17,1},{33,17},{49,33},{2,50}... | collective-permute-start | bytes 3145736 | tf_op jit(solution)/shard_map/ppermute | solution.py:16
  19.3 23.2 %collective-permute-start.5 = (bf16[512,1024]{1,0:T(8,128)(2,1)}, bf16[512,1024]{1,0:T(8,128)(2,1)S(1)}, u32[]{:S(2)}, u32[]{:S(2)}) collective-permute-start(bf16[512,1024]{1,0:T(8,128)(2,1)} %pad_maximum_fusion.2), channel_id=1, source_target_pairs={{0,64},{64,0},{1,65},{65,1},{2,66},{66,2},{3,67},{67,3},{4,68},{68... | collective-permute-start | bytes 3145736 | tf_op jit(solution)/shard_map/ppermute | solution.py:16
  20.9 29.1 %collective-permute-start.6 = (bf16[512,1024]{1,0:T(8,128)(2,1)}, bf16[512,1024]{1,0:T(8,128)(2,1)S(1)}, u32[]{:S(2)}, u32[]{:S(2)}) collective-permute-start(bf16[512,1024]{1,0:T(8,128)(2,1)} %pad_maximum_fusion.2), channel_id=1, source_target_pairs={{0,16},{16,32},{32,48},{48,0},{1,17},{17,33},{33,49},{49,1},{2,18}... | collective-permute-start | bytes 3145736 | tf_op jit(solution)/shard_map/ppermute | solution.py:16
  45.7 15.8 %all-to-all-start = ((bf16[8,64,1024]{2,1,0:T(8,128)(2,1)}), bf16[8,64,1024]{2,1,0:T(8,128)(2,1)S(1)}, u32[]{:S(2)}, u32[]{:S(2)}) async-start(bf16[8,64,1024]{2,1,0:T(8,128)(2,1)} %bitcast.89), calls=%async_computation | async-start | bytes 2097152 | tf_op jit(solution)/shard_map/all_to_all | solution.py:38
  50.0 10.3 %collective-permute-start.7 = (bf16[256,1024]{1,0:T(8,128)(2,1)S(1)}, bf16[256,1024]{1,0:T(8,128)(2,1)S(1)}, u32[]{:S(2)}, u32[]{:S(2)}) collective-permute-start(bf16[256,1024]{1,0:T(8,128)(2,1)S(1)} %slice.151), channel_id=1, source_target_pairs={{0,16},{16,32},{32,48},{48,0},{1,17},{17,33},{33,49},{49,1},{2,18}... | collective-permute-start | bytes 1572872 | tf_op jit(solution)/shard_map/ppermute | solution.py:16
  51.6 9.4 %collective-permute-start.9 = (bf16[256,1024]{1,0:T(8,128)(2,1)S(1)}, bf16[256,1024]{1,0:T(8,128)(2,1)}, u32[]{:S(2)}, u32[]{:S(2)}) collective-permute-start(bf16[256,1024]{1,0:T(8,128)(2,1)S(1)} %slice.152), channel_id=1, source_target_pairs={{0,48},{16,0},{32,16},{48,32},{1,49},{17,1},{33,17},{49,33},{2,50}... | collective-permute-start | bytes 1572872 | tf_op jit(solution)/shard_map/ppermute | solution.py:16
  61.5 17.5 %all-to-all-start.1 = ((bf16[8,64,1024]{2,1,0:T(8,128)(2,1)}), bf16[8,64,1024]{2,1,0:T(8,128)(2,1)}, u32[]{:S(2)}, u32[]{:S(2)}) async-start(bf16[8,64,1024]{2,1,0:T(8,128)(2,1)} %bitcast.90), calls=%async_computation.1 | async-start | bytes 2097152 | tf_op jit(solution)/shard_map/all_to_all | solution.py:38
  79.1 18.4 %all-to-all-start.2 = ((bf16[8,128,512]{2,1,0:T(8,128)(2,1)}), bf16[8,128,512]{2,1,0:T(8,128)(2,1)}, u32[]{:S(2)}, u32[]{:S(2)}) async-start(bf16[8,128,512]{2,1,0:T(8,128)(2,1)} %bitcast.88), calls=%async_computation.2 | async-start | bytes 2097152 | tf_op jit(solution)/shard_map/all_to_all | solution.py:38
  85.1 6.8 %collective-permute-start.10 = (bf16[64,512]{1,0:T(8,128)(2,1)S(1)}, bf16[64,512]{1,0:T(8,128)(2,1)S(1)}, u32[]{:S(2)}, u32[]{:S(2)}) collective-permute-start(bf16[64,512]{1,0:T(8,128)(2,1)S(1)} %slice.153), channel_id=1, source_target_pairs={{0,80},{16,96},{32,112},{48,64},{64,16},{80,32},{96,48},{112,0},{1... | collective-permute-start | bytes 196616 | tf_op jit(solution)/shard_map/ppermute | solution.py:29
  86.7 12.7 %collective-permute-start.11 = (bf16[64,512]{1,0:T(8,128)(2,1)S(1)}, bf16[64,512]{1,0:T(8,128)(2,1)S(1)}, u32[]{:S(2)}, u32[]{:S(2)}) collective-permute-start(bf16[64,512]{1,0:T(8,128)(2,1)S(1)} %slice.155), channel_id=1, source_target_pairs={{0,16},{16,32},{32,48},{48,0},{64,80},{80,96},{96,112},{112,64},{1... | collective-permute-start | bytes 196616 | tf_op jit(solution)/shard_map/ppermute | solution.py:29
  99.0 5.3 %collective-permute-start.13 = (bf16[64,2048]{1,0:T(8,128)(2,1)S(1)}, bf16[64,2048]{1,0:T(8,128)(2,1)S(1)}, u32[]{:S(2)}, u32[]{:S(2)}) collective-permute-start(bf16[64,2048]{1,0:T(8,128)(2,1)S(1)} %pad_maximum_fusion.14), channel_id=1, source_target_pairs={{0,2},{2,0},{1,3},{3,1},{4,6},{6,4},{5,7},{7,5},{8,10},{10,8},{9,1... | collective-permute-start | bytes 786440 | tf_op jit(solution)/shard_map/ppermute | solution.py:16
  99.4 9.5 %collective-permute-start.12 = (bf16[64,2176]{1,0:T(8,128)(2,1)S(1)}, bf16[64,2176]{1,0:T(8,128)(2,1)S(1)}, u32[]{:S(2)}, u32[]{:S(2)}) collective-permute-start(bf16[64,2176]{1,0:T(8,128)(2,1)S(1)} %pad_maximum_fusion.13), channel_id=1, source_target_pairs={{0,2},{2,0},{1,3},{3,1},{4,6},{6,4},{5,7},{7,5},{8,10},{10,8},{9,1... | collective-permute-start | bytes 835592 | tf_op jit(solution)/shard_map/ppermute | solution.py:16
  104.5 9.3 %collective-permute-start.14 = (bf16[2,64,2048]{2,1,0:T(8,128)(2,1)S(1)}, bf16[2,64,2048]{2,1,0:T(8,128)(2,1)S(1)}, u32[]{:S(2)}, u32[]{:S(2)}) collective-permute-start(bf16[2,64,2048]{2,1,0:T(8,128)(2,1)S(1)} %pad_maximum_fusion.5), channel_id=1, source_target_pairs={{0,4},{4,8},{8,12},{12,0},{1,5},{5,9},{9,13},{13,1},{2,6},{6,10},{... | collective-permute-start | bytes 1572872 | tf_op jit(solution)/shard_map/ppermute | solution.py:16
  104.9 11.5 %collective-permute-start.19 = (bf16[2,64,2048]{2,1,0:T(8,128)(2,1)S(1)}, bf16[2,64,2048]{2,1,0:T(8,128)(2,1)S(1)}, u32[]{:S(2)}, u32[]{:S(2)}) collective-permute-start(bf16[2,64,2048]{2,1,0:T(8,128)(2,1)S(1)} %pad_maximum_fusion.5), channel_id=1, source_target_pairs={{0,12},{4,0},{8,4},{12,8},{1,13},{5,1},{9,5},{13,9},{2,14},{6,2},{... | collective-permute-start | bytes 1572872 | tf_op jit(solution)/shard_map/ppermute | solution.py:16
  113.8 23.2 %collective-permute-start.15 = (bf16[2,64,2176]{2,1,0:T(8,128)(2,1)S(1)}, bf16[2,64,2176]{2,1,0:T(8,128)(2,1)S(1)}, u32[]{:S(2)}, u32[]{:S(2)}) collective-permute-start(bf16[2,64,2176]{2,1,0:T(8,128)(2,1)S(1)} %pad_maximum_fusion.4), channel_id=1, source_target_pairs={{0,4},{4,8},{8,12},{12,0},{1,5},{5,9},{9,13},{13,1},{2,6},{6,10},{... | collective-permute-start | bytes 1671176 | tf_op jit(solution)/shard_map/ppermute | solution.py:16
  113.8 20.8 %collective-permute-start.16 = (bf16[2,64,2176]{2,1,0:T(8,128)(2,1)S(1)}, bf16[2,64,2176]{2,1,0:T(8,128)(2,1)S(1)}, u32[]{:S(2)}, u32[]{:S(2)}) collective-permute-start(bf16[2,64,2176]{2,1,0:T(8,128)(2,1)S(1)} %pad_maximum_fusion.4), channel_id=1, source_target_pairs={{0,12},{4,0},{8,4},{12,8},{1,13},{5,1},{9,5},{13,9},{2,14},{6,2},{... | collective-permute-start | bytes 1671176 | tf_op jit(solution)/shard_map/ppermute | solution.py:16
  116.5 14.8 %collective-permute-start.21 = (bf16[64,2048]{1,0:T(8,128)(2,1)S(1)}, bf16[64,2048]{1,0:T(8,128)(2,1)S(1)}, u32[]{:S(2)}, u32[]{:S(2)}) collective-permute-start(bf16[64,2048]{1,0:T(8,128)(2,1)S(1)} %slice_bitcast_fusion.2), channel_id=1, source_target_pairs={{0,12},{4,0},{8,4},{12,8},{1,13},{5,1},{9,5},{13,9},{2,14},{6,2},{... | collective-permute-start | bytes 786440 | tf_op jit(solution)/shard_map/ppermute | solution.py:16
  116.7 14.5 %collective-permute-start.20 = (bf16[64,2048]{1,0:T(8,128)(2,1)S(1)}, bf16[64,2048]{1,0:T(8,128)(2,1)S(1)}, u32[]{:S(2)}, u32[]{:S(2)}) collective-permute-start(bf16[64,2048]{1,0:T(8,128)(2,1)S(1)} %slice_bitcast_fusion.3), channel_id=1, source_target_pairs={{0,4},{4,8},{8,12},{12,0},{1,5},{5,9},{9,13},{13,1},{2,6},{6,10},{... | collective-permute-start | bytes 786440 | tf_op jit(solution)/shard_map/ppermute | solution.py:16
  134.6 30.9 %collective-permute-start.22 = (bf16[512,1024]{1,0:T(8,128)(2,1)S(1)}, bf16[512,1024]{1,0:T(8,128)(2,1)S(1)}, u32[]{:S(2)}, u32[]{:S(2)}) collective-permute-start(bf16[512,1024]{1,0:T(8,128)(2,1)S(1)} %add_convert_fusion), channel_id=1, source_target_pairs={{0,64},{64,0},{1,65},{65,1},{2,66},{66,2},{3,67},{67,3},{4,68},{68... | collective-permute-start | bytes 3145736 | tf_op jit(solution)/shard_map/ppermute | solution.py:16
  134.7 7.1 %collective-permute-start.18 = (bf16[64,2176]{1,0:T(8,128)(2,1)S(1)}, bf16[64,2176]{1,0:T(8,128)(2,1)S(1)}, u32[]{:S(2)}, u32[]{:S(2)}) collective-permute-start(bf16[64,2176]{1,0:T(8,128)(2,1)S(1)} %slice_bitcast_fusion), channel_id=1, source_target_pairs={{0,12},{4,0},{8,4},{12,8},{1,13},{5,1},{9,5},{13,9},{2,14},{6,2},{... | collective-permute-start | bytes 835592 | tf_op jit(solution)/shard_map/ppermute | solution.py:16
  137.0 6.7 %collective-permute-start.17 = (bf16[64,2176]{1,0:T(8,128)(2,1)S(1)}, bf16[64,2176]{1,0:T(8,128)(2,1)S(1)}, u32[]{:S(2)}, u32[]{:S(2)}) collective-permute-start(bf16[64,2176]{1,0:T(8,128)(2,1)S(1)} %slice_bitcast_fusion.1), channel_id=1, source_target_pairs={{0,4},{4,8},{8,12},{12,0},{1,5},{5,9},{9,13},{13,1},{2,6},{6,10},{... | collective-permute-start | bytes 835592 | tf_op jit(solution)/shard_map/ppermute | solution.py:16
  143.8 9.7 %collective-permute-start.23 = (f32[8,128]{1,0:T(8,128)S(1)}, f32[8,128]{1,0:T(8,128)S(1)}, u32[]{:S(2)}, u32[]{:S(2)}) collective-permute-start(f32[8,128]{1,0:T(8,128)S(1)} %broadcast_in_dim.73), channel_id=1, source_target_pairs={{0,16},{16,0},{32,48},{48,32},{1,17},{17,1},{33,49},{49,33},{2,18}... | collective-permute-start | bytes 12296 | tf_op jit(solution)/shard_map/ppermute | solution.py:24
  157.6 7.9 %collective-permute-start.25 = (f32[8,128]{1,0:T(8,128)S(1)}, f32[8,128]{1,0:T(8,128)S(1)}, u32[]{:S(2)}, u32[]{:S(2)}) collective-permute-start(f32[8,128]{1,0:T(8,128)S(1)} %fusion.44), channel_id=1, source_target_pairs={{0,1},{1,0},{2,3},{3,2},{4,5},{5,4},{6,7},{7,6},{8,9},{9,8},{10,11... | collective-permute-start | bytes 12296 | tf_op jit(solution)/shard_map/ppermute | solution.py:24
  (24 other events, 106.8 us)

commit v3 on v2

--- a/solution.py
+++ b/solution.py
@@ -87,7 +87,11 @@
     local_dev = mine32 - local_sum / rows
     local_square = jnp.sum(local_dev * local_dev, axis=0)
     stats = jnp.stack([local_sum, local_square])
-    stats = merge(merge(stats, "z", 1, 512.0), "z", 3, 1024.0)
+    everyone = [stats] + [shift(stats, "z", step) for step in (1, 3, 2)]
+    total = sum(one[0] for one in everyone)
+    gaps = [one[0] / 512.0 - total / 2048.0 for one in everyone]
+    spread = sum(one[1] + 512.0 * gap * gap for one, gap in zip(everyone, gaps, strict=True))
+    stats = jnp.stack([total, spread])
     ring, stats = lax.optimization_barrier((mine, stats))
     stats = merge(stats, "yh", 1, 2048.0)
     sent, stats = lax.optimization_barrier((mine, stats))
@@ -106,21 +110,22 @@
 
     cent = mine32 - mean
     own = cent.astype(BF16)
-    pair = centre(partner, mean)
-    near = jnp.concatenate([own, centre(right, mean)])
-    far0, far1, mean1 = lax.optimization_barrier((far0, far1, mean))
+    part = nt(own, own).astype(BF16).reshape(4, 128, 512)
+    got_self = lax.all_to_all(part, "x", 0, 0)
+    partner, right, mean0, got_self = lax.optimization_barrier((partner, right, mean, got_self))
+    pair = centre(partner, mean0)
+    after = centre(right, mean0)
+    near = jnp.concatenate([own, after])
+    far0, far1, mean1 = lax.optimization_barrier((far0, far1, mean0))
     far = jnp.concatenate([centre(far0, mean1), centre(far1, mean1)])
-
-    got_near = send_gram(nt(pair, near).astype(BF16))
     rows = jnp.stack([pair.reshape(8, 64, 1024), own.reshape(8, 64, 1024)], axis=1)
     part_far = nt(rows.reshape(1024, 1024), far).astype(BF16)
-    part_own, got_near, mean2, left = lax.optimization_barrier(
-        (nt(own, near).astype(BF16), got_near, mean1, left)
-    )
-    got_own = send_gram(part_own)
-    part_far, got_own = lax.optimization_barrier((part_far, got_own))
+    part = jnp.concatenate([nt(pair, near), nt(own, after)], axis=1).astype(BF16)
+    got_near = send_gram(part)
+    part_far, got_near, mean2, left = lax.optimization_barrier((part_far, got_near, mean1, left))
     got_far = send_gram(part_far)
     before = centre(left, mean2)
+    got_near, got_own = got_near[:, :, :1024], got_near[:, :, 1024:]
 
     red_near = sum_gram(got_near)
     low_near = red_near.astype(BF16)
@@ -130,10 +135,15 @@
     low_far = red_far.astype(BF16)
     low_pair = jnp.concatenate([low_near, low_far[:64], turned_near], axis=1)
     both_pair = spread_gram(low_pair)
-    red_own = sum_gram(got_own)
+    red_self, red_own = sum_gram(got_self), sum_gram(got_own)
+    even = lax.axis_index("yl") == 0
+    rest = jnp.where(even, red_self[64:], red_self[:64]).astype(BF16)
+    red_self = jnp.where(even, red_self[:64], red_self[64:]) + shift(rest, "yl", 1).astype(F32)
     low_own = red_own.astype(BF16)
-    turned_own = batch_shift(low_own[:, 512:], 0, 1)
-    low_own = jnp.concatenate([low_own, low_far[64:], turned_own], axis=1)
+    turned_own = batch_shift(low_own, 0, 1)
+    low_own = jnp.concatenate(
+        [red_self.astype(BF16), low_own, low_far[64:], turned_own], axis=1
+    )
 
     def lanes(value):
         return jnp.sum(value.reshape(-1, 128), axis=0)
@@ -141,9 +151,11 @@
     def rows_of(value):
         return lanes(jnp.sum(value, axis=0))
 
-    frobenius = rows_of(red_far * red_far) + sum(
-        rows_of(red[:, :512] * red[:, :512]) + 2.0 * rows_of(red[:, 512:] * red[:, 512:])
-        for red in (red_near, red_own)
+    frobenius = (
+        rows_of(red_far * red_far)
+        + rows_of(red_self * red_self)
+        + rows_of(red_near[:, :512] * red_near[:, :512])
+        + 2.0 * rows_of(red_near[:, 512:] * red_near[:, 512:] + red_own * red_own)
     )
     diff = view_a.astype(F32) - view_b.astype(F32)
     column_part = lanes(12.5 * jax.nn.relu(1.0 - std) - var * var)
@@ -157,40 +169,52 @@
     low = loss - high - middle
     line = lax.broadcasted_iota(jnp.int32, (64, 128), 0)
     loss = jnp.where(line == 0, high, jnp.where(line == 1, middle, jnp.where(line == 2, low, 0.0)))
-    low_own = jnp.concatenate([low_own, loss.astype(BF16)], axis=1)
-
-    def times(gram):
-        return (
-            jnp.dot(gram[:, :1024], near, preferred_element_type=F32)
-            + jnp.dot(gram[:, 1024:1536], far, preferred_element_type=F32)
-            + lax.dot_general(
-                gram[:, 1536:2048], before, (((0,), (0,)), ((), ())), preferred_element_type=F32
-            )
+    first = lax.axis_index("yl") == 0
+    zeros = jnp.zeros((64, 128), BF16)
+    loss = loss.astype(BF16)
+    loss = jnp.stack([jnp.where(first, loss, zeros), jnp.where(first, zeros, loss)])
+    both_pair = jnp.concatenate([both_pair, loss], axis=2)
+
+    three = jnp.concatenate([near, far])
+
+    def times(gram, start, stop):
+        return jnp.dot(
+            gram[:, :1536], three[:, start:stop], preferred_element_type=F32
+        ) + lax.dot_general(
+            gram[:, 1536:2048],
+            before[:, start:stop],
+            (((0,), (0,)), ((), ())),
+            preferred_element_type=F32,
         )
 
     gram_pair, came = gather_gram(both_pair)
-    inner_pair = times(gram_pair).astype(BF16)
+    cols = view_a.shape[1]
+    inner_pair = times(gram_pair, 0, 2 * cols).astype(BF16)
     from_pair = shift(inner_pair, "yh", 1)
     both_own, _ = lax.optimization_barrier((spread_gram(low_own), came))
-    gram_own, _ = gather_gram(both_own)
-    loss = jnp.sum(gram_own.reshape(8, 64, 2176)[:, :3, 2048:].astype(F32), axis=(0, 1))
+    gram_own, came = gather_gram(both_own)
+    loss = jnp.sum(gram_pair.reshape(8, 64, 2176)[:, :3, 2048:].astype(F32), axis=(0, 1))
     loss = jnp.broadcast_to(loss, (8, 128))
-    for axis, mask in (("z", 1), ("z", 3), ("c", 1)):
+    loss, _ = lax.optimization_barrier((loss, came))
+    for axis, mask in (("yl", 1), ("z", 1), ("z", 3), ("c", 1), ("yh", 1)):
         loss = loss + swap(loss, axis, mask)
+
+    ratio = samples / divisor
+    weight = 3.125 * ratio * jnp.where(std < 1.0, 1.0 / std, 0.0)
+
+    def gradient(got, start, stop):
+        inner = (times(gram_own, start, stop) + got.astype(F32)) / divisor
+        own_cols = cent[:, start:stop]
+        term = ratio * (inner - own_cols * var[start:stop]) - weight[start:stop] * own_cols
+        diff = mine32[:, start:stop] - other[:, start:stop].astype(F32)
+        return (term + 12.5 * diff).astype(BF16)
+
     from_pair, loss = lax.optimization_barrier((from_pair, loss))
-    loss = loss + swap(loss, "yh", 1)
-    inner = (times(gram_own) + from_pair.astype(F32)) / divisor
-
-    ratio = samples / divisor
-    term = (
-        ratio * (inner - cent * var)
-        - 3.125 * ratio * jnp.where(std < 1.0, 1.0 / std, 0.0) * cent
-    )
-    grad = (term + 12.5 * (mine32 - other.astype(F32))).astype(BF16)
-    cols = view_a.shape[1]
+    grad = gradient(from_pair, 0, 2 * cols)
     back = shift(grad[:, cols:], "c", 1)
-    grad_a = jnp.where(core0, grad[:, :cols], back)
-    grad_b = jnp.where(core0, back, grad[:, :cols])
+    keep = grad[:, :cols]
+    grad_a = jnp.where(core0, keep, back)
+    grad_b = jnp.where(core0, back, keep)
 
     return grad_a, grad_b, jnp.sum(loss[0])
 

time: 174 us -> 169 us (0.971); the launches traced: 173 us -> 166 us
  waiting for transfers between devices: 78.4 us -> 60.4 us
  starting transfers between devices: 61 us -> 69.2 us
  other arithmetic: 14.2 us -> 17.8 us
    ppermute x19 -> x23, waiting for transfers between devices: 54.4 us -> 38.2 us  [shift(): lax.ppermute(value, axis, [(i, (i + step) % size) for i in range(size)])]
    ppermute x19 -> x23, starting transfers between devices: 19.7 us -> 34.5 us  [shift(): lax.ppermute(value, axis, [(i, (i + step) % size) for i in range(size)])]
    ppermute x7 -> x6, starting transfers between devices: 25.5 us -> 17.7 us  [swap(): lax.ppermute(value, axis, [(i, i ^ mask) for i in range(COUNT[axis])])]
    all_to_all x3 -> x2, starting transfers between devices: 15.6 us -> 9.39 us  [send_gram(): return lax.all_to_all(pieces, ('x', 'yl'), 0, 0)]
    all_to_all x3 -> x2, waiting for transfers between devices: 12 us -> 6.52 us  [send_gram(): return lax.all_to_all(pieces, ('x', 'yl'), 0, 0)]
    all_to_all x0 -> x1, waiting for transfers between devices: none -> 4.84 us  [body(): got_self = lax.all_to_all(part, 'x', 0, 0)]
    all_to_all x0 -> x1, starting transfers between devices: none -> 4.14 us  [body(): got_self = lax.all_to_all(part, 'x', 0, 0)]
    ppermute x2, starting transfers between devices: 0.15 us -> 3.43 us  [batch_shift(): return lax.ppermute(value, ('yh', 'z'), pairs)]
  transfers between devices with their start and end apart: 31 -> 34, of which waited for: 18 -> 21; matrix products, arithmetic and copies ran while one was open for 15% -> 18% of each run, Pallas kernels for 0% -> 0%
where the time goes in v3:
time: 169 us; the launch traced here: 166 us
  starting transfers between devices  69.2 us (41%)
  waiting for transfers between devices  60.4 us (36%)
  other arithmetic  17.8 us (11%)
  matrix products  13.4 us (8%)
  local copies, waits for them, and re-layouts  4.03 us (2%)
    ppermute x23, waiting for transfers between devices, shift(): lax.ppermute(value, axis, [(i, (i + step) % size) for i in range(size)])  38.2 us
    ppermute x23, starting transfers between devices, shift(): lax.ppermute(value, axis, [(i, (i + step) % size) for i in range(size)])  34.5 us
    ppermute x6, starting transfers between devices, swap(): lax.ppermute(value, axis, [(i, i ^ mask) for i in range(COUNT[axis])])  17.7 us
    all_to_all x2, starting transfers between devices, send_gram(): return lax.all_to_all(pieces, ('x', 'yl'), 0, 0)  9.39 us
    all_to_all x2, waiting for transfers between devices, send_gram(): return lax.all_to_all(pieces, ('x', 'yl'), 0, 0)  6.52 us
    dot_general x4, matrix products, nt(): lax.dot_general(lhs, rhs, (((1,), (1,)), ((), ())), preferred_element_typ...  5.86 us
    ppermute x6, waiting for transfers between devices, swap(): lax.ppermute(value, axis, [(i, i ^ mask) for i in range(COUNT[axis])])  5.64 us
    ppermute x2, waiting for transfers between devices, batch_shift(): return lax.ppermute(value, ('yh', 'z'), pairs)  5.17 us
  transfers between devices with their start and end apart: 34, of which 21 were waited for; matrix products, arithmetic and copies ran while one was open for 18% of the time, Pallas kernels for 0%

profile of v3, /device:TPU:1, one launch (start us, length us, event | category | flops | bytes accessed | tf_op | source)
XLA Modules:
  0.0 166.0 jit_solution(7829627368696440515)
XLA Ops:
  6.0 3.8 %collective-permute-start.4 = (f32[2,1024]{1,0:T(2,128)S(1)}, f32[2,1024]{1,0:T(2,128)S(1)}, u32[]{:S(2)}, u32[]{:S(2)}) collective-permute-start(f32[2,1024]{1,0:T(2,128)S(1)} %pad_maximum_fusion.9), channel_id=1, source_target_pairs={{0,32},{16,48},{32,0},{48,16},{1,33},{17,49},{33,1},{49,17},{2,34}... | collective-permute-start | bytes 24584 | tf_op jit(solution)/shard_map/ppermute | solution.py:16
  14.0 3.0 %collective-permute-start.5 = (f32[2,1024]{1,0:T(2,128)S(1)}, f32[2,1024]{1,0:T(2,128)S(1)}, u32[]{:S(2)}, u32[]{:S(2)}) collective-permute-start(f32[2,1024]{1,0:T(2,128)S(1)} %pad_maximum_fusion.10), channel_id=1, source_target_pairs={{0,64},{64,0},{1,65},{65,1},{2,66},{66,2},{3,67},{67,3},{4,68},{68... | collective-permute-start | bytes 24584 | tf_op jit(solution)/shard_map/ppermute | solution.py:24
  18.1 3.0 %collective-permute-start.6 = (bf16[512,1024]{1,0:T(8,128)(2,1)}, bf16[512,1024]{1,0:T(8,128)(2,1)}, u32[]{:S(2)}, u32[]{:S(2)}) collective-permute-start(bf16[512,1024]{1,0:T(8,128)(2,1)} %pad_maximum_fusion.3), channel_id=1, source_target_pairs={{0,64},{64,0},{1,65},{65,1},{2,66},{66,2},{3,67},{67,3},{4,68},{68... | collective-permute-start | bytes 3145736 | tf_op jit(solution)/shard_map/ppermute | solution.py:16
  23.9 4.1 %all-to-all-start = ((bf16[4,128,512]{2,1,0:T(8,128)(2,1)}), bf16[4,128,512]{2,1,0:T(8,128)(2,1)}, u32[]{:S(2)}, u32[]{:S(2)}) async-start(bf16[4,128,512]{2,1,0:T(8,128)(2,1)} %bitcast.90), calls=%async_computation | async-start | bytes 1048576 | tf_op jit(solution)/shard_map/all_to_all | solution.py:114
  30.5 4.8 %all-to-all-done = bf16[4,128,512]{2,1,0:T(8,128)(2,1)} async-done(((bf16[4,128,512]{2,1,0:T(8,128)(2,1)}), bf16[4,128,512]{2,1,0:T(8,128)(2,1)}, u32[]{:S(2)}, u32[]{:S(2)}) %all-to-all-start) | async-done | bytes 524320 | tf_op jit(solution)/shard_map/all_to_all | solution.py:114
  35.3 4.8 %collective-permute-done.7 = bf16[512,1024]{1,0:T(8,128)(2,1)S(1)} collective-permute-done((bf16[512,1024]{1,0:T(8,128)(2,1)}, bf16[512,1024]{1,0:T(8,128)(2,1)S(1)}, u32[]{:S(2)}, u32[]{:S(2)}) %collective-permute-start.7) | collective-permute-done | bytes 1048608 | tf_op jit(solution)/shard_map/ppermute | solution.py:16
  46.6 5.0 %all-to-all-start.1 = ((bf16[8,64,1536]{2,1,0:T(8,128)(2,1)}), bf16[8,64,1536]{2,1,0:T(8,128)(2,1)S(1)}, u32[]{:S(2)}, u32[]{:S(2)}) async-start(bf16[8,64,1536]{2,1,0:T(8,128)(2,1)} %pad_maximum_fusion.2), calls=%async_computation.1 | async-start | bytes 3145728 | tf_op jit(solution)/shard_map/all_to_all | solution.py:38
  53.7 2.7 %collective-permute-start.11 = (bf16[256,1024]{1,0:T(8,128)(2,1)S(1)}, bf16[256,1024]{1,0:T(8,128)(2,1)S(1)}, u32[]{:S(2)}, u32[]{:S(2)}) collective-permute-start(bf16[256,1024]{1,0:T(8,128)(2,1)S(1)} %slice.160), channel_id=1, source_target_pairs={{0,48},{16,0},{32,16},{48,32},{1,49},{17,1},{33,17},{49,33},{2,50}... | collective-permute-start | bytes 1572872 | tf_op jit(solution)/shard_map/ppermute | solution.py:16
  58.8 4.8 %collective-permute-done.10 = bf16[256,1024]{1,0:T(8,128)(2,1)S(1)} collective-permute-done((bf16[256,1024]{1,0:T(8,128)(2,1)S(1)}, bf16[256,1024]{1,0:T(8,128)(2,1)S(1)}, u32[]{:S(2)}, u32[]{:S(2)}) %collective-permute-start.10) | collective-permute-done | bytes 524320 | tf_op jit(solution)/shard_map/ppermute | solution.py:16
  64.9 2.3 %convolution_convert_fusion = bf16[1024,512]{1,0:T(8,128)(2,1)} fusion(bf16[1024,1024]{1,0:T(8,128)(2,1)S(1)} %bitcast.87, bf16[256,1024]{1,0:T(8,128)(2,1)S(1)} %get-tuple-element.77, bf16[256,1024]{1,0:T(8,128)(2,1)S(1)} %get-tuple-element.76), kind=kOutput, calls=%fused_computation.34 | convolution fusion | flops 1076363264 | bytes 4194304 | tf_op jit(solution)/shard_map/dot_general | solution.py:33
  67.2 3.7 %all-to-all-done.1 = bf16[8,64,1536]{2,1,0:T(8,128)(2,1)S(1)} async-done(((bf16[8,64,1536]{2,1,0:T(8,128)(2,1)}), bf16[8,64,1536]{2,1,0:T(8,128)(2,1)S(1)}, u32[]{:S(2)}, u32[]{:S(2)}) %all-to-all-start.1) | async-done | bytes 1572896 | tf_op jit(solution)/shard_map/all_to_all | solution.py:38
  70.9 4.4 %all-to-all-start.2 = ((bf16[8,128,512]{2,1,0:T(8,128)(2,1)}), bf16[8,128,512]{2,1,0:T(8,128)(2,1)}, u32[]{:S(2)}, u32[]{:S(2)}) async-start(bf16[8,128,512]{2,1,0:T(8,128)(2,1)} %bitcast.89), calls=%async_computation.2 | async-start | bytes 2097152 | tf_op jit(solution)/shard_map/all_to_all | solution.py:38
  76.2 2.2 %collective-permute-start.12 = (bf16[64,512]{1,0:T(8,128)(2,1)S(1)}, bf16[64,512]{1,0:T(8,128)(2,1)S(1)}, u32[]{:S(2)}, u32[]{:S(2)}) collective-permute-start(bf16[64,512]{1,0:T(8,128)(2,1)S(1)} %slice.161), channel_id=1, source_target_pairs={{0,80},{16,96},{32,112},{48,64},{64,16},{80,32},{96,48},{112,0},{1... | collective-permute-start | bytes 196616 | tf_op jit(solution)/shard_map/ppermute | solution.py:29
  79.7 5.2 %collective-permute-done.12 = bf16[64,512]{1,0:T(8,128)(2,1)S(1)} collective-permute-done((bf16[64,512]{1,0:T(8,128)(2,1)S(1)}, bf16[64,512]{1,0:T(8,128)(2,1)S(1)}, u32[]{:S(2)}, u32[]{:S(2)}) %collective-permute-start.12) | collective-permute-done | bytes 65568 | tf_op jit(solution)/shard_map/ppermute | solution.py:29
  84.9 2.8 %all-to-all-done.2 = bf16[8,128,512]{2,1,0:T(8,128)(2,1)} async-done(((bf16[8,128,512]{2,1,0:T(8,128)(2,1)}), bf16[8,128,512]{2,1,0:T(8,128)(2,1)}, u32[]{:S(2)}, u32[]{:S(2)}) %all-to-all-start.2) | async-done | bytes 1048608 | tf_op jit(solution)/shard_map/all_to_all | solution.py:38
  91.0 3.5 %collective-permute-done.15 = bf16[64,2048]{1,0:T(8,128)(2,1)S(1)} collective-permute-done((bf16[64,2048]{1,0:T(8,128)(2,1)S(1)}, bf16[64,2048]{1,0:T(8,128)(2,1)S(1)}, u32[]{:S(2)}, u32[]{:S(2)}) %collective-permute-start.15) | collective-permute-done | bytes 262176 | tf_op jit(solution)/shard_map/ppermute | solution.py:16
  95.0 3.9 %collective-permute-start.21 = (bf16[2,64,2176]{2,1,0:T(8,128)(2,1)S(1)}, bf16[2,64,2176]{2,1,0:T(8,128)(2,1)S(1)}, u32[]{:S(2)}, u32[]{:S(2)}) collective-permute-start(bf16[2,64,2176]{2,1,0:T(8,128)(2,1)S(1)} %maximum_maximum_fusion), channel_id=1, source_target_pairs={{0,12},{4,0},{8,4},{12,8},{1,13},{5,1},{9,5},{13,9},{2,14},{6,2},{... | collective-permute-start | bytes 1671176 | tf_op jit(solution)/shard_map/ppermute | solution.py:16
  99.5 6.3 %collective-permute-done.16 = bf16[2,64,2176]{2,1,0:T(8,128)(2,1)S(1)} collective-permute-done((bf16[2,64,2176]{2,1,0:T(8,128)(2,1)S(1)}, bf16[2,64,2176]{2,1,0:T(8,128)(2,1)S(1)}, u32[]{:S(2)}, u32[]{:S(2)}) %collective-permute-start.16) | collective-permute-done | bytes 557088 | tf_op jit(solution)/shard_map/ppermute | solution.py:16
  105.8 4.1 %collective-permute-start.17 = (bf16[2,64,2048]{2,1,0:T(8,128)(2,1)S(1)}, bf16[2,64,2048]{2,1,0:T(8,128)(2,1)S(1)}, u32[]{:S(2)}, u32[]{:S(2)}) collective-permute-start(bf16[2,64,2048]{2,1,0:T(8,128)(2,1)S(1)} %pad_maximum_fusion.6), channel_id=1, source_target_pairs={{0,4},{4,8},{8,12},{12,0},{1,5},{5,9},{9,13},{13,1},{2,6},{6,10},{... | collective-permute-start | bytes 1572872 | tf_op jit(solution)/shard_map/ppermute | solution.py:16
  113.7 13.3 %collective-permute-done.23 = bf16[64,2176]{1,0:T(8,128)(2,1)S(1)} collective-permute-done((bf16[64,2176]{1,0:T(8,128)(2,1)S(1)}, bf16[64,2176]{1,0:T(8,128)(2,1)S(1)}, u32[]{:S(2)}, u32[]{:S(2)}) %collective-permute-start.23) | collective-permute-done | bytes 278560 | tf_op jit(solution)/shard_map/ppermute | solution.py:16
  131.8 4.3 %collective-permute-start.26 = (f32[8,128]{1,0:T(8,128)S(1)}, f32[8,128]{1,0:T(8,128)S(1)}, u32[]{:S(2)}, u32[]{:S(2)}) collective-permute-start(f32[8,128]{1,0:T(8,128)S(1)} %add.196), channel_id=1, source_target_pairs={{0,16},{16,0},{32,48},{48,32},{1,17},{17,1},{33,49},{49,33},{2,18}... | collective-permute-start | bytes 12296 | tf_op jit(solution)/shard_map/ppermute | solution.py:24
  140.8 7.3 %collective-permute-start.28 = (f32[8,128]{1,0:T(8,128)S(1)}, f32[8,128]{1,0:T(8,128)S(1)}, u32[]{:S(2)}, u32[]{:S(2)}) collective-permute-start(f32[8,128]{1,0:T(8,128)S(1)} %add.198), channel_id=1, source_target_pairs={{0,1},{1,0},{2,3},{3,2},{4,5},{5,4},{6,7},{7,6},{8,9},{9,8},{10,11... | collective-permute-start | bytes 12296 | tf_op jit(solution)/shard_map/ppermute | solution.py:24
  150.6 2.7 %collective-permute-done.29 = f32[8,128]{1,0:T(8,128)S(1)} collective-permute-done((f32[8,128]{1,0:T(8,128)S(1)}, f32[8,128]{1,0:T(8,128)S(1)}, u32[]{:S(2)}, u32[]{:S(2)}) %collective-permute-start.29) | collective-permute-done | bytes 4128 | tf_op jit(solution)/shard_map/ppermute | solution.py:24
  158.3 5.1 %collective-permute-start.30 = (bf16[512,512]{1,0:T(8,128)(2,1)S(1)}, bf16[512,512]{1,0:T(8,128)(2,1)S(1)}, u32[]{:S(2)}, u32[]{:S(2)}) collective-permute-start(bf16[512,512]{1,0:T(8,128)(2,1)S(1)} %slice.176), channel_id=1, source_target_pairs={{0,1},{1,0},{2,3},{3,2},{4,5},{5,4},{6,7},{7,6},{8,9},{9,8},{10,11... | collective-permute-start | bytes 1572872 | tf_op jit(solution)/shard_map/ppermute | solution.py:16
  (166 shorter events, 57.4 us)
Async XLA Ops:
  6.0 6.4 %collective-permute-start.4 = (f32[2,1024]{1,0:T(2,128)S(1)}, f32[2,1024]{1,0:T(2,128)S(1)}, u32[]{:S(2)}, u32[]{:S(2)}) collective-permute-start(f32[2,1024]{1,0:T(2,128)S(1)} %pad_maximum_fusion.9), channel_id=1, source_target_pairs={{0,32},{16,48},{32,0},{48,16},{1,33},{17,49},{33,1},{49,17},{2,34}... | collective-permute-start | bytes 24584 | tf_op jit(solution)/shard_map/ppermute | solution.py:16
  17.6 22.6 %collective-permute-start.7 = (bf16[512,1024]{1,0:T(8,128)(2,1)}, bf16[512,1024]{1,0:T(8,128)(2,1)S(1)}, u32[]{:S(2)}, u32[]{:S(2)}) collective-permute-start(bf16[512,1024]{1,0:T(8,128)(2,1)} %pad_maximum_fusion.3), channel_id=1, source_target_pairs={{0,48},{16,0},{32,16},{48,32},{1,49},{17,1},{33,17},{49,33},{2,50}... | collective-permute-start | bytes 3145736 | tf_op jit(solution)/shard_map/ppermute | solution.py:16
  18.1 23.3 %collective-permute-start.6 = (bf16[512,1024]{1,0:T(8,128)(2,1)}, bf16[512,1024]{1,0:T(8,128)(2,1)}, u32[]{:S(2)}, u32[]{:S(2)}) collective-permute-start(bf16[512,1024]{1,0:T(8,128)(2,1)} %pad_maximum_fusion.3), channel_id=1, source_target_pairs={{0,64},{64,0},{1,65},{65,1},{2,66},{66,2},{3,67},{67,3},{4,68},{68... | collective-permute-start | bytes 3145736 | tf_op jit(solution)/shard_map/ppermute | solution.py:16
  23.9 11.4 %all-to-all-start = ((bf16[4,128,512]{2,1,0:T(8,128)(2,1)}), bf16[4,128,512]{2,1,0:T(8,128)(2,1)}, u32[]{:S(2)}, u32[]{:S(2)}) async-start(bf16[4,128,512]{2,1,0:T(8,128)(2,1)} %bitcast.90), calls=%async_computation | async-start | bytes 1048576 | tf_op jit(solution)/shard_map/all_to_all | solution.py:114
  29.9 22.6 %collective-permute-start.9 = (bf16[512,1024]{1,0:T(8,128)(2,1)}, bf16[512,1024]{1,0:T(8,128)(2,1)}, u32[]{:S(2)}, u32[]{:S(2)}) collective-permute-start(bf16[512,1024]{1,0:T(8,128)(2,1)} %pad_maximum_fusion.3), channel_id=1, source_target_pairs={{0,16},{16,32},{32,48},{48,0},{1,17},{17,33},{33,49},{49,1},{2,18}... | collective-permute-start | bytes 3145736 | tf_op jit(solution)/shard_map/ppermute | solution.py:16
  46.6 24.3 %all-to-all-start.1 = ((bf16[8,64,1536]{2,1,0:T(8,128)(2,1)}), bf16[8,64,1536]{2,1,0:T(8,128)(2,1)S(1)}, u32[]{:S(2)}, u32[]{:S(2)}) async-start(bf16[8,64,1536]{2,1,0:T(8,128)(2,1)} %pad_maximum_fusion.2), calls=%async_computation.1 | async-start | bytes 3145728 | tf_op jit(solution)/shard_map/all_to_all | solution.py:38
  53.6 10.1 %collective-permute-start.10 = (bf16[256,1024]{1,0:T(8,128)(2,1)S(1)}, bf16[256,1024]{1,0:T(8,128)(2,1)S(1)}, u32[]{:S(2)}, u32[]{:S(2)}) collective-permute-start(bf16[256,1024]{1,0:T(8,128)(2,1)S(1)} %slice.159), channel_id=1, source_target_pairs={{0,16},{16,32},{32,48},{48,0},{1,17},{17,33},{33,49},{49,1},{2,18}... | collective-permute-start | bytes 1572872 | tf_op jit(solution)/shard_map/ppermute | solution.py:16
  53.7 9.9 %collective-permute-start.11 = (bf16[256,1024]{1,0:T(8,128)(2,1)S(1)}, bf16[256,1024]{1,0:T(8,128)(2,1)S(1)}, u32[]{:S(2)}, u32[]{:S(2)}) collective-permute-start(bf16[256,1024]{1,0:T(8,128)(2,1)S(1)} %slice.160), channel_id=1, source_target_pairs={{0,48},{16,0},{32,16},{48,32},{1,49},{17,1},{33,17},{49,33},{2,50}... | collective-permute-start | bytes 1572872 | tf_op jit(solution)/shard_map/ppermute | solution.py:16
  57.6 17.7 %collective-permute-start.8 = (bf16[64,512]{1,0:T(8,128)(2,1)S(1)}, bf16[64,512]{1,0:T(8,128)(2,1)S(1)}, u32[]{:S(2)}, u32[]{:S(2)}) collective-permute-start(bf16[64,512]{1,0:T(8,128)(2,1)S(1)} %select_convert_fusion), channel_id=1, source_target_pairs={{0,2},{2,0},{1,3},{3,1},{4,6},{6,4},{5,7},{7,5},{8,10},{10,8},{9,1... | collective-permute-start | bytes 196616 | tf_op jit(solution)/shard_map/ppermute | solution.py:16
  70.9 16.8 %all-to-all-start.2 = ((bf16[8,128,512]{2,1,0:T(8,128)(2,1)}), bf16[8,128,512]{2,1,0:T(8,128)(2,1)}, u32[]{:S(2)}, u32[]{:S(2)}) async-start(bf16[8,128,512]{2,1,0:T(8,128)(2,1)} %bitcast.89), calls=%async_computation.2 | async-start | bytes 2097152 | tf_op jit(solution)/shard_map/all_to_all | solution.py:38
  76.2 8.7 %collective-permute-start.12 = (bf16[64,512]{1,0:T(8,128)(2,1)S(1)}, bf16[64,512]{1,0:T(8,128)(2,1)S(1)}, u32[]{:S(2)}, u32[]{:S(2)}) collective-permute-start(bf16[64,512]{1,0:T(8,128)(2,1)S(1)} %slice.161), channel_id=1, source_target_pairs={{0,80},{16,96},{32,112},{48,64},{64,16},{80,32},{96,48},{112,0},{1... | collective-permute-start | bytes 196616 | tf_op jit(solution)/shard_map/ppermute | solution.py:29
  78.5 12.1 %collective-permute-start.13 = (bf16[64,512]{1,0:T(8,128)(2,1)S(1)}, bf16[64,512]{1,0:T(8,128)(2,1)S(1)}, u32[]{:S(2)}, u32[]{:S(2)}) collective-permute-start(bf16[64,512]{1,0:T(8,128)(2,1)S(1)} %get-tuple-element.67), channel_id=1, source_target_pairs={{0,16},{16,32},{32,48},{48,0},{64,80},{80,96},{96,112},{112,64},{1... | collective-permute-start | bytes 196616 | tf_op jit(solution)/shard_map/ppermute | solution.py:29
  90.7 8.3 %collective-permute-start.14 = (bf16[64,2048]{1,0:T(8,128)(2,1)S(1)}, bf16[64,2048]{1,0:T(8,128)(2,1)S(1)}, u32[]{:S(2)}, u32[]{:S(2)}) collective-permute-start(bf16[64,2048]{1,0:T(8,128)(2,1)S(1)} %pad_maximum_fusion.7), channel_id=1, source_target_pairs={{0,2},{2,0},{1,3},{3,1},{4,6},{6,4},{5,7},{7,5},{8,10},{10,8},{9,1... | collective-permute-start | bytes 786440 | tf_op jit(solution)/shard_map/ppermute | solution.py:16
  94.7 11.1 %collective-permute-start.16 = (bf16[2,64,2176]{2,1,0:T(8,128)(2,1)S(1)}, bf16[2,64,2176]{2,1,0:T(8,128)(2,1)S(1)}, u32[]{:S(2)}, u32[]{:S(2)}) collective-permute-start(bf16[2,64,2176]{2,1,0:T(8,128)(2,1)S(1)} %maximum_maximum_fusion), channel_id=1, source_target_pairs={{0,4},{4,8},{8,12},{12,0},{1,5},{5,9},{9,13},{13,1},{2,6},{6,10},{... | collective-permute-start | bytes 1671176 | tf_op jit(solution)/shard_map/ppermute | solution.py:16
  95.0 16.6 %collective-permute-start.21 = (bf16[2,64,2176]{2,1,0:T(8,128)(2,1)S(1)}, bf16[2,64,2176]{2,1,0:T(8,128)(2,1)S(1)}, u32[]{:S(2)}, u32[]{:S(2)}) collective-permute-start(bf16[2,64,2176]{2,1,0:T(8,128)(2,1)S(1)} %maximum_maximum_fusion), channel_id=1, source_target_pairs={{0,12},{4,0},{8,4},{12,8},{1,13},{5,1},{9,5},{13,9},{2,14},{6,2},{... | collective-permute-start | bytes 1671176 | tf_op jit(solution)/shard_map/ppermute | solution.py:16
  105.8 23.2 %collective-permute-start.17 = (bf16[2,64,2048]{2,1,0:T(8,128)(2,1)S(1)}, bf16[2,64,2048]{2,1,0:T(8,128)(2,1)S(1)}, u32[]{:S(2)}, u32[]{:S(2)}) collective-permute-start(bf16[2,64,2048]{2,1,0:T(8,128)(2,1)S(1)} %pad_maximum_fusion.6), channel_id=1, source_target_pairs={{0,4},{4,8},{8,12},{12,0},{1,5},{5,9},{9,13},{13,1},{2,6},{6,10},{... | collective-permute-start | bytes 1572872 | tf_op jit(solution)/shard_map/ppermute | solution.py:16
  109.9 26.2 %collective-permute-start.18 = (bf16[2,64,2048]{2,1,0:T(8,128)(2,1)S(1)}, bf16[2,64,2048]{2,1,0:T(8,128)(2,1)S(1)}, u32[]{:S(2)}, u32[]{:S(2)}) collective-permute-start(bf16[2,64,2048]{2,1,0:T(8,128)(2,1)S(1)} %pad_maximum_fusion.6), channel_id=1, source_target_pairs={{0,12},{4,0},{8,4},{12,8},{1,13},{5,1},{9,5},{13,9},{2,14},{6,2},{... | collective-permute-start | bytes 1572872 | tf_op jit(solution)/shard_map/ppermute | solution.py:16
  111.6 15.4 %collective-permute-start.23 = (bf16[64,2176]{1,0:T(8,128)(2,1)S(1)}, bf16[64,2176]{1,0:T(8,128)(2,1)S(1)}, u32[]{:S(2)}, u32[]{:S(2)}) collective-permute-start(bf16[64,2176]{1,0:T(8,128)(2,1)S(1)} %slice_bitcast_fusion), channel_id=1, source_target_pairs={{0,12},{4,0},{8,4},{12,8},{1,13},{5,1},{9,5},{13,9},{2,14},{6,2},{... | collective-permute-start | bytes 835592 | tf_op jit(solution)/shard_map/ppermute | solution.py:16
  113.1 13.9 %collective-permute-start.22 = (bf16[64,2176]{1,0:T(8,128)(2,1)S(1)}, bf16[64,2176]{1,0:T(8,128)(2,1)S(1)}, u32[]{:S(2)}, u32[]{:S(2)}) collective-permute-start(bf16[64,2176]{1,0:T(8,128)(2,1)S(1)} %slice_bitcast_fusion.1), channel_id=1, source_target_pairs={{0,4},{4,8},{8,12},{12,0},{1,5},{5,9},{9,13},{13,1},{2,6},{6,10},{... | collective-permute-start | bytes 835592 | tf_op jit(solution)/shard_map/ppermute | solution.py:16
  131.0 26.1 %collective-permute-start.24 = (bf16[512,1024]{1,0:T(8,128)(2,1)S(1)}, bf16[512,1024]{1,0:T(8,128)(2,1)S(1)}, u32[]{:S(2)}, u32[]{:S(2)}) collective-permute-start(bf16[512,1024]{1,0:T(8,128)(2,1)S(1)} %add_convert_fusion), channel_id=1, source_target_pairs={{0,64},{64,0},{1,65},{65,1},{2,66},{66,2},{3,67},{67,3},{4,68},{68... | collective-permute-start | bytes 3145736 | tf_op jit(solution)/shard_map/ppermute | solution.py:16
  136.1 17.2 %collective-permute-start.20 = (bf16[64,2048]{1,0:T(8,128)(2,1)S(1)}, bf16[64,2048]{1,0:T(8,128)(2,1)S(1)}, u32[]{:S(2)}, u32[]{:S(2)}) collective-permute-start(bf16[64,2048]{1,0:T(8,128)(2,1)S(1)} %slice_bitcast_fusion.2), channel_id=1, source_target_pairs={{0,12},{4,0},{8,4},{12,8},{1,13},{5,1},{9,5},{13,9},{2,14},{6,2},{... | collective-permute-start | bytes 786440 | tf_op jit(solution)/shard_map/ppermute | solution.py:16
  138.5 14.8 %collective-permute-start.19 = (bf16[64,2048]{1,0:T(8,128)(2,1)S(1)}, bf16[64,2048]{1,0:T(8,128)(2,1)S(1)}, u32[]{:S(2)}, u32[]{:S(2)}) collective-permute-start(bf16[64,2048]{1,0:T(8,128)(2,1)S(1)} %slice_bitcast_fusion.3), channel_id=1, source_target_pairs={{0,4},{4,8},{8,12},{12,0},{1,5},{5,9},{9,13},{13,1},{2,6},{6,10},{... | collective-permute-start | bytes 786440 | tf_op jit(solution)/shard_map/ppermute | solution.py:16
  140.8 8.2 %collective-permute-start.28 = (f32[8,128]{1,0:T(8,128)S(1)}, f32[8,128]{1,0:T(8,128)S(1)}, u32[]{:S(2)}, u32[]{:S(2)}) collective-permute-start(f32[8,128]{1,0:T(8,128)S(1)} %add.198), channel_id=1, source_target_pairs={{0,1},{1,0},{2,3},{3,2},{4,5},{5,4},{6,7},{7,6},{8,9},{9,8},{10,11... | collective-permute-start | bytes 12296 | tf_op jit(solution)/shard_map/ppermute | solution.py:24
  158.3 6.7 %collective-permute-start.30 = (bf16[512,512]{1,0:T(8,128)(2,1)S(1)}, bf16[512,512]{1,0:T(8,128)(2,1)S(1)}, u32[]{:S(2)}, u32[]{:S(2)}) collective-permute-start(bf16[512,512]{1,0:T(8,128)(2,1)S(1)} %slice.176), channel_id=1, source_target_pairs={{0,1},{1,0},{2,3},{3,2},{4,5},{5,4},{6,7},{7,6},{8,9},{9,8},{10,11... | collective-permute-start | bytes 1572872 | tf_op jit(solution)/shard_map/ppermute | solution.py:16
  (30 other events, 200.9 us)

commit v4 on v3

--- a/solution.py
+++ b/solution.py
@@ -58,7 +58,7 @@
     rows = jnp.zeros((4, 2, 64, n), BF16)
     for step, block in ((0, both), (3, prev), (1, succ), (2, jnp.stack([far0, far1]))):
         rows = lax.dynamic_update_slice_in_dim(rows, block[None], (x + step) % 4, 0)
-    return rows.reshape(512, n), prev
+    return rows.reshape(512, n), prev, far0
 
 
 def merge(stats, axis, mask, held):
@@ -187,30 +187,29 @@
             preferred_element_type=F32,
         )
 
-    gram_pair, came = gather_gram(both_pair)
+    gram_pair, _, came = gather_gram(both_pair)
     cols = view_a.shape[1]
     inner_pair = times(gram_pair, 0, 2 * cols).astype(BF16)
+    loss = jnp.sum(gram_pair.reshape(8, 64, 2176)[:, :3, 2048:].astype(F32), axis=(0, 1))
+    loss = jnp.broadcast_to(loss, (8, 128))
+    loss = loss + swap(loss, "yl", 1)
+    inner_pair, loss = lax.optimization_barrier((inner_pair, loss))
     from_pair = shift(inner_pair, "yh", 1)
     both_own, _ = lax.optimization_barrier((spread_gram(low_own), came))
-    gram_own, came = gather_gram(both_own)
-    loss = jnp.sum(gram_pair.reshape(8, 64, 2176)[:, :3, 2048:].astype(F32), axis=(0, 1))
-    loss = jnp.broadcast_to(loss, (8, 128))
+    gram_own, came, _ = gather_gram(both_own)
     loss, _ = lax.optimization_barrier((loss, came))
-    for axis, mask in (("yl", 1), ("z", 1), ("z", 3), ("c", 1), ("yh", 1)):
+    for axis, mask in (("z", 1), ("z", 3), ("c", 1)):
         loss = loss + swap(loss, axis, mask)
+    inner_own, loss = lax.optimization_barrier((times(gram_own, 0, 2 * cols), loss))
+    loss = loss + swap(loss, "yh", 1)
+    from_pair, loss = lax.optimization_barrier((from_pair, loss))
 
     ratio = samples / divisor
     weight = 3.125 * ratio * jnp.where(std < 1.0, 1.0 / std, 0.0)
 
-    def gradient(got, start, stop):
-        inner = (times(gram_own, start, stop) + got.astype(F32)) / divisor
-        own_cols = cent[:, start:stop]
-        term = ratio * (inner - own_cols * var[start:stop]) - weight[start:stop] * own_cols
-        diff = mine32[:, start:stop] - other[:, start:stop].astype(F32)
-        return (term + 12.5 * diff).astype(BF16)
-
-    from_pair, loss = lax.optimization_barrier((from_pair, loss))
-    grad = gradient(from_pair, 0, 2 * cols)
+    inner = (inner_own + from_pair.astype(F32)) / divisor
+    term = ratio * (inner - cent * var) - weight * cent
+    grad = (term + 12.5 * (mine32 - other.astype(F32))).astype(BF16)
     back = shift(grad[:, cols:], "c", 1)
     keep = grad[:, :cols]
     grad_a = jnp.where(core0, keep, back)

time: 169 us -> 161 us (0.953); the launches traced: 166 us -> 160 us
  starting transfers between devices: 69.2 us -> 66.3 us
  other arithmetic: 17.8 us -> 15.2 us
    ppermute x23, waiting for transfers between devices: 38.2 us -> 32.4 us  [shift(): lax.ppermute(value, axis, [(i, (i + step) % size) for i in range(size)])]
    ppermute x6, starting transfers between devices: 17.7 us -> 14.8 us  [swap(): lax.ppermute(value, axis, [(i, i ^ mask) for i in range(COUNT[axis])])]
    all_to_all x1, waiting for transfers between devices: 4.84 us -> 6.93 us  [body(): got_self = lax.all_to_all(part, 'x', 0, 0)]
  transfers between devices with their start and end apart: 34 -> 34, of which waited for: 21 -> 18; matrix products, arithmetic and copies ran while one was open for 18% -> 17% of each run, Pallas kernels for 0% -> 0%
where the time goes in v4:
time: 161 us; the launch traced here: 160 us
  starting transfers between devices  66.3 us (41%)
  waiting for transfers between devices  59.5 us (37%)
  other arithmetic  15.2 us (9%)
  matrix products  13.4 us (8%)
  local copies, waits for them, and re-layouts  4.17 us (3%)
    ppermute x23, starting transfers between devices, shift(): lax.ppermute(value, axis, [(i, (i + step) % size) for i in range(size)])  35.6 us
    ppermute x23, waiting for transfers between devices, shift(): lax.ppermute(value, axis, [(i, (i + step) % size) for i in range(size)])  32.4 us
    ppermute x6, starting transfers between devices, swap(): lax.ppermute(value, axis, [(i, i ^ mask) for i in range(COUNT[axis])])  14.8 us
    all_to_all x2, starting transfers between devices, send_gram(): return lax.all_to_all(pieces, ('x', 'yl'), 0, 0)  8.68 us
    ppermute x6, waiting for transfers between devices, swap(): lax.ppermute(value, axis, [(i, i ^ mask) for i in range(COUNT[axis])])  7.26 us
    all_to_all x1, waiting for transfers between devices, body(): got_self = lax.all_to_all(part, 'x', 0, 0)  6.93 us
    all_to_all x2, waiting for transfers between devices, send_gram(): return lax.all_to_all(pieces, ('x', 'yl'), 0, 0)  6.49 us
    ppermute x2, waiting for transfers between devices, batch_shift(): return lax.ppermute(value, ('yh', 'z'), pairs)  6.44 us
  transfers between devices with their start and end apart: 34, of which 18 were waited for; matrix products, arithmetic and copies ran while one was open for 17% of the time, Pallas kernels for 0%

profile of v4, /device:TPU:1, one launch (start us, length us, event | category | flops | bytes accessed | tf_op | source)
XLA Modules:
  0.0 159.9 jit_solution(5887291797299615631)
XLA Ops:
  14.1 3.0 %collective-permute-start.5 = (f32[2,1024]{1,0:T(2,128)S(1)}, f32[2,1024]{1,0:T(2,128)S(1)}, u32[]{:S(2)}, u32[]{:S(2)}) collective-permute-start(f32[2,1024]{1,0:T(2,128)S(1)} %pad_maximum_fusion.10), channel_id=1, source_target_pairs={{0,64},{64,0},{1,65},{65,1},{2,66},{66,2},{3,67},{67,3},{4,68},{68... | collective-permute-start | bytes 24584 | tf_op jit(solution)/shard_map/ppermute | solution.py:24
  18.5 2.7 %collective-permute-start.6 = (bf16[512,1024]{1,0:T(8,128)(2,1)}, bf16[512,1024]{1,0:T(8,128)(2,1)}, u32[]{:S(2)}, u32[]{:S(2)}) collective-permute-start(bf16[512,1024]{1,0:T(8,128)(2,1)} %pad_maximum_fusion.3), channel_id=1, source_target_pairs={{0,64},{64,0},{1,65},{65,1},{2,66},{66,2},{3,67},{67,3},{4,68},{68... | collective-permute-start | bytes 3145736 | tf_op jit(solution)/shard_map/ppermute | solution.py:16
  24.0 4.1 %all-to-all-start = ((bf16[4,128,512]{2,1,0:T(8,128)(2,1)}), bf16[4,128,512]{2,1,0:T(8,128)(2,1)}, u32[]{:S(2)}, u32[]{:S(2)}) async-start(bf16[4,128,512]{2,1,0:T(8,128)(2,1)} %bitcast.90), calls=%async_computation | async-start | bytes 1048576 | tf_op jit(solution)/shard_map/all_to_all | solution.py:114
  28.5 6.9 %all-to-all-done = bf16[4,128,512]{2,1,0:T(8,128)(2,1)} async-done(((bf16[4,128,512]{2,1,0:T(8,128)(2,1)}), bf16[4,128,512]{2,1,0:T(8,128)(2,1)}, u32[]{:S(2)}, u32[]{:S(2)}) %all-to-all-start) | async-done | bytes 524320 | tf_op jit(solution)/shard_map/all_to_all | solution.py:114
  35.4 4.5 %collective-permute-done.7 = bf16[512,1024]{1,0:T(8,128)(2,1)S(1)} collective-permute-done((bf16[512,1024]{1,0:T(8,128)(2,1)}, bf16[512,1024]{1,0:T(8,128)(2,1)S(1)}, u32[]{:S(2)}, u32[]{:S(2)}) %collective-permute-start.7) | collective-permute-done | bytes 1048608 | tf_op jit(solution)/shard_map/ppermute | solution.py:16
  40.0 2.4 %collective-permute-done.6 = bf16[512,1024]{1,0:T(8,128)(2,1)} collective-permute-done((bf16[512,1024]{1,0:T(8,128)(2,1)}, bf16[512,1024]{1,0:T(8,128)(2,1)}, u32[]{:S(2)}, u32[]{:S(2)}) %collective-permute-start.6) | collective-permute-done | bytes 1048608 | tf_op jit(solution)/shard_map/ppermute | solution.py:16
  47.6 4.4 %all-to-all-start.1 = ((bf16[8,64,1536]{2,1,0:T(8,128)(2,1)}), bf16[8,64,1536]{2,1,0:T(8,128)(2,1)S(1)}, u32[]{:S(2)}, u32[]{:S(2)}) async-start(bf16[8,64,1536]{2,1,0:T(8,128)(2,1)} %pad_maximum_fusion.2), calls=%async_computation.1 | async-start | bytes 3145728 | tf_op jit(solution)/shard_map/all_to_all | solution.py:38
  53.6 2.7 %collective-permute-start.11 = (bf16[256,1024]{1,0:T(8,128)(2,1)S(1)}, bf16[256,1024]{1,0:T(8,128)(2,1)S(1)}, u32[]{:S(2)}, u32[]{:S(2)}) collective-permute-start(bf16[256,1024]{1,0:T(8,128)(2,1)S(1)} %slice.160), channel_id=1, source_target_pairs={{0,48},{16,0},{32,16},{48,32},{1,49},{17,1},{33,17},{49,33},{2,50}... | collective-permute-start | bytes 1572872 | tf_op jit(solution)/shard_map/ppermute | solution.py:16
  59.2 4.8 %collective-permute-done.10 = bf16[256,1024]{1,0:T(8,128)(2,1)S(1)} collective-permute-done((bf16[256,1024]{1,0:T(8,128)(2,1)S(1)}, bf16[256,1024]{1,0:T(8,128)(2,1)S(1)}, u32[]{:S(2)}, u32[]{:S(2)}) %collective-permute-start.10) | collective-permute-done | bytes 524320 | tf_op jit(solution)/shard_map/ppermute | solution.py:16
  65.2 2.3 %convolution_convert_fusion = bf16[1024,512]{1,0:T(8,128)(2,1)} fusion(bf16[1024,1024]{1,0:T(8,128)(2,1)S(1)} %bitcast.87, bf16[256,1024]{1,0:T(8,128)(2,1)S(1)} %get-tuple-element.85, bf16[256,1024]{1,0:T(8,128)(2,1)S(1)} %get-tuple-element.84), kind=kOutput, calls=%fused_computation.35 | convolution fusion | flops 1076363264 | bytes 4194304 | tf_op jit(solution)/shard_map/dot_general | solution.py:33
  67.5 4.0 %all-to-all-done.1 = bf16[8,64,1536]{2,1,0:T(8,128)(2,1)S(1)} async-done(((bf16[8,64,1536]{2,1,0:T(8,128)(2,1)}), bf16[8,64,1536]{2,1,0:T(8,128)(2,1)S(1)}, u32[]{:S(2)}, u32[]{:S(2)}) %all-to-all-start.1) | async-done | bytes 1572896 | tf_op jit(solution)/shard_map/all_to_all | solution.py:38
  71.5 4.2 %all-to-all-start.2 = ((bf16[8,128,512]{2,1,0:T(8,128)(2,1)}), bf16[8,128,512]{2,1,0:T(8,128)(2,1)}, u32[]{:S(2)}, u32[]{:S(2)}) async-start(bf16[8,128,512]{2,1,0:T(8,128)(2,1)} %bitcast.89), calls=%async_computation.2 | async-start | bytes 2097152 | tf_op jit(solution)/shard_map/all_to_all | solution.py:38
  79.3 6.4 %collective-permute-done.12 = bf16[64,512]{1,0:T(8,128)(2,1)S(1)} collective-permute-done((bf16[64,512]{1,0:T(8,128)(2,1)S(1)}, bf16[64,512]{1,0:T(8,128)(2,1)S(1)}, u32[]{:S(2)}, u32[]{:S(2)}) %collective-permute-start.12) | collective-permute-done | bytes 65568 | tf_op jit(solution)/shard_map/ppermute | solution.py:29
  85.7 2.5 %all-to-all-done.2 = bf16[8,128,512]{2,1,0:T(8,128)(2,1)} async-done(((bf16[8,128,512]{2,1,0:T(8,128)(2,1)}), bf16[8,128,512]{2,1,0:T(8,128)(2,1)}, u32[]{:S(2)}, u32[]{:S(2)}) %all-to-all-start.2) | async-done | bytes 1048608 | tf_op jit(solution)/shard_map/all_to_all | solution.py:38
  91.5 3.5 %collective-permute-done.15 = bf16[64,2048]{1,0:T(8,128)(2,1)S(1)} collective-permute-done((bf16[64,2048]{1,0:T(8,128)(2,1)S(1)}, bf16[64,2048]{1,0:T(8,128)(2,1)S(1)}, u32[]{:S(2)}, u32[]{:S(2)}) %collective-permute-start.15) | collective-permute-done | bytes 262176 | tf_op jit(solution)/shard_map/ppermute | solution.py:16
  95.2 2.7 %collective-permute-start.16 = (bf16[2,64,2176]{2,1,0:T(8,128)(2,1)S(1)}, bf16[2,64,2176]{2,1,0:T(8,128)(2,1)S(1)}, u32[]{:S(2)}, u32[]{:S(2)}) collective-permute-start(bf16[2,64,2176]{2,1,0:T(8,128)(2,1)S(1)} %maximum_maximum_fusion), channel_id=1, source_target_pairs={{0,4},{4,8},{8,12},{12,0},{1,5},{5,9},{9,13},{13,1},{2,6},{6,10},{... | collective-permute-start | bytes 1671176 | tf_op jit(solution)/shard_map/ppermute | solution.py:16
  97.8 3.6 %collective-permute-start.22 = (bf16[2,64,2176]{2,1,0:T(8,128)(2,1)S(1)}, bf16[2,64,2176]{2,1,0:T(8,128)(2,1)S(1)}, u32[]{:S(2)}, u32[]{:S(2)}) collective-permute-start(bf16[2,64,2176]{2,1,0:T(8,128)(2,1)S(1)} %maximum_maximum_fusion), channel_id=1, source_target_pairs={{0,12},{4,0},{8,4},{12,8},{1,13},{5,1},{9,5},{13,9},{2,14},{6,2},{... | collective-permute-start | bytes 1671176 | tf_op jit(solution)/shard_map/ppermute | solution.py:16
  102.0 6.7 %collective-permute-done.16 = bf16[2,64,2176]{2,1,0:T(8,128)(2,1)S(1)} collective-permute-done((bf16[2,64,2176]{2,1,0:T(8,128)(2,1)S(1)}, bf16[2,64,2176]{2,1,0:T(8,128)(2,1)S(1)}, u32[]{:S(2)}, u32[]{:S(2)}) %collective-permute-start.16) | collective-permute-done | bytes 557088 | tf_op jit(solution)/shard_map/ppermute | solution.py:16
  108.8 4.9 %collective-permute-start.17 = (bf16[64,2176]{1,0:T(8,128)(2,1)S(1)}, bf16[64,2176]{1,0:T(8,128)(2,1)S(1)}, u32[]{:S(2)}, u32[]{:S(2)}) collective-permute-start(bf16[64,2176]{1,0:T(8,128)(2,1)S(1)} %slice_bitcast_fusion.1), channel_id=1, source_target_pairs={{0,4},{4,8},{8,12},{12,0},{1,5},{5,9},{9,13},{13,1},{2,6},{6,10},{... | collective-permute-start | bytes 835592 | tf_op jit(solution)/shard_map/ppermute | solution.py:16
  114.6 3.7 %collective-permute-done.17 = bf16[64,2176]{1,0:T(8,128)(2,1)S(1)} collective-permute-done((bf16[64,2176]{1,0:T(8,128)(2,1)S(1)}, bf16[64,2176]{1,0:T(8,128)(2,1)S(1)}, u32[]{:S(2)}, u32[]{:S(2)}) %collective-permute-start.17) | collective-permute-done | bytes 278560 | tf_op jit(solution)/shard_map/ppermute | solution.py:16
  125.6 3.2 %collective-permute-done.18 = bf16[2,64,2048]{2,1,0:T(8,128)(2,1)S(1)} collective-permute-done((bf16[2,64,2048]{2,1,0:T(8,128)(2,1)S(1)}, bf16[2,64,2048]{2,1,0:T(8,128)(2,1)S(1)}, u32[]{:S(2)}, u32[]{:S(2)}) %collective-permute-start.18) | collective-permute-done | bytes 524320 | tf_op jit(solution)/shard_map/ppermute | solution.py:16
  133.1 3.4 %collective-permute-done.26 = f32[8,128]{1,0:T(8,128)S(1)} collective-permute-done((f32[8,128]{1,0:T(8,128)S(1)}, f32[8,128]{1,0:T(8,128)S(1)}, u32[]{:S(2)}, u32[]{:S(2)}) %collective-permute-start.26) | collective-permute-done | bytes 4128 | tf_op jit(solution)/shard_map/ppermute | solution.py:24
  136.5 9.4 %collective-permute-start.27 = (f32[8,128]{1,0:T(8,128)S(1)}, f32[8,128]{1,0:T(8,128)S(1)}, u32[]{:S(2)}, u32[]{:S(2)}) collective-permute-start(f32[8,128]{1,0:T(8,128)S(1)} %add.198), channel_id=1, source_target_pairs={{0,1},{1,0},{2,3},{3,2},{4,5},{5,4},{6,7},{7,6},{8,9},{9,8},{10,11... | collective-permute-start | bytes 12296 | tf_op jit(solution)/shard_map/ppermute | solution.py:24
  151.7 3.1 %collective-permute-done.29 = f32[8,128]{1,0:T(8,128)S(1)} collective-permute-done((f32[8,128]{1,0:T(8,128)S(1)}, f32[8,128]{1,0:T(8,128)S(1)}, u32[]{:S(2)}, u32[]{:S(2)}) %collective-permute-start.29) | collective-permute-done | bytes 4128 | tf_op jit(solution)/shard_map/ppermute | solution.py:24
  (160 shorter events, 59.4 us)
Async XLA Ops:
  6.0 6.4 %collective-permute-start.2 = (f32[2,1024]{1,0:T(2,128)S(1)}, f32[2,1024]{1,0:T(2,128)S(1)}, u32[]{:S(2)}, u32[]{:S(2)}) collective-permute-start(f32[2,1024]{1,0:T(2,128)S(1)} %pad_maximum_fusion.9), channel_id=1, source_target_pairs={{0,16},{16,32},{32,48},{48,0},{1,17},{17,33},{33,49},{49,1},{2,18}... | collective-permute-start | bytes 24584 | tf_op jit(solution)/shard_map/ppermute | solution.py:16
  17.1 22.9 %collective-permute-start.7 = (bf16[512,1024]{1,0:T(8,128)(2,1)}, bf16[512,1024]{1,0:T(8,128)(2,1)S(1)}, u32[]{:S(2)}, u32[]{:S(2)}) collective-permute-start(bf16[512,1024]{1,0:T(8,128)(2,1)} %pad_maximum_fusion.3), channel_id=1, source_target_pairs={{0,48},{16,0},{32,16},{48,32},{1,49},{17,1},{33,17},{49,33},{2,50}... | collective-permute-start | bytes 3145736 | tf_op jit(solution)/shard_map/ppermute | solution.py:16
  18.5 23.9 %collective-permute-start.6 = (bf16[512,1024]{1,0:T(8,128)(2,1)}, bf16[512,1024]{1,0:T(8,128)(2,1)}, u32[]{:S(2)}, u32[]{:S(2)}) collective-permute-start(bf16[512,1024]{1,0:T(8,128)(2,1)} %pad_maximum_fusion.3), channel_id=1, source_target_pairs={{0,64},{64,0},{1,65},{65,1},{2,66},{66,2},{3,67},{67,3},{4,68},{68... | collective-permute-start | bytes 3145736 | tf_op jit(solution)/shard_map/ppermute | solution.py:16
  24.0 11.4 %all-to-all-start = ((bf16[4,128,512]{2,1,0:T(8,128)(2,1)}), bf16[4,128,512]{2,1,0:T(8,128)(2,1)}, u32[]{:S(2)}, u32[]{:S(2)}) async-start(bf16[4,128,512]{2,1,0:T(8,128)(2,1)} %bitcast.90), calls=%async_computation | async-start | bytes 1048576 | tf_op jit(solution)/shard_map/all_to_all | solution.py:114
  28.4 23.8 %collective-permute-start.9 = (bf16[512,1024]{1,0:T(8,128)(2,1)}, bf16[512,1024]{1,0:T(8,128)(2,1)}, u32[]{:S(2)}, u32[]{:S(2)}) collective-permute-start(bf16[512,1024]{1,0:T(8,128)(2,1)} %pad_maximum_fusion.3), channel_id=1, source_target_pairs={{0,16},{16,32},{32,48},{48,0},{1,17},{17,33},{33,49},{49,1},{2,18}... | collective-permute-start | bytes 3145736 | tf_op jit(solution)/shard_map/ppermute | solution.py:16
  47.6 24.0 %all-to-all-start.1 = ((bf16[8,64,1536]{2,1,0:T(8,128)(2,1)}), bf16[8,64,1536]{2,1,0:T(8,128)(2,1)S(1)}, u32[]{:S(2)}, u32[]{:S(2)}) async-start(bf16[8,64,1536]{2,1,0:T(8,128)(2,1)} %pad_maximum_fusion.2), calls=%async_computation.1 | async-start | bytes 3145728 | tf_op jit(solution)/shard_map/all_to_all | solution.py:38
  53.5 10.5 %collective-permute-start.10 = (bf16[256,1024]{1,0:T(8,128)(2,1)S(1)}, bf16[256,1024]{1,0:T(8,128)(2,1)S(1)}, u32[]{:S(2)}, u32[]{:S(2)}) collective-permute-start(bf16[256,1024]{1,0:T(8,128)(2,1)S(1)} %slice.159), channel_id=1, source_target_pairs={{0,16},{16,32},{32,48},{48,0},{1,17},{17,33},{33,49},{49,1},{2,18}... | collective-permute-start | bytes 1572872 | tf_op jit(solution)/shard_map/ppermute | solution.py:16
  53.6 10.4 %collective-permute-start.11 = (bf16[256,1024]{1,0:T(8,128)(2,1)S(1)}, bf16[256,1024]{1,0:T(8,128)(2,1)S(1)}, u32[]{:S(2)}, u32[]{:S(2)}) collective-permute-start(bf16[256,1024]{1,0:T(8,128)(2,1)S(1)} %slice.160), channel_id=1, source_target_pairs={{0,48},{16,0},{32,16},{48,32},{1,49},{17,1},{33,17},{49,33},{2,50}... | collective-permute-start | bytes 1572872 | tf_op jit(solution)/shard_map/ppermute | solution.py:16
  57.5 18.3 %collective-permute-start.8 = (bf16[64,512]{1,0:T(8,128)(2,1)S(1)}, bf16[64,512]{1,0:T(8,128)(2,1)S(1)}, u32[]{:S(2)}, u32[]{:S(2)}) collective-permute-start(bf16[64,512]{1,0:T(8,128)(2,1)S(1)} %select_convert_fusion), channel_id=1, source_target_pairs={{0,2},{2,0},{1,3},{3,1},{4,6},{6,4},{5,7},{7,5},{8,10},{10,8},{9,1... | collective-permute-start | bytes 196616 | tf_op jit(solution)/shard_map/ppermute | solution.py:16
  71.5 16.7 %all-to-all-start.2 = ((bf16[8,128,512]{2,1,0:T(8,128)(2,1)}), bf16[8,128,512]{2,1,0:T(8,128)(2,1)}, u32[]{:S(2)}, u32[]{:S(2)}) async-start(bf16[8,128,512]{2,1,0:T(8,128)(2,1)} %bitcast.89), calls=%async_computation.2 | async-start | bytes 2097152 | tf_op jit(solution)/shard_map/all_to_all | solution.py:38
  76.0 9.7 %collective-permute-start.12 = (bf16[64,512]{1,0:T(8,128)(2,1)S(1)}, bf16[64,512]{1,0:T(8,128)(2,1)S(1)}, u32[]{:S(2)}, u32[]{:S(2)}) collective-permute-start(bf16[64,512]{1,0:T(8,128)(2,1)S(1)} %slice.161), channel_id=1, source_target_pairs={{0,80},{16,96},{32,112},{48,64},{64,16},{80,32},{96,48},{112,0},{1... | collective-permute-start | bytes 196616 | tf_op jit(solution)/shard_map/ppermute | solution.py:29
  77.8 13.5 %collective-permute-start.13 = (bf16[64,512]{1,0:T(8,128)(2,1)S(1)}, bf16[64,512]{1,0:T(8,128)(2,1)S(1)}, u32[]{:S(2)}, u32[]{:S(2)}) collective-permute-start(bf16[64,512]{1,0:T(8,128)(2,1)S(1)} %get-tuple-element.75), channel_id=1, source_target_pairs={{0,16},{16,32},{32,48},{48,0},{64,80},{80,96},{96,112},{112,64},{1... | collective-permute-start | bytes 196616 | tf_op jit(solution)/shard_map/ppermute | solution.py:29
  89.7 5.3 %collective-permute-start.15 = (bf16[64,2048]{1,0:T(8,128)(2,1)S(1)}, bf16[64,2048]{1,0:T(8,128)(2,1)S(1)}, u32[]{:S(2)}, u32[]{:S(2)}) collective-permute-start(bf16[64,2048]{1,0:T(8,128)(2,1)S(1)} %pad_maximum_fusion.8), channel_id=1, source_target_pairs={{0,2},{2,0},{1,3},{3,1},{4,6},{6,4},{5,7},{7,5},{8,10},{10,8},{9,1... | collective-permute-start | bytes 786440 | tf_op jit(solution)/shard_map/ppermute | solution.py:16
  91.3 10.1 %collective-permute-start.14 = (bf16[64,2048]{1,0:T(8,128)(2,1)S(1)}, bf16[64,2048]{1,0:T(8,128)(2,1)S(1)}, u32[]{:S(2)}, u32[]{:S(2)}) collective-permute-start(bf16[64,2048]{1,0:T(8,128)(2,1)S(1)} %pad_maximum_fusion.7), channel_id=1, source_target_pairs={{0,2},{2,0},{1,3},{3,1},{4,6},{6,4},{5,7},{7,5},{8,10},{10,8},{9,1... | collective-permute-start | bytes 786440 | tf_op jit(solution)/shard_map/ppermute | solution.py:16
  95.2 13.5 %collective-permute-start.16 = (bf16[2,64,2176]{2,1,0:T(8,128)(2,1)S(1)}, bf16[2,64,2176]{2,1,0:T(8,128)(2,1)S(1)}, u32[]{:S(2)}, u32[]{:S(2)}) collective-permute-start(bf16[2,64,2176]{2,1,0:T(8,128)(2,1)S(1)} %maximum_maximum_fusion), channel_id=1, source_target_pairs={{0,4},{4,8},{8,12},{12,0},{1,5},{5,9},{9,13},{13,1},{2,6},{6,10},{... | collective-permute-start | bytes 1671176 | tf_op jit(solution)/shard_map/ppermute | solution.py:16
  97.8 16.4 %collective-permute-start.22 = (bf16[2,64,2176]{2,1,0:T(8,128)(2,1)S(1)}, bf16[2,64,2176]{2,1,0:T(8,128)(2,1)S(1)}, u32[]{:S(2)}, u32[]{:S(2)}) collective-permute-start(bf16[2,64,2176]{2,1,0:T(8,128)(2,1)S(1)} %maximum_maximum_fusion), channel_id=1, source_target_pairs={{0,12},{4,0},{8,4},{12,8},{1,13},{5,1},{9,5},{13,9},{2,14},{6,2},{... | collective-permute-start | bytes 1671176 | tf_op jit(solution)/shard_map/ppermute | solution.py:16
  108.8 9.5 %collective-permute-start.17 = (bf16[64,2176]{1,0:T(8,128)(2,1)S(1)}, bf16[64,2176]{1,0:T(8,128)(2,1)S(1)}, u32[]{:S(2)}, u32[]{:S(2)}) collective-permute-start(bf16[64,2176]{1,0:T(8,128)(2,1)S(1)} %slice_bitcast_fusion.1), channel_id=1, source_target_pairs={{0,4},{4,8},{8,12},{12,0},{1,5},{5,9},{9,13},{13,1},{2,6},{6,10},{... | collective-permute-start | bytes 835592 | tf_op jit(solution)/shard_map/ppermute | solution.py:16
  114.3 6.7 %collective-permute-start.23 = (bf16[64,2176]{1,0:T(8,128)(2,1)S(1)}, bf16[64,2176]{1,0:T(8,128)(2,1)S(1)}, u32[]{:S(2)}, u32[]{:S(2)}) collective-permute-start(bf16[64,2176]{1,0:T(8,128)(2,1)S(1)} %slice_bitcast_fusion), channel_id=1, source_target_pairs={{0,12},{4,0},{8,4},{12,8},{1,13},{5,1},{9,5},{13,9},{2,14},{6,2},{... | collective-permute-start | bytes 835592 | tf_op jit(solution)/shard_map/ppermute | solution.py:16
  118.3 10.6 %collective-permute-start.18 = (bf16[2,64,2048]{2,1,0:T(8,128)(2,1)S(1)}, bf16[2,64,2048]{2,1,0:T(8,128)(2,1)S(1)}, u32[]{:S(2)}, u32[]{:S(2)}) collective-permute-start(bf16[2,64,2048]{2,1,0:T(8,128)(2,1)S(1)} %pad_maximum_fusion.6), channel_id=1, source_target_pairs={{0,4},{4,8},{8,12},{12,0},{1,5},{5,9},{9,13},{13,1},{2,6},{6,10},{... | collective-permute-start | bytes 1572872 | tf_op jit(solution)/shard_map/ppermute | solution.py:16
  119.8 11.1 %collective-permute-start.19 = (bf16[2,64,2048]{2,1,0:T(8,128)(2,1)S(1)}, bf16[2,64,2048]{2,1,0:T(8,128)(2,1)S(1)}, u32[]{:S(2)}, u32[]{:S(2)}) collective-permute-start(bf16[2,64,2048]{2,1,0:T(8,128)(2,1)S(1)} %pad_maximum_fusion.6), channel_id=1, source_target_pairs={{0,12},{4,0},{8,4},{12,8},{1,13},{5,1},{9,5},{13,9},{2,14},{6,2},{... | collective-permute-start | bytes 1572872 | tf_op jit(solution)/shard_map/ppermute | solution.py:16
  125.3 29.4 %collective-permute-start.28 = (bf16[512,1024]{1,0:T(8,128)(2,1)S(1)}, bf16[512,1024]{1,0:T(8,128)(2,1)S(1)}, u32[]{:S(2)}, u32[]{:S(2)}) collective-permute-start(bf16[512,1024]{1,0:T(8,128)(2,1)S(1)} %add_convert_fusion), channel_id=1, source_target_pairs={{0,64},{64,0},{1,65},{65,1},{2,66},{66,2},{3,67},{67,3},{4,68},{68... | collective-permute-start | bytes 3145736 | tf_op jit(solution)/shard_map/ppermute | solution.py:16
  130.0 16.7 %collective-permute-start.20 = (bf16[64,2048]{1,0:T(8,128)(2,1)S(1)}, bf16[64,2048]{1,0:T(8,128)(2,1)S(1)}, u32[]{:S(2)}, u32[]{:S(2)}) collective-permute-start(bf16[64,2048]{1,0:T(8,128)(2,1)S(1)} %slice_bitcast_fusion.3), channel_id=1, source_target_pairs={{0,4},{4,8},{8,12},{12,0},{1,5},{5,9},{9,13},{13,1},{2,6},{6,10},{... | collective-permute-start | bytes 786440 | tf_op jit(solution)/shard_map/ppermute | solution.py:16
  131.0 15.8 %collective-permute-start.21 = (bf16[64,2048]{1,0:T(8,128)(2,1)S(1)}, bf16[64,2048]{1,0:T(8,128)(2,1)S(1)}, u32[]{:S(2)}, u32[]{:S(2)}) collective-permute-start(bf16[64,2048]{1,0:T(8,128)(2,1)S(1)} %slice_bitcast_fusion.2), channel_id=1, source_target_pairs={{0,12},{4,0},{8,4},{12,8},{1,13},{5,1},{9,5},{13,9},{2,14},{6,2},{... | collective-permute-start | bytes 786440 | tf_op jit(solution)/shard_map/ppermute | solution.py:16
  136.5 10.2 %collective-permute-start.27 = (f32[8,128]{1,0:T(8,128)S(1)}, f32[8,128]{1,0:T(8,128)S(1)}, u32[]{:S(2)}, u32[]{:S(2)}) collective-permute-start(f32[8,128]{1,0:T(8,128)S(1)} %add.198), channel_id=1, source_target_pairs={{0,1},{1,0},{2,3},{3,2},{4,5},{5,4},{6,7},{7,6},{8,9},{9,8},{10,11... | collective-permute-start | bytes 12296 | tf_op jit(solution)/shard_map/ppermute | solution.py:24
  (27 other events, 147.0 us)

commit v5 on v4

--- a/solution.py
+++ b/solution.py
@@ -198,7 +198,7 @@
     both_own, _ = lax.optimization_barrier((spread_gram(low_own), came))
     gram_own, came, _ = gather_gram(both_own)
     loss, _ = lax.optimization_barrier((loss, came))
-    for axis, mask in (("z", 1), ("z", 3), ("c", 1)):
+    for axis, mask in (("z", 1), ("z", 3)):
         loss = loss + swap(loss, axis, mask)
     inner_own, loss = lax.optimization_barrier((times(gram_own, 0, 2 * cols), loss))
     loss = loss + swap(loss, "yh", 1)
@@ -215,6 +215,7 @@
     grad_a = jnp.where(core0, keep, back)
     grad_b = jnp.where(core0, back, keep)
 
+    loss = loss + swap(loss, "c", 1)
     return grad_a, grad_b, jnp.sum(loss[0])
 
 

time: 161 us -> 161 us (level)
  starting transfers between devices: 66.3 us -> 63.5 us
  waiting for transfers between devices: 59.5 us -> 62 us
    ppermute x6, starting transfers between devices: 14.8 us -> 5.07 us  [swap(): lax.ppermute(value, axis, [(i, i ^ mask) for i in range(COUNT[axis])])]
    ppermute x23, starting transfers between devices: 35.6 us -> 42.5 us  [shift(): lax.ppermute(value, axis, [(i, (i + step) % size) for i in range(size)])]
  transfers between devices with their start and end apart: 34 -> 34, of which waited for: 18 -> 19; matrix products, arithmetic and copies ran while one was open for 17% -> 17% of each run, Pallas kernels for 0% -> 0%
where the time goes in v5:
time: 161 us; the launch traced here: 160 us
  starting transfers between devices  63.5 us (39%)
  waiting for transfers between devices  62 us (39%)
  other arithmetic  15.2 us (9%)
  matrix products  13.4 us (8%)
  local copies, waits for them, and re-layouts  4.17 us (3%)
    ppermute x23, starting transfers between devices, shift(): lax.ppermute(value, axis, [(i, (i + step) % size) for i in range(size)])  42.5 us
    ppermute x23, waiting for transfers between devices, shift(): lax.ppermute(value, axis, [(i, (i + step) % size) for i in range(size)])  33.3 us
    ppermute x6, waiting for transfers between devices, swap(): lax.ppermute(value, axis, [(i, i ^ mask) for i in range(COUNT[axis])])  8.83 us
    all_to_all x2, starting transfers between devices, send_gram(): return lax.all_to_all(pieces, ('x', 'yl'), 0, 0)  8.68 us
    all_to_all x1, waiting for transfers between devices, body(): got_self = lax.all_to_all(part, 'x', 0, 0)  6.93 us
    all_to_all x2, waiting for transfers between devices, send_gram(): return lax.all_to_all(pieces, ('x', 'yl'), 0, 0)  6.49 us
    ppermute x2, waiting for transfers between devices, batch_shift(): return lax.ppermute(value, ('yh', 'z'), pairs)  6.44 us
    dot_general x4, matrix products, nt(): lax.dot_general(lhs, rhs, (((1,), (1,)), ((), ())), preferred_element_typ...  5.85 us
  transfers between devices with their start and end apart: 34, of which 19 were waited for; matrix products, arithmetic and copies ran while one was open for 17% of the time, Pallas kernels for 0%

profile of v5, /device:TPU:1, one launch (start us, length us, event | category | flops | bytes accessed | tf_op | source)
XLA Modules:
  0.0 159.5 jit_solution(16626682991968240641)
XLA Ops:
  14.1 3.0 %collective-permute-start.5 = (f32[2,1024]{1,0:T(2,128)S(1)}, f32[2,1024]{1,0:T(2,128)S(1)}, u32[]{:S(2)}, u32[]{:S(2)}) collective-permute-start(f32[2,1024]{1,0:T(2,128)S(1)} %pad_maximum_fusion.10), channel_id=1, source_target_pairs={{0,64},{64,0},{1,65},{65,1},{2,66},{66,2},{3,67},{67,3},{4,68},{68... | collective-permute-start | bytes 24584 | tf_op jit(solution)/shard_map/ppermute | solution.py:24
  18.5 2.7 %collective-permute-start.6 = (bf16[512,1024]{1,0:T(8,128)(2,1)}, bf16[512,1024]{1,0:T(8,128)(2,1)}, u32[]{:S(2)}, u32[]{:S(2)}) collective-permute-start(bf16[512,1024]{1,0:T(8,128)(2,1)} %pad_maximum_fusion.3), channel_id=1, source_target_pairs={{0,64},{64,0},{1,65},{65,1},{2,66},{66,2},{3,67},{67,3},{4,68},{68... | collective-permute-start | bytes 3145736 | tf_op jit(solution)/shard_map/ppermute | solution.py:16
  24.0 4.1 %all-to-all-start = ((bf16[4,128,512]{2,1,0:T(8,128)(2,1)}), bf16[4,128,512]{2,1,0:T(8,128)(2,1)}, u32[]{:S(2)}, u32[]{:S(2)}) async-start(bf16[4,128,512]{2,1,0:T(8,128)(2,1)} %bitcast.90), calls=%async_computation | async-start | bytes 1048576 | tf_op jit(solution)/shard_map/all_to_all | solution.py:114
  28.5 6.9 %all-to-all-done = bf16[4,128,512]{2,1,0:T(8,128)(2,1)} async-done(((bf16[4,128,512]{2,1,0:T(8,128)(2,1)}), bf16[4,128,512]{2,1,0:T(8,128)(2,1)}, u32[]{:S(2)}, u32[]{:S(2)}) %all-to-all-start) | async-done | bytes 524320 | tf_op jit(solution)/shard_map/all_to_all | solution.py:114
  35.4 4.5 %collective-permute-done.7 = bf16[512,1024]{1,0:T(8,128)(2,1)S(1)} collective-permute-done((bf16[512,1024]{1,0:T(8,128)(2,1)}, bf16[512,1024]{1,0:T(8,128)(2,1)S(1)}, u32[]{:S(2)}, u32[]{:S(2)}) %collective-permute-start.7) | collective-permute-done | bytes 1048608 | tf_op jit(solution)/shard_map/ppermute | solution.py:16
  40.0 2.4 %collective-permute-done.6 = bf16[512,1024]{1,0:T(8,128)(2,1)} collective-permute-done((bf16[512,1024]{1,0:T(8,128)(2,1)}, bf16[512,1024]{1,0:T(8,128)(2,1)}, u32[]{:S(2)}, u32[]{:S(2)}) %collective-permute-start.6) | collective-permute-done | bytes 1048608 | tf_op jit(solution)/shard_map/ppermute | solution.py:16
  47.6 4.4 %all-to-all-start.1 = ((bf16[8,64,1536]{2,1,0:T(8,128)(2,1)}), bf16[8,64,1536]{2,1,0:T(8,128)(2,1)S(1)}, u32[]{:S(2)}, u32[]{:S(2)}) async-start(bf16[8,64,1536]{2,1,0:T(8,128)(2,1)} %pad_maximum_fusion.2), calls=%async_computation.1 | async-start | bytes 3145728 | tf_op jit(solution)/shard_map/all_to_all | solution.py:38
  53.6 2.7 %collective-permute-start.11 = (bf16[256,1024]{1,0:T(8,128)(2,1)S(1)}, bf16[256,1024]{1,0:T(8,128)(2,1)S(1)}, u32[]{:S(2)}, u32[]{:S(2)}) collective-permute-start(bf16[256,1024]{1,0:T(8,128)(2,1)S(1)} %slice.160), channel_id=1, source_target_pairs={{0,48},{16,0},{32,16},{48,32},{1,49},{17,1},{33,17},{49,33},{2,50}... | collective-permute-start | bytes 1572872 | tf_op jit(solution)/shard_map/ppermute | solution.py:16
  59.2 4.8 %collective-permute-done.10 = bf16[256,1024]{1,0:T(8,128)(2,1)S(1)} collective-permute-done((bf16[256,1024]{1,0:T(8,128)(2,1)S(1)}, bf16[256,1024]{1,0:T(8,128)(2,1)S(1)}, u32[]{:S(2)}, u32[]{:S(2)}) %collective-permute-start.10) | collective-permute-done | bytes 524320 | tf_op jit(solution)/shard_map/ppermute | solution.py:16
  65.2 2.3 %convolution_convert_fusion = bf16[1024,512]{1,0:T(8,128)(2,1)} fusion(bf16[1024,1024]{1,0:T(8,128)(2,1)S(1)} %bitcast.87, bf16[256,1024]{1,0:T(8,128)(2,1)S(1)} %get-tuple-element.85, bf16[256,1024]{1,0:T(8,128)(2,1)S(1)} %get-tuple-element.84), kind=kOutput, calls=%fused_computation.35 | convolution fusion | flops 1076363264 | bytes 4194304 | tf_op jit(solution)/shard_map/dot_general | solution.py:33
  67.5 4.0 %all-to-all-done.1 = bf16[8,64,1536]{2,1,0:T(8,128)(2,1)S(1)} async-done(((bf16[8,64,1536]{2,1,0:T(8,128)(2,1)}), bf16[8,64,1536]{2,1,0:T(8,128)(2,1)S(1)}, u32[]{:S(2)}, u32[]{:S(2)}) %all-to-all-start.1) | async-done | bytes 1572896 | tf_op jit(solution)/shard_map/all_to_all | solution.py:38
  71.5 4.2 %all-to-all-start.2 = ((bf16[8,128,512]{2,1,0:T(8,128)(2,1)}), bf16[8,128,512]{2,1,0:T(8,128)(2,1)}, u32[]{:S(2)}, u32[]{:S(2)}) async-start(bf16[8,128,512]{2,1,0:T(8,128)(2,1)} %bitcast.89), calls=%async_computation.2 | async-start | bytes 2097152 | tf_op jit(solution)/shard_map/all_to_all | solution.py:38
  79.3 6.4 %collective-permute-done.12 = bf16[64,512]{1,0:T(8,128)(2,1)S(1)} collective-permute-done((bf16[64,512]{1,0:T(8,128)(2,1)S(1)}, bf16[64,512]{1,0:T(8,128)(2,1)S(1)}, u32[]{:S(2)}, u32[]{:S(2)}) %collective-permute-start.12) | collective-permute-done | bytes 65568 | tf_op jit(solution)/shard_map/ppermute | solution.py:29
  85.7 2.5 %all-to-all-done.2 = bf16[8,128,512]{2,1,0:T(8,128)(2,1)} async-done(((bf16[8,128,512]{2,1,0:T(8,128)(2,1)}), bf16[8,128,512]{2,1,0:T(8,128)(2,1)}, u32[]{:S(2)}, u32[]{:S(2)}) %all-to-all-start.2) | async-done | bytes 1048608 | tf_op jit(solution)/shard_map/all_to_all | solution.py:38
  91.5 3.5 %collective-permute-done.15 = bf16[64,2048]{1,0:T(8,128)(2,1)S(1)} collective-permute-done((bf16[64,2048]{1,0:T(8,128)(2,1)S(1)}, bf16[64,2048]{1,0:T(8,128)(2,1)S(1)}, u32[]{:S(2)}, u32[]{:S(2)}) %collective-permute-start.15) | collective-permute-done | bytes 262176 | tf_op jit(solution)/shard_map/ppermute | solution.py:16
  95.2 2.7 %collective-permute-start.16 = (bf16[2,64,2176]{2,1,0:T(8,128)(2,1)S(1)}, bf16[2,64,2176]{2,1,0:T(8,128)(2,1)S(1)}, u32[]{:S(2)}, u32[]{:S(2)}) collective-permute-start(bf16[2,64,2176]{2,1,0:T(8,128)(2,1)S(1)} %maximum_maximum_fusion), channel_id=1, source_target_pairs={{0,4},{4,8},{8,12},{12,0},{1,5},{5,9},{9,13},{13,1},{2,6},{6,10},{... | collective-permute-start | bytes 1671176 | tf_op jit(solution)/shard_map/ppermute | solution.py:16
  97.8 3.6 %collective-permute-start.22 = (bf16[2,64,2176]{2,1,0:T(8,128)(2,1)S(1)}, bf16[2,64,2176]{2,1,0:T(8,128)(2,1)S(1)}, u32[]{:S(2)}, u32[]{:S(2)}) collective-permute-start(bf16[2,64,2176]{2,1,0:T(8,128)(2,1)S(1)} %maximum_maximum_fusion), channel_id=1, source_target_pairs={{0,12},{4,0},{8,4},{12,8},{1,13},{5,1},{9,5},{13,9},{2,14},{6,2},{... | collective-permute-start | bytes 1671176 | tf_op jit(solution)/shard_map/ppermute | solution.py:16
  102.0 6.7 %collective-permute-done.16 = bf16[2,64,2176]{2,1,0:T(8,128)(2,1)S(1)} collective-permute-done((bf16[2,64,2176]{2,1,0:T(8,128)(2,1)S(1)}, bf16[2,64,2176]{2,1,0:T(8,128)(2,1)S(1)}, u32[]{:S(2)}, u32[]{:S(2)}) %collective-permute-start.16) | collective-permute-done | bytes 557088 | tf_op jit(solution)/shard_map/ppermute | solution.py:16
  108.8 4.9 %collective-permute-start.17 = (bf16[64,2176]{1,0:T(8,128)(2,1)S(1)}, bf16[64,2176]{1,0:T(8,128)(2,1)S(1)}, u32[]{:S(2)}, u32[]{:S(2)}) collective-permute-start(bf16[64,2176]{1,0:T(8,128)(2,1)S(1)} %slice_bitcast_fusion.1), channel_id=1, source_target_pairs={{0,4},{4,8},{8,12},{12,0},{1,5},{5,9},{9,13},{13,1},{2,6},{6,10},{... | collective-permute-start | bytes 835592 | tf_op jit(solution)/shard_map/ppermute | solution.py:16
  114.6 3.7 %collective-permute-done.17 = bf16[64,2176]{1,0:T(8,128)(2,1)S(1)} collective-permute-done((bf16[64,2176]{1,0:T(8,128)(2,1)S(1)}, bf16[64,2176]{1,0:T(8,128)(2,1)S(1)}, u32[]{:S(2)}, u32[]{:S(2)}) %collective-permute-start.17) | collective-permute-done | bytes 278560 | tf_op jit(solution)/shard_map/ppermute | solution.py:16
  125.6 3.2 %collective-permute-done.18 = bf16[2,64,2048]{2,1,0:T(8,128)(2,1)S(1)} collective-permute-done((bf16[2,64,2048]{2,1,0:T(8,128)(2,1)S(1)}, bf16[2,64,2048]{2,1,0:T(8,128)(2,1)S(1)}, u32[]{:S(2)}, u32[]{:S(2)}) %collective-permute-start.18) | collective-permute-done | bytes 524320 | tf_op jit(solution)/shard_map/ppermute | solution.py:16
  133.2 3.4 %collective-permute-done.26 = f32[8,128]{1,0:T(8,128)S(1)} collective-permute-done((f32[8,128]{1,0:T(8,128)S(1)}, f32[8,128]{1,0:T(8,128)S(1)}, u32[]{:S(2)}, u32[]{:S(2)}) %collective-permute-start.26) | collective-permute-done | bytes 4128 | tf_op jit(solution)/shard_map/ppermute | solution.py:24
  142.9 3.9 %collective-permute-done.28 = f32[8,128]{1,0:T(8,128)S(1)} collective-permute-done((f32[8,128]{1,0:T(8,128)S(1)}, f32[8,128]{1,0:T(8,128)S(1)}, u32[]{:S(2)}, u32[]{:S(2)}) %collective-permute-start.28) | collective-permute-done | bytes 4128 | tf_op jit(solution)/shard_map/ppermute | solution.py:24
  147.9 8.4 %collective-permute-start.29 = (bf16[512,512]{1,0:T(8,128)(2,1)S(1)}, bf16[512,512]{1,0:T(8,128)(2,1)S(1)}, u32[]{:S(2)}, u32[]{:S(2)}) collective-permute-start(bf16[512,512]{1,0:T(8,128)(2,1)S(1)} %slice.176), channel_id=1, source_target_pairs={{0,1},{1,0},{2,3},{3,2},{4,5},{5,4},{6,7},{7,6},{8,9},{9,8},{10,11... | collective-permute-start | bytes 1572872 | tf_op jit(solution)/shard_map/ppermute | solution.py:16
  (160 shorter events, 59.1 us)
Async XLA Ops:
  6.0 6.4 %collective-permute-start.2 = (f32[2,1024]{1,0:T(2,128)S(1)}, f32[2,1024]{1,0:T(2,128)S(1)}, u32[]{:S(2)}, u32[]{:S(2)}) collective-permute-start(f32[2,1024]{1,0:T(2,128)S(1)} %pad_maximum_fusion.9), channel_id=1, source_target_pairs={{0,16},{16,32},{32,48},{48,0},{1,17},{17,33},{33,49},{49,1},{2,18}... | collective-permute-start | bytes 24584 | tf_op jit(solution)/shard_map/ppermute | solution.py:16
  17.1 22.9 %collective-permute-start.7 = (bf16[512,1024]{1,0:T(8,128)(2,1)}, bf16[512,1024]{1,0:T(8,128)(2,1)S(1)}, u32[]{:S(2)}, u32[]{:S(2)}) collective-permute-start(bf16[512,1024]{1,0:T(8,128)(2,1)} %pad_maximum_fusion.3), channel_id=1, source_target_pairs={{0,48},{16,0},{32,16},{48,32},{1,49},{17,1},{33,17},{49,33},{2,50}... | collective-permute-start | bytes 3145736 | tf_op jit(solution)/shard_map/ppermute | solution.py:16
  18.5 23.9 %collective-permute-start.6 = (bf16[512,1024]{1,0:T(8,128)(2,1)}, bf16[512,1024]{1,0:T(8,128)(2,1)}, u32[]{:S(2)}, u32[]{:S(2)}) collective-permute-start(bf16[512,1024]{1,0:T(8,128)(2,1)} %pad_maximum_fusion.3), channel_id=1, source_target_pairs={{0,64},{64,0},{1,65},{65,1},{2,66},{66,2},{3,67},{67,3},{4,68},{68... | collective-permute-start | bytes 3145736 | tf_op jit(solution)/shard_map/ppermute | solution.py:16
  24.0 11.4 %all-to-all-start = ((bf16[4,128,512]{2,1,0:T(8,128)(2,1)}), bf16[4,128,512]{2,1,0:T(8,128)(2,1)}, u32[]{:S(2)}, u32[]{:S(2)}) async-start(bf16[4,128,512]{2,1,0:T(8,128)(2,1)} %bitcast.90), calls=%async_computation | async-start | bytes 1048576 | tf_op jit(solution)/shard_map/all_to_all | solution.py:114
  28.4 23.8 %collective-permute-start.9 = (bf16[512,1024]{1,0:T(8,128)(2,1)}, bf16[512,1024]{1,0:T(8,128)(2,1)}, u32[]{:S(2)}, u32[]{:S(2)}) collective-permute-start(bf16[512,1024]{1,0:T(8,128)(2,1)} %pad_maximum_fusion.3), channel_id=1, source_target_pairs={{0,16},{16,32},{32,48},{48,0},{1,17},{17,33},{33,49},{49,1},{2,18}... | collective-permute-start | bytes 3145736 | tf_op jit(solution)/shard_map/ppermute | solution.py:16
  47.6 24.0 %all-to-all-start.1 = ((bf16[8,64,1536]{2,1,0:T(8,128)(2,1)}), bf16[8,64,1536]{2,1,0:T(8,128)(2,1)S(1)}, u32[]{:S(2)}, u32[]{:S(2)}) async-start(bf16[8,64,1536]{2,1,0:T(8,128)(2,1)} %pad_maximum_fusion.2), calls=%async_computation.1 | async-start | bytes 3145728 | tf_op jit(solution)/shard_map/all_to_all | solution.py:38
  53.5 10.5 %collective-permute-start.10 = (bf16[256,1024]{1,0:T(8,128)(2,1)S(1)}, bf16[256,1024]{1,0:T(8,128)(2,1)S(1)}, u32[]{:S(2)}, u32[]{:S(2)}) collective-permute-start(bf16[256,1024]{1,0:T(8,128)(2,1)S(1)} %slice.159), channel_id=1, source_target_pairs={{0,16},{16,32},{32,48},{48,0},{1,17},{17,33},{33,49},{49,1},{2,18}... | collective-permute-start | bytes 1572872 | tf_op jit(solution)/shard_map/ppermute | solution.py:16
  53.6 10.4 %collective-permute-start.11 = (bf16[256,1024]{1,0:T(8,128)(2,1)S(1)}, bf16[256,1024]{1,0:T(8,128)(2,1)S(1)}, u32[]{:S(2)}, u32[]{:S(2)}) collective-permute-start(bf16[256,1024]{1,0:T(8,128)(2,1)S(1)} %slice.160), channel_id=1, source_target_pairs={{0,48},{16,0},{32,16},{48,32},{1,49},{17,1},{33,17},{49,33},{2,50}... | collective-permute-start | bytes 1572872 | tf_op jit(solution)/shard_map/ppermute | solution.py:16
  57.5 18.3 %collective-permute-start.8 = (bf16[64,512]{1,0:T(8,128)(2,1)S(1)}, bf16[64,512]{1,0:T(8,128)(2,1)S(1)}, u32[]{:S(2)}, u32[]{:S(2)}) collective-permute-start(bf16[64,512]{1,0:T(8,128)(2,1)S(1)} %select_convert_fusion), channel_id=1, source_target_pairs={{0,2},{2,0},{1,3},{3,1},{4,6},{6,4},{5,7},{7,5},{8,10},{10,8},{9,1... | collective-permute-start | bytes 196616 | tf_op jit(solution)/shard_map/ppermute | solution.py:16
  71.5 16.7 %all-to-all-start.2 = ((bf16[8,128,512]{2,1,0:T(8,128)(2,1)}), bf16[8,128,512]{2,1,0:T(8,128)(2,1)}, u32[]{:S(2)}, u32[]{:S(2)}) async-start(bf16[8,128,512]{2,1,0:T(8,128)(2,1)} %bitcast.89), calls=%async_computation.2 | async-start | bytes 2097152 | tf_op jit(solution)/shard_map/all_to_all | solution.py:38
  76.0 9.7 %collective-permute-start.12 = (bf16[64,512]{1,0:T(8,128)(2,1)S(1)}, bf16[64,512]{1,0:T(8,128)(2,1)S(1)}, u32[]{:S(2)}, u32[]{:S(2)}) collective-permute-start(bf16[64,512]{1,0:T(8,128)(2,1)S(1)} %slice.161), channel_id=1, source_target_pairs={{0,80},{16,96},{32,112},{48,64},{64,16},{80,32},{96,48},{112,0},{1... | collective-permute-start | bytes 196616 | tf_op jit(solution)/shard_map/ppermute | solution.py:29
  77.8 13.5 %collective-permute-start.13 = (bf16[64,512]{1,0:T(8,128)(2,1)S(1)}, bf16[64,512]{1,0:T(8,128)(2,1)S(1)}, u32[]{:S(2)}, u32[]{:S(2)}) collective-permute-start(bf16[64,512]{1,0:T(8,128)(2,1)S(1)} %get-tuple-element.75), channel_id=1, source_target_pairs={{0,16},{16,32},{32,48},{48,0},{64,80},{80,96},{96,112},{112,64},{1... | collective-permute-start | bytes 196616 | tf_op jit(solution)/shard_map/ppermute | solution.py:29
  89.7 5.3 %collective-permute-start.15 = (bf16[64,2048]{1,0:T(8,128)(2,1)S(1)}, bf16[64,2048]{1,0:T(8,128)(2,1)S(1)}, u32[]{:S(2)}, u32[]{:S(2)}) collective-permute-start(bf16[64,2048]{1,0:T(8,128)(2,1)S(1)} %pad_maximum_fusion.8), channel_id=1, source_target_pairs={{0,2},{2,0},{1,3},{3,1},{4,6},{6,4},{5,7},{7,5},{8,10},{10,8},{9,1... | collective-permute-start | bytes 786440 | tf_op jit(solution)/shard_map/ppermute | solution.py:16
  91.3 10.1 %collective-permute-start.14 = (bf16[64,2048]{1,0:T(8,128)(2,1)S(1)}, bf16[64,2048]{1,0:T(8,128)(2,1)S(1)}, u32[]{:S(2)}, u32[]{:S(2)}) collective-permute-start(bf16[64,2048]{1,0:T(8,128)(2,1)S(1)} %pad_maximum_fusion.7), channel_id=1, source_target_pairs={{0,2},{2,0},{1,3},{3,1},{4,6},{6,4},{5,7},{7,5},{8,10},{10,8},{9,1... | collective-permute-start | bytes 786440 | tf_op jit(solution)/shard_map/ppermute | solution.py:16
  95.2 13.5 %collective-permute-start.16 = (bf16[2,64,2176]{2,1,0:T(8,128)(2,1)S(1)}, bf16[2,64,2176]{2,1,0:T(8,128)(2,1)S(1)}, u32[]{:S(2)}, u32[]{:S(2)}) collective-permute-start(bf16[2,64,2176]{2,1,0:T(8,128)(2,1)S(1)} %maximum_maximum_fusion), channel_id=1, source_target_pairs={{0,4},{4,8},{8,12},{12,0},{1,5},{5,9},{9,13},{13,1},{2,6},{6,10},{... | collective-permute-start | bytes 1671176 | tf_op jit(solution)/shard_map/ppermute | solution.py:16
  97.8 16.4 %collective-permute-start.22 = (bf16[2,64,2176]{2,1,0:T(8,128)(2,1)S(1)}, bf16[2,64,2176]{2,1,0:T(8,128)(2,1)S(1)}, u32[]{:S(2)}, u32[]{:S(2)}) collective-permute-start(bf16[2,64,2176]{2,1,0:T(8,128)(2,1)S(1)} %maximum_maximum_fusion), channel_id=1, source_target_pairs={{0,12},{4,0},{8,4},{12,8},{1,13},{5,1},{9,5},{13,9},{2,14},{6,2},{... | collective-permute-start | bytes 1671176 | tf_op jit(solution)/shard_map/ppermute | solution.py:16
  108.8 9.5 %collective-permute-start.17 = (bf16[64,2176]{1,0:T(8,128)(2,1)S(1)}, bf16[64,2176]{1,0:T(8,128)(2,1)S(1)}, u32[]{:S(2)}, u32[]{:S(2)}) collective-permute-start(bf16[64,2176]{1,0:T(8,128)(2,1)S(1)} %slice_bitcast_fusion.1), channel_id=1, source_target_pairs={{0,4},{4,8},{8,12},{12,0},{1,5},{5,9},{9,13},{13,1},{2,6},{6,10},{... | collective-permute-start | bytes 835592 | tf_op jit(solution)/shard_map/ppermute | solution.py:16
  114.3 6.7 %collective-permute-start.23 = (bf16[64,2176]{1,0:T(8,128)(2,1)S(1)}, bf16[64,2176]{1,0:T(8,128)(2,1)S(1)}, u32[]{:S(2)}, u32[]{:S(2)}) collective-permute-start(bf16[64,2176]{1,0:T(8,128)(2,1)S(1)} %slice_bitcast_fusion), channel_id=1, source_target_pairs={{0,12},{4,0},{8,4},{12,8},{1,13},{5,1},{9,5},{13,9},{2,14},{6,2},{... | collective-permute-start | bytes 835592 | tf_op jit(solution)/shard_map/ppermute | solution.py:16
  118.3 10.6 %collective-permute-start.18 = (bf16[2,64,2048]{2,1,0:T(8,128)(2,1)S(1)}, bf16[2,64,2048]{2,1,0:T(8,128)(2,1)S(1)}, u32[]{:S(2)}, u32[]{:S(2)}) collective-permute-start(bf16[2,64,2048]{2,1,0:T(8,128)(2,1)S(1)} %pad_maximum_fusion.6), channel_id=1, source_target_pairs={{0,4},{4,8},{8,12},{12,0},{1,5},{5,9},{9,13},{13,1},{2,6},{6,10},{... | collective-permute-start | bytes 1572872 | tf_op jit(solution)/shard_map/ppermute | solution.py:16
  119.8 11.1 %collective-permute-start.19 = (bf16[2,64,2048]{2,1,0:T(8,128)(2,1)S(1)}, bf16[2,64,2048]{2,1,0:T(8,128)(2,1)S(1)}, u32[]{:S(2)}, u32[]{:S(2)}) collective-permute-start(bf16[2,64,2048]{2,1,0:T(8,128)(2,1)S(1)} %pad_maximum_fusion.6), channel_id=1, source_target_pairs={{0,12},{4,0},{8,4},{12,8},{1,13},{5,1},{9,5},{13,9},{2,14},{6,2},{... | collective-permute-start | bytes 1572872 | tf_op jit(solution)/shard_map/ppermute | solution.py:16
  125.3 21.6 %collective-permute-start.27 = (bf16[512,1024]{1,0:T(8,128)(2,1)S(1)}, bf16[512,1024]{1,0:T(8,128)(2,1)S(1)}, u32[]{:S(2)}, u32[]{:S(2)}) collective-permute-start(bf16[512,1024]{1,0:T(8,128)(2,1)S(1)} %add_convert_fusion), channel_id=1, source_target_pairs={{0,64},{64,0},{1,65},{65,1},{2,66},{66,2},{3,67},{67,3},{4,68},{68... | collective-permute-start | bytes 3145736 | tf_op jit(solution)/shard_map/ppermute | solution.py:16
  130.0 7.7 %collective-permute-start.20 = (bf16[64,2048]{1,0:T(8,128)(2,1)S(1)}, bf16[64,2048]{1,0:T(8,128)(2,1)S(1)}, u32[]{:S(2)}, u32[]{:S(2)}) collective-permute-start(bf16[64,2048]{1,0:T(8,128)(2,1)S(1)} %slice_bitcast_fusion.3), channel_id=1, source_target_pairs={{0,4},{4,8},{8,12},{12,0},{1,5},{5,9},{9,13},{13,1},{2,6},{6,10},{... | collective-permute-start | bytes 786440 | tf_op jit(solution)/shard_map/ppermute | solution.py:16
  131.0 7.6 %collective-permute-start.21 = (bf16[64,2048]{1,0:T(8,128)(2,1)S(1)}, bf16[64,2048]{1,0:T(8,128)(2,1)S(1)}, u32[]{:S(2)}, u32[]{:S(2)}) collective-permute-start(bf16[64,2048]{1,0:T(8,128)(2,1)S(1)} %slice_bitcast_fusion.2), channel_id=1, source_target_pairs={{0,12},{4,0},{8,4},{12,8},{1,13},{5,1},{9,5},{13,9},{2,14},{6,2},{... | collective-permute-start | bytes 786440 | tf_op jit(solution)/shard_map/ppermute | solution.py:16
  147.9 10.6 %collective-permute-start.29 = (bf16[512,512]{1,0:T(8,128)(2,1)S(1)}, bf16[512,512]{1,0:T(8,128)(2,1)S(1)}, u32[]{:S(2)}, u32[]{:S(2)}) collective-permute-start(bf16[512,512]{1,0:T(8,128)(2,1)S(1)} %slice.176), channel_id=1, source_target_pairs={{0,1},{1,0},{2,3},{3,2},{4,5},{5,4},{6,7},{7,6},{8,9},{9,8},{10,11... | collective-permute-start | bytes 1572872 | tf_op jit(solution)/shard_map/ppermute | solution.py:16
  (27 other events, 146.8 us)

commit v6 on v5

--- a/solution.py
+++ b/solution.py
@@ -59,6 +59,13 @@
     for step, block in ((0, both), (3, prev), (1, succ), (2, jnp.stack([far0, far1]))):
         rows = lax.dynamic_update_slice_in_dim(rows, block[None], (x + step) % 4, 0)
     return rows.reshape(512, n), prev, far0
+
+
+def place(x, own, prev, opposite, succ):
+    rows = jnp.zeros((4,) + own.shape, own.dtype)
+    for step, block in ((0, own), (3, prev), (2, opposite), (1, succ)):
+        rows = lax.dynamic_update_slice_in_dim(rows, block[None], (x + step) % 4, 0)
+    return rows
 
 
 def merge(stats, axis, mask, held):
@@ -130,10 +137,16 @@
     red_near = sum_gram(got_near)
     low_near = red_near.astype(BF16)
     turned_near = batch_shift(low_near[:, 512:], 1, 1)
-    got_far, turned_near = lax.optimization_barrier((got_far, turned_near))
+    got_far, low_near = lax.optimization_barrier((got_far, low_near))
+    x = lax.axis_index("x")
+    first = lax.axis_index("yl") == 0
+    here = place(x, low_near, *[shift(low_near, "x", step) for step in (1, 2, 3)])
+    there = shift(here, "yl", 1)
+    gram_near = jnp.stack([jnp.where(first, here, there), jnp.where(first, there, here)], axis=1)
+    gram_near = gram_near.reshape(512, 1024)
     red_far = sum_gram(got_far)
     low_far = red_far.astype(BF16)
-    low_pair = jnp.concatenate([low_near, low_far[:64], turned_near], axis=1)
+    low_pair = jnp.concatenate([low_far[:64], turned_near], axis=1)
     both_pair = spread_gram(low_pair)
     red_self, red_own = sum_gram(got_self), sum_gram(got_own)
     even = lax.axis_index("yl") == 0
@@ -189,8 +202,16 @@
 
     gram_pair, _, came = gather_gram(both_pair)
     cols = view_a.shape[1]
-    inner_pair = times(gram_pair, 0, 2 * cols).astype(BF16)
-    loss = jnp.sum(gram_pair.reshape(8, 64, 2176)[:, :3, 2048:].astype(F32), axis=(0, 1))
+    inner_near = jnp.dot(gram_near, near, preferred_element_type=F32)
+    inner_near, gram_pair = lax.optimization_barrier((inner_near, gram_pair))
+    inner_pair = (
+        inner_near
+        + jnp.dot(gram_pair[:, :512], far, preferred_element_type=F32)
+        + lax.dot_general(
+            gram_pair[:, 512:1024], before, (((0,), (0,)), ((), ())), preferred_element_type=F32
+        )
+    ).astype(BF16)
+    loss = jnp.sum(gram_pair.reshape(8, 64, 1152)[:, :3, 1024:].astype(F32), axis=(0, 1))
     loss = jnp.broadcast_to(loss, (8, 128))
     loss = loss + swap(loss, "yl", 1)
     inner_pair, loss = lax.optimization_barrier((inner_pair, loss))

time: 161 us -> 159 us (0.988)
  waiting for transfers between devices: 62 us -> 50.6 us
  starting transfers between devices: 63.5 us -> 68.7 us
  other arithmetic: 15.2 us -> 18 us
    ppermute x23 -> x27, waiting for transfers between devices: 33.3 us -> 25.1 us  [shift(): lax.ppermute(value, axis, [(i, (i + step) % size) for i in range(size)])]
    ppermute x2, waiting for transfers between devices: 6.44 us -> 0.01 us  [batch_shift(): return lax.ppermute(value, ('yh', 'z'), pairs)]
    all_to_all x2, waiting for transfers between devices: 6.49 us -> 12.2 us  [send_gram(): return lax.all_to_all(pieces, ('x', 'yl'), 0, 0)]
    ppermute x23 -> x27, starting transfers between devices: 42.5 us -> 47 us  [shift(): lax.ppermute(value, axis, [(i, (i + step) % size) for i in range(size)])]
    dot_general x0 -> x3, matrix products: none -> 3.97 us  [the longest x1 1.97 us: body(): lax.dot_general(gram_pair[:, 512:1024], before, (((0,), (0,)), ((), ())),...]
    dot_general x2 -> x1, matrix products: 4.01 us -> 1.99 us  [times(): lax.dot_general(gram[:, 1536:2048], before[:, start:stop], (((0,), (0,)),...]
    dot_general x2 -> x1, matrix products: 3.58 us -> 1.81 us  [times(): jnp.dot(gram[:, :1536], three[:, start:stop], preferred_element_type=F32)]
  transfers between devices with their start and end apart: 34 -> 38, of which waited for: 19 -> 16; matrix products, arithmetic and copies ran while one was open for 17% -> 20% of each run, Pallas kernels for 0% -> 0%
where the time goes in v6:
time: 159 us; the launch traced here: 158 us
  starting transfers between devices  68.7 us (43%)
  waiting for transfers between devices  50.6 us (32%)
  other arithmetic  18 us (11%)
  matrix products  13.7 us (9%)
  local copies, waits for them, and re-layouts  5.77 us (4%)
    ppermute x27, starting transfers between devices, shift(): lax.ppermute(value, axis, [(i, (i + step) % size) for i in range(size)])  47 us
    ppermute x27, waiting for transfers between devices, shift(): lax.ppermute(value, axis, [(i, (i + step) % size) for i in range(size)])  25.1 us
    all_to_all x2, waiting for transfers between devices, send_gram(): return lax.all_to_all(pieces, ('x', 'yl'), 0, 0)  12.2 us
    all_to_all x2, starting transfers between devices, send_gram(): return lax.all_to_all(pieces, ('x', 'yl'), 0, 0)  8.26 us
    ppermute x6, waiting for transfers between devices, swap(): lax.ppermute(value, axis, [(i, i ^ mask) for i in range(COUNT[axis])])  7.44 us
    ppermute x6, starting transfers between devices, swap(): lax.ppermute(value, axis, [(i, i ^ mask) for i in range(COUNT[axis])])  6.51 us
    all_to_all x1, waiting for transfers between devices, body(): got_self = lax.all_to_all(part, 'x', 0, 0)  5.88 us
    dot_general x4, matrix products, nt(): lax.dot_general(lhs, rhs, (((1,), (1,)), ((), ())), preferred_element_typ...  5.87 us
  transfers between devices with their start and end apart: 38, of which 16 were waited for; matrix products, arithmetic and copies ran while one was open for 20% of the time, Pallas kernels for 0%

profile of v6, /device:TPU:1, one launch (start us, length us, event | category | flops | bytes accessed | tf_op | source)
XLA Modules:
  0.0 158.1 jit_solution(12178969716130360551)
XLA Ops:
  7.8 2.2 %collective-permute-start.3 = (f32[2,1024]{1,0:T(2,128)S(1)}, f32[2,1024]{1,0:T(2,128)S(1)}, u32[]{:S(2)}, u32[]{:S(2)}) collective-permute-start(f32[2,1024]{1,0:T(2,128)S(1)} %pad_maximum_fusion.13), channel_id=1, source_target_pairs={{0,48},{16,0},{32,16},{48,32},{1,49},{17,1},{33,17},{49,33},{2,50}... | collective-permute-start | bytes 24584 | tf_op jit(solution)/shard_map/ppermute | solution.py:16
  14.1 3.0 %collective-permute-start.5 = (f32[2,1024]{1,0:T(2,128)S(1)}, f32[2,1024]{1,0:T(2,128)S(1)}, u32[]{:S(2)}, u32[]{:S(2)}) collective-permute-start(f32[2,1024]{1,0:T(2,128)S(1)} %pad_maximum_fusion.14), channel_id=1, source_target_pairs={{0,64},{64,0},{1,65},{65,1},{2,66},{66,2},{3,67},{67,3},{4,68},{68... | collective-permute-start | bytes 24584 | tf_op jit(solution)/shard_map/ppermute | solution.py:24
  24.0 4.2 %all-to-all-start = ((bf16[4,128,512]{2,1,0:T(8,128)(2,1)}), bf16[4,128,512]{2,1,0:T(8,128)(2,1)}, u32[]{:S(2)}, u32[]{:S(2)}) async-start(bf16[4,128,512]{2,1,0:T(8,128)(2,1)} %bitcast.107), calls=%async_computation | async-start | bytes 1048576 | tf_op jit(solution)/shard_map/all_to_all | solution.py:121
  29.6 5.9 %all-to-all-done = bf16[4,128,512]{2,1,0:T(8,128)(2,1)} async-done(((bf16[4,128,512]{2,1,0:T(8,128)(2,1)}), bf16[4,128,512]{2,1,0:T(8,128)(2,1)}, u32[]{:S(2)}, u32[]{:S(2)}) %all-to-all-start) | async-done | bytes 524320 | tf_op jit(solution)/shard_map/all_to_all | solution.py:121
  35.5 5.0 %collective-permute-done.7 = bf16[512,1024]{1,0:T(8,128)(2,1)S(1)} collective-permute-done((bf16[512,1024]{1,0:T(8,128)(2,1)}, bf16[512,1024]{1,0:T(8,128)(2,1)S(1)}, u32[]{:S(2)}, u32[]{:S(2)}) %collective-permute-start.7) | collective-permute-done | bytes 1048608 | tf_op jit(solution)/shard_map/ppermute | solution.py:16
  40.5 2.5 %collective-permute-done.6 = bf16[512,1024]{1,0:T(8,128)(2,1)} collective-permute-done((bf16[512,1024]{1,0:T(8,128)(2,1)}, bf16[512,1024]{1,0:T(8,128)(2,1)}, u32[]{:S(2)}, u32[]{:S(2)}) %collective-permute-start.6) | collective-permute-done | bytes 1048608 | tf_op jit(solution)/shard_map/ppermute | solution.py:16
  48.1 4.0 %all-to-all-start.1 = ((bf16[8,64,1536]{2,1,0:T(8,128)(2,1)}), bf16[8,64,1536]{2,1,0:T(8,128)(2,1)S(1)}, u32[]{:S(2)}, u32[]{:S(2)}) async-start(bf16[8,64,1536]{2,1,0:T(8,128)(2,1)} %pad_maximum_fusion.2), calls=%async_computation.1 | async-start | bytes 3145728 | tf_op jit(solution)/shard_map/all_to_all | solution.py:38
  54.1 2.4 %collective-permute-start.11 = (bf16[256,1024]{1,0:T(8,128)(2,1)S(1)}, bf16[256,1024]{1,0:T(8,128)(2,1)S(1)}, u32[]{:S(2)}, u32[]{:S(2)}) collective-permute-start(bf16[256,1024]{1,0:T(8,128)(2,1)S(1)} %slice.160), channel_id=1, source_target_pairs={{0,48},{16,0},{32,16},{48,32},{1,49},{17,1},{33,17},{49,33},{2,50}... | collective-permute-start | bytes 1572872 | tf_op jit(solution)/shard_map/ppermute | solution.py:16
  59.3 4.9 %collective-permute-done.10 = bf16[256,1024]{1,0:T(8,128)(2,1)S(1)} collective-permute-done((bf16[256,1024]{1,0:T(8,128)(2,1)S(1)}, bf16[256,1024]{1,0:T(8,128)(2,1)S(1)}, u32[]{:S(2)}, u32[]{:S(2)}) %collective-permute-start.10) | collective-permute-done | bytes 524320 | tf_op jit(solution)/shard_map/ppermute | solution.py:16
  65.3 2.3 %convolution_convert_fusion.1 = bf16[1024,512]{1,0:T(8,128)(2,1)} fusion(bf16[1024,1024]{1,0:T(8,128)(2,1)S(1)} %bitcast.103, bf16[256,1024]{1,0:T(8,128)(2,1)S(1)} %get-tuple-element.91, bf16[256,1024]{1,0:T(8,128)(2,1)S(1)} %get-tuple-element.90), kind=kOutput, calls=%fused_computation.36 | convolution fusion | flops 1076363264 | bytes 4194304 | tf_op jit(solution)/shard_map/dot_general | solution.py:33
  67.6 4.2 %all-to-all-done.1 = bf16[8,64,1536]{2,1,0:T(8,128)(2,1)S(1)} async-done(((bf16[8,64,1536]{2,1,0:T(8,128)(2,1)}), bf16[8,64,1536]{2,1,0:T(8,128)(2,1)S(1)}, u32[]{:S(2)}, u32[]{:S(2)}) %all-to-all-start.1) | async-done | bytes 1572896 | tf_op jit(solution)/shard_map/all_to_all | solution.py:38
  71.8 4.2 %all-to-all-start.2 = ((bf16[8,128,512]{2,1,0:T(8,128)(2,1)}), bf16[8,128,512]{2,1,0:T(8,128)(2,1)}, u32[]{:S(2)}, u32[]{:S(2)}) async-start(bf16[8,128,512]{2,1,0:T(8,128)(2,1)} %bitcast.105), calls=%async_computation.2 | async-start | bytes 2097152 | tf_op jit(solution)/shard_map/all_to_all | solution.py:38
  80.4 8.0 %all-to-all-done.2 = bf16[8,128,512]{2,1,0:T(8,128)(2,1)} async-done(((bf16[8,128,512]{2,1,0:T(8,128)(2,1)}), bf16[8,128,512]{2,1,0:T(8,128)(2,1)}, u32[]{:S(2)}, u32[]{:S(2)}) %all-to-all-start.2) | async-done | bytes 1048608 | tf_op jit(solution)/shard_map/all_to_all | solution.py:38
  94.4 2.3 %collective-permute-start.15 = (bf16[64,1024]{1,0:T(8,128)(2,1)S(1)}, bf16[64,1024]{1,0:T(8,128)(2,1)S(1)}, u32[]{:S(2)}, u32[]{:S(2)}) collective-permute-start(bf16[64,1024]{1,0:T(8,128)(2,1)S(1)} %pad_maximum_fusion.12), channel_id=1, source_target_pairs={{0,2},{2,0},{1,3},{3,1},{4,6},{6,4},{5,7},{7,5},{8,10},{10,8},{9,1... | collective-permute-start | bytes 393224 | tf_op jit(solution)/shard_map/ppermute | solution.py:16
  99.5 2.7 %collective-permute-start.26 = (bf16[2,64,1152]{2,1,0:T(8,128)(2,1)S(1)}, bf16[2,64,1152]{2,1,0:T(8,128)(2,1)S(1)}, u32[]{:S(2)}, u32[]{:S(2)}) collective-permute-start(bf16[2,64,1152]{2,1,0:T(8,128)(2,1)S(1)} %maximum_maximum_fusion), channel_id=1, source_target_pairs={{0,12},{4,0},{8,4},{12,8},{1,13},{5,1},{9,5},{13,9},{2,14},{6,2},{... | collective-permute-start | bytes 884744 | tf_op jit(solution)/shard_map/ppermute | solution.py:16
  106.4 2.7 %collective-permute-start.27 = (bf16[64,1152]{1,0:T(8,128)(2,1)S(1)}, bf16[64,1152]{1,0:T(8,128)(2,1)S(1)}, u32[]{:S(2)}, u32[]{:S(2)}) collective-permute-start(bf16[64,1152]{1,0:T(8,128)(2,1)S(1)} %slice_bitcast_fusion.2), channel_id=1, source_target_pairs={{0,12},{4,0},{8,4},{12,8},{1,13},{5,1},{9,5},{13,9},{2,14},{6,2},{... | collective-permute-start | bytes 442376 | tf_op jit(solution)/shard_map/ppermute | solution.py:16
  109.2 4.2 %collective-permute-done.17 = bf16[64,1152]{1,0:T(8,128)(2,1)S(1)} collective-permute-done((bf16[64,1152]{1,0:T(8,128)(2,1)S(1)}, bf16[64,1152]{1,0:T(8,128)(2,1)S(1)}, u32[]{:S(2)}, u32[]{:S(2)}) %collective-permute-start.17) | collective-permute-done | bytes 147488 | tf_op jit(solution)/shard_map/ppermute | solution.py:16
  113.4 2.7 %collective-permute-start.19 = (bf16[2,64,2048]{2,1,0:T(8,128)(2,1)S(1)}, bf16[2,64,2048]{2,1,0:T(8,128)(2,1)S(1)}, u32[]{:S(2)}, u32[]{:S(2)}) collective-permute-start(bf16[2,64,2048]{2,1,0:T(8,128)(2,1)S(1)} %pad_maximum_fusion.10), channel_id=1, source_target_pairs={{0,12},{4,0},{8,4},{12,8},{1,13},{5,1},{9,5},{13,9},{2,14},{6,2},{... | collective-permute-start | bytes 1572872 | tf_op jit(solution)/shard_map/ppermute | solution.py:16
  123.0 2.4 %collective-permute-start.31 = (bf16[512,1024]{1,0:T(8,128)(2,1)S(1)}, bf16[512,1024]{1,0:T(8,128)(2,1)S(1)}, u32[]{:S(2)}, u32[]{:S(2)}) collective-permute-start(bf16[512,1024]{1,0:T(8,128)(2,1)S(1)} %add_convert_fusion), channel_id=1, source_target_pairs={{0,64},{64,0},{1,65},{65,1},{2,66},{66,2},{3,67},{67,3},{4,68},{68... | collective-permute-start | bytes 3145736 | tf_op jit(solution)/shard_map/ppermute | solution.py:16
  125.6 2.7 %collective-permute-start.21 = (bf16[64,2048]{1,0:T(8,128)(2,1)S(1)}, bf16[64,2048]{1,0:T(8,128)(2,1)S(1)}, u32[]{:S(2)}, u32[]{:S(2)}) collective-permute-start(bf16[64,2048]{1,0:T(8,128)(2,1)S(1)} %slice_bitcast_fusion), channel_id=1, source_target_pairs={{0,12},{4,0},{8,4},{12,8},{1,13},{5,1},{9,5},{13,9},{2,14},{6,2},{... | collective-permute-start | bytes 786440 | tf_op jit(solution)/shard_map/ppermute | solution.py:16
  129.7 2.7 %collective-permute-done.30 = f32[8,128]{1,0:T(8,128)S(1)} collective-permute-done((f32[8,128]{1,0:T(8,128)S(1)}, f32[8,128]{1,0:T(8,128)S(1)}, u32[]{:S(2)}, u32[]{:S(2)}) %collective-permute-start.30) | collective-permute-done | bytes 4128 | tf_op jit(solution)/shard_map/ppermute | solution.py:24
  132.4 2.7 %collective-permute-done.20 = bf16[64,2048]{1,0:T(8,128)(2,1)S(1)} collective-permute-done((bf16[64,2048]{1,0:T(8,128)(2,1)S(1)}, bf16[64,2048]{1,0:T(8,128)(2,1)S(1)}, u32[]{:S(2)}, u32[]{:S(2)}) %collective-permute-start.20) | collective-permute-done | bytes 262176 | tf_op jit(solution)/shard_map/ppermute | solution.py:16
  140.2 3.3 %collective-permute-done.32 = f32[8,128]{1,0:T(8,128)S(1)} collective-permute-done((f32[8,128]{1,0:T(8,128)S(1)}, f32[8,128]{1,0:T(8,128)S(1)}, u32[]{:S(2)}, u32[]{:S(2)}) %collective-permute-start.32) | collective-permute-done | bytes 4128 | tf_op jit(solution)/shard_map/ppermute | solution.py:24
  144.6 10.3 %collective-permute-start.33 = (bf16[512,512]{1,0:T(8,128)(2,1)S(1)}, bf16[512,512]{1,0:T(8,128)(2,1)S(1)}, u32[]{:S(2)}, u32[]{:S(2)}) collective-permute-start(bf16[512,512]{1,0:T(8,128)(2,1)S(1)} %slice.174), channel_id=1, source_target_pairs={{0,1},{1,0},{2,3},{3,2},{4,5},{5,4},{6,7},{7,6},{8,9},{9,8},{10,11... | collective-permute-start | bytes 1572872 | tf_op jit(solution)/shard_map/ppermute | solution.py:16
  (177 shorter events, 65.2 us)
Async XLA Ops:
  17.6 22.9 %collective-permute-start.7 = (bf16[512,1024]{1,0:T(8,128)(2,1)}, bf16[512,1024]{1,0:T(8,128)(2,1)S(1)}, u32[]{:S(2)}, u32[]{:S(2)}) collective-permute-start(bf16[512,1024]{1,0:T(8,128)(2,1)} %pad_maximum_fusion.5), channel_id=1, source_target_pairs={{0,48},{16,0},{32,16},{48,32},{1,49},{17,1},{33,17},{49,33},{2,50}... | collective-permute-start | bytes 3145736 | tf_op jit(solution)/shard_map/ppermute | solution.py:16
  19.0 23.9 %collective-permute-start.6 = (bf16[512,1024]{1,0:T(8,128)(2,1)}, bf16[512,1024]{1,0:T(8,128)(2,1)}, u32[]{:S(2)}, u32[]{:S(2)}) collective-permute-start(bf16[512,1024]{1,0:T(8,128)(2,1)} %pad_maximum_fusion.5), channel_id=1, source_target_pairs={{0,64},{64,0},{1,65},{65,1},{2,66},{66,2},{3,67},{67,3},{4,68},{68... | collective-permute-start | bytes 3145736 | tf_op jit(solution)/shard_map/ppermute | solution.py:16
  24.0 11.5 %all-to-all-start = ((bf16[4,128,512]{2,1,0:T(8,128)(2,1)}), bf16[4,128,512]{2,1,0:T(8,128)(2,1)}, u32[]{:S(2)}, u32[]{:S(2)}) async-start(bf16[4,128,512]{2,1,0:T(8,128)(2,1)} %bitcast.107), calls=%async_computation | async-start | bytes 1048576 | tf_op jit(solution)/shard_map/all_to_all | solution.py:121
  28.9 23.5 %collective-permute-start.9 = (bf16[512,1024]{1,0:T(8,128)(2,1)}, bf16[512,1024]{1,0:T(8,128)(2,1)}, u32[]{:S(2)}, u32[]{:S(2)}) collective-permute-start(bf16[512,1024]{1,0:T(8,128)(2,1)} %pad_maximum_fusion.5), channel_id=1, source_target_pairs={{0,16},{16,32},{32,48},{48,0},{1,17},{17,33},{33,49},{49,1},{2,18}... | collective-permute-start | bytes 3145736 | tf_op jit(solution)/shard_map/ppermute | solution.py:16
  48.1 23.7 %all-to-all-start.1 = ((bf16[8,64,1536]{2,1,0:T(8,128)(2,1)}), bf16[8,64,1536]{2,1,0:T(8,128)(2,1)S(1)}, u32[]{:S(2)}, u32[]{:S(2)}) async-start(bf16[8,64,1536]{2,1,0:T(8,128)(2,1)} %pad_maximum_fusion.2), calls=%async_computation.1 | async-start | bytes 3145728 | tf_op jit(solution)/shard_map/all_to_all | solution.py:38
  53.6 10.7 %collective-permute-start.10 = (bf16[256,1024]{1,0:T(8,128)(2,1)S(1)}, bf16[256,1024]{1,0:T(8,128)(2,1)S(1)}, u32[]{:S(2)}, u32[]{:S(2)}) collective-permute-start(bf16[256,1024]{1,0:T(8,128)(2,1)S(1)} %slice.159), channel_id=1, source_target_pairs={{0,16},{16,32},{32,48},{48,0},{1,17},{17,33},{33,49},{49,1},{2,18}... | collective-permute-start | bytes 1572872 | tf_op jit(solution)/shard_map/ppermute | solution.py:16
  54.1 10.2 %collective-permute-start.11 = (bf16[256,1024]{1,0:T(8,128)(2,1)S(1)}, bf16[256,1024]{1,0:T(8,128)(2,1)S(1)}, u32[]{:S(2)}, u32[]{:S(2)}) collective-permute-start(bf16[256,1024]{1,0:T(8,128)(2,1)S(1)} %slice.160), channel_id=1, source_target_pairs={{0,48},{16,0},{32,16},{48,32},{1,49},{17,1},{33,17},{49,33},{2,50}... | collective-permute-start | bytes 1572872 | tf_op jit(solution)/shard_map/ppermute | solution.py:16
  57.6 18.4 %collective-permute-start.8 = (bf16[64,512]{1,0:T(8,128)(2,1)S(1)}, bf16[64,512]{1,0:T(8,128)(2,1)S(1)}, u32[]{:S(2)}, u32[]{:S(2)}) collective-permute-start(bf16[64,512]{1,0:T(8,128)(2,1)S(1)} %select_convert_fusion), channel_id=1, source_target_pairs={{0,2},{2,0},{1,3},{3,1},{4,6},{6,4},{5,7},{7,5},{8,10},{10,8},{9,1... | collective-permute-start | bytes 196616 | tf_op jit(solution)/shard_map/ppermute | solution.py:16
  71.8 16.6 %all-to-all-start.2 = ((bf16[8,128,512]{2,1,0:T(8,128)(2,1)}), bf16[8,128,512]{2,1,0:T(8,128)(2,1)}, u32[]{:S(2)}, u32[]{:S(2)}) async-start(bf16[8,128,512]{2,1,0:T(8,128)(2,1)} %bitcast.105), calls=%async_computation.2 | async-start | bytes 2097152 | tf_op jit(solution)/shard_map/all_to_all | solution.py:38
  77.4 17.0 %collective-permute-start.14 = (bf16[64,512]{1,0:T(8,128)(2,1)}, bf16[64,512]{1,0:T(8,128)(2,1)S(1)}, u32[]{:S(2)}, u32[]{:S(2)}) collective-permute-start(bf16[64,512]{1,0:T(8,128)(2,1)} %slice.163), channel_id=1, source_target_pairs={{0,80},{16,96},{32,112},{48,64},{64,16},{80,32},{96,48},{112,0},{1... | collective-permute-start | bytes 196616 | tf_op jit(solution)/shard_map/ppermute | solution.py:29
  78.9 18.5 %collective-permute-start.12 = (bf16[64,512]{1,0:T(8,128)(2,1)S(1)}, bf16[64,512]{1,0:T(8,128)(2,1)S(1)}, u32[]{:S(2)}, u32[]{:S(2)}) collective-permute-start(bf16[64,512]{1,0:T(8,128)(2,1)S(1)} %get-tuple-element.81), channel_id=1, source_target_pairs={{0,16},{16,32},{32,48},{48,0},{64,80},{80,96},{96,112},{112,64},{1... | collective-permute-start | bytes 196616 | tf_op jit(solution)/shard_map/ppermute | solution.py:29
  88.4 11.2 %collective-permute-start.22 = (bf16[64,1024]{1,0:T(8,128)(2,1)S(1)}, bf16[64,1024]{1,0:T(8,128)(2,1)S(1)}, u32[]{:S(2)}, u32[]{:S(2)}) collective-permute-start(bf16[64,1024]{1,0:T(8,128)(2,1)S(1)} %convert_element_type.148), channel_id=1, source_target_pairs={{0,4},{4,8},{8,12},{12,0},{1,5},{5,9},{9,13},{13,1},{2,6},{6,10},{... | collective-permute-start | bytes 393224 | tf_op jit(solution)/shard_map/ppermute | solution.py:16
  88.9 13.3 %collective-permute-start.23 = (bf16[64,1024]{1,0:T(8,128)(2,1)S(1)}, bf16[64,1024]{1,0:T(8,128)(2,1)S(1)}, u32[]{:S(2)}, u32[]{:S(2)}) collective-permute-start(bf16[64,1024]{1,0:T(8,128)(2,1)S(1)} %convert_element_type.148), channel_id=1, source_target_pairs={{0,8},{4,12},{8,0},{12,4},{1,9},{5,13},{9,1},{13,5},{2,10},{6,14},... | collective-permute-start | bytes 393224 | tf_op jit(solution)/shard_map/ppermute | solution.py:16
  90.9 11.4 %collective-permute-start.24 = (bf16[64,1024]{1,0:T(8,128)(2,1)S(1)}, bf16[64,1024]{1,0:T(8,128)(2,1)S(1)}, u32[]{:S(2)}, u32[]{:S(2)}) collective-permute-start(bf16[64,1024]{1,0:T(8,128)(2,1)S(1)} %convert_element_type.148), channel_id=1, source_target_pairs={{0,12},{4,0},{8,4},{12,8},{1,13},{5,1},{9,5},{13,9},{2,14},{6,2},{... | collective-permute-start | bytes 393224 | tf_op jit(solution)/shard_map/ppermute | solution.py:16
  97.4 7.0 %collective-permute-start.13 = (bf16[64,2048]{1,0:T(8,128)(2,1)S(1)}, bf16[64,2048]{1,0:T(8,128)(2,1)S(1)}, u32[]{:S(2)}, u32[]{:S(2)}) collective-permute-start(bf16[64,2048]{1,0:T(8,128)(2,1)S(1)} %pad_maximum_fusion.11), channel_id=1, source_target_pairs={{0,2},{2,0},{1,3},{3,1},{4,6},{6,4},{5,7},{7,5},{8,10},{10,8},{9,1... | collective-permute-start | bytes 786440 | tf_op jit(solution)/shard_map/ppermute | solution.py:16
  102.3 14.2 %collective-permute-start.25 = (bf16[4,64,1024]{2,1,0:T(8,128)(2,1)S(1)}, bf16[4,64,1024]{2,1,0:T(8,128)(2,1)S(1)}, u32[]{:S(2)}, u32[]{:S(2)}) collective-permute-start(bf16[4,64,1024]{2,1,0:T(8,128)(2,1)S(1)} %bitcast_dynamic-update-slice_fusion.6), channel_id=1, source_target_pairs={{0,2},{2,0},{1,3},{3,1},{4,6},{6,4},{5,7},{7,5},{8,10},{10,8},{9,1... | collective-permute-start | bytes 1572872 | tf_op jit(solution)/shard_map/ppermute | solution.py:16
  106.3 7.1 %collective-permute-start.17 = (bf16[64,1152]{1,0:T(8,128)(2,1)S(1)}, bf16[64,1152]{1,0:T(8,128)(2,1)S(1)}, u32[]{:S(2)}, u32[]{:S(2)}) collective-permute-start(bf16[64,1152]{1,0:T(8,128)(2,1)S(1)} %slice_bitcast_fusion.3), channel_id=1, source_target_pairs={{0,4},{4,8},{8,12},{12,0},{1,5},{5,9},{9,13},{13,1},{2,6},{6,10},{... | collective-permute-start | bytes 442376 | tf_op jit(solution)/shard_map/ppermute | solution.py:16
  106.4 9.7 %collective-permute-start.27 = (bf16[64,1152]{1,0:T(8,128)(2,1)S(1)}, bf16[64,1152]{1,0:T(8,128)(2,1)S(1)}, u32[]{:S(2)}, u32[]{:S(2)}) collective-permute-start(bf16[64,1152]{1,0:T(8,128)(2,1)S(1)} %slice_bitcast_fusion.2), channel_id=1, source_target_pairs={{0,12},{4,0},{8,4},{12,8},{1,13},{5,1},{9,5},{13,9},{2,14},{6,2},{... | collective-permute-start | bytes 442376 | tf_op jit(solution)/shard_map/ppermute | solution.py:16
  113.4 12.0 %collective-permute-start.18 = (bf16[2,64,2048]{2,1,0:T(8,128)(2,1)S(1)}, bf16[2,64,2048]{2,1,0:T(8,128)(2,1)S(1)}, u32[]{:S(2)}, u32[]{:S(2)}) collective-permute-start(bf16[2,64,2048]{2,1,0:T(8,128)(2,1)S(1)} %pad_maximum_fusion.10), channel_id=1, source_target_pairs={{0,4},{4,8},{8,12},{12,0},{1,5},{5,9},{9,13},{13,1},{2,6},{6,10},{... | collective-permute-start | bytes 1572872 | tf_op jit(solution)/shard_map/ppermute | solution.py:16
  113.4 12.1 %collective-permute-start.19 = (bf16[2,64,2048]{2,1,0:T(8,128)(2,1)S(1)}, bf16[2,64,2048]{2,1,0:T(8,128)(2,1)S(1)}, u32[]{:S(2)}, u32[]{:S(2)}) collective-permute-start(bf16[2,64,2048]{2,1,0:T(8,128)(2,1)S(1)} %pad_maximum_fusion.10), channel_id=1, source_target_pairs={{0,12},{4,0},{8,4},{12,8},{1,13},{5,1},{9,5},{13,9},{2,14},{6,2},{... | collective-permute-start | bytes 1572872 | tf_op jit(solution)/shard_map/ppermute | solution.py:16
  123.0 20.5 %collective-permute-start.31 = (bf16[512,1024]{1,0:T(8,128)(2,1)S(1)}, bf16[512,1024]{1,0:T(8,128)(2,1)S(1)}, u32[]{:S(2)}, u32[]{:S(2)}) collective-permute-start(bf16[512,1024]{1,0:T(8,128)(2,1)S(1)} %add_convert_fusion), channel_id=1, source_target_pairs={{0,64},{64,0},{1,65},{65,1},{2,66},{66,2},{3,67},{67,3},{4,68},{68... | collective-permute-start | bytes 3145736 | tf_op jit(solution)/shard_map/ppermute | solution.py:16
  125.5 9.7 %collective-permute-start.20 = (bf16[64,2048]{1,0:T(8,128)(2,1)S(1)}, bf16[64,2048]{1,0:T(8,128)(2,1)S(1)}, u32[]{:S(2)}, u32[]{:S(2)}) collective-permute-start(bf16[64,2048]{1,0:T(8,128)(2,1)S(1)} %slice_bitcast_fusion.1), channel_id=1, source_target_pairs={{0,4},{4,8},{8,12},{12,0},{1,5},{5,9},{9,13},{13,1},{2,6},{6,10},{... | collective-permute-start | bytes 786440 | tf_op jit(solution)/shard_map/ppermute | solution.py:16
  125.6 9.6 %collective-permute-start.21 = (bf16[64,2048]{1,0:T(8,128)(2,1)S(1)}, bf16[64,2048]{1,0:T(8,128)(2,1)S(1)}, u32[]{:S(2)}, u32[]{:S(2)}) collective-permute-start(bf16[64,2048]{1,0:T(8,128)(2,1)S(1)} %slice_bitcast_fusion), channel_id=1, source_target_pairs={{0,12},{4,0},{8,4},{12,8},{1,13},{5,1},{9,5},{13,9},{2,14},{6,2},{... | collective-permute-start | bytes 786440 | tf_op jit(solution)/shard_map/ppermute | solution.py:16
  144.6 12.5 %collective-permute-start.33 = (bf16[512,512]{1,0:T(8,128)(2,1)S(1)}, bf16[512,512]{1,0:T(8,128)(2,1)S(1)}, u32[]{:S(2)}, u32[]{:S(2)}) collective-permute-start(bf16[512,512]{1,0:T(8,128)(2,1)S(1)} %slice.174), channel_id=1, source_target_pairs={{0,1},{1,0},{2,3},{3,2},{4,5},{5,4},{6,7},{7,6},{8,9},{9,8},{10,11... | collective-permute-start | bytes 1572872 | tf_op jit(solution)/shard_map/ppermute | solution.py:16
  (32 other events, 180.4 us)

commit v7 on v6

--- a/solution.py
+++ b/solution.py
@@ -140,7 +140,8 @@
     got_far, low_near = lax.optimization_barrier((got_far, low_near))
     x = lax.axis_index("x")
     first = lax.axis_index("yl") == 0
-    here = place(x, low_near, *[shift(low_near, "x", step) for step in (1, 2, 3)])
+    opposite = shift(low_near, "x", 2)
+    here = place(x, low_near, shift(low_near, "x", 1), opposite, shift(low_near, "x", 3))
     there = shift(here, "yl", 1)
     gram_near = jnp.stack([jnp.where(first, here, there), jnp.where(first, there, here)], axis=1)
     gram_near = gram_near.reshape(512, 1024)

time: 159 us -> 159 us (level)
  no operation moved by 1% of the time
where the time goes in v7:
time: 159 us; the launch traced here: 158 us
  starting transfers between devices  68.7 us (43%)
  waiting for transfers between devices  50.6 us (32%)
  other arithmetic  18 us (11%)
  matrix products  13.7 us (9%)
  local copies, waits for them, and re-layouts  5.77 us (4%)
    ppermute x27, starting transfers between devices, shift(): lax.ppermute(value, axis, [(i, (i + step) % size) for i in range(size)])  47 us
    ppermute x27, waiting for transfers between devices, shift(): lax.ppermute(value, axis, [(i, (i + step) % size) for i in range(size)])  25.1 us
    all_to_all x2, waiting for transfers between devices, send_gram(): return lax.all_to_all(pieces, ('x', 'yl'), 0, 0)  12.2 us
    all_to_all x2, starting transfers between devices, send_gram(): return lax.all_to_all(pieces, ('x', 'yl'), 0, 0)  8.26 us
    ppermute x6, waiting for transfers between devices, swap(): lax.ppermute(value, axis, [(i, i ^ mask) for i in range(COUNT[axis])])  7.44 us
    ppermute x6, starting transfers between devices, swap(): lax.ppermute(value, axis, [(i, i ^ mask) for i in range(COUNT[axis])])  6.51 us
    all_to_all x1, waiting for transfers between devices, body(): got_self = lax.all_to_all(part, 'x', 0, 0)  5.88 us
    dot_general x4, matrix products, nt(): lax.dot_general(lhs, rhs, (((1,), (1,)), ((), ())), preferred_element_typ...  5.87 us
  transfers between devices with their start and end apart: 38, of which 16 were waited for; matrix products, arithmetic and copies ran while one was open for 20% of the time, Pallas kernels for 0%

profile of v7, /device:TPU:1, one launch (start us, length us, event | category | flops | bytes accessed | tf_op | source)
XLA Modules:
  0.0 158.1 jit_solution(12178969716130360551)
XLA Ops:
  7.8 2.2 %collective-permute-start.3 = (f32[2,1024]{1,0:T(2,128)S(1)}, f32[2,1024]{1,0:T(2,128)S(1)}, u32[]{:S(2)}, u32[]{:S(2)}) collective-permute-start(f32[2,1024]{1,0:T(2,128)S(1)} %pad_maximum_fusion.13), channel_id=1, source_target_pairs={{0,48},{16,0},{32,16},{48,32},{1,49},{17,1},{33,17},{49,33},{2,50}... | collective-permute-start | bytes 24584 | tf_op jit(solution)/shard_map/ppermute | solution.py:16
  14.1 3.0 %collective-permute-start.5 = (f32[2,1024]{1,0:T(2,128)S(1)}, f32[2,1024]{1,0:T(2,128)S(1)}, u32[]{:S(2)}, u32[]{:S(2)}) collective-permute-start(f32[2,1024]{1,0:T(2,128)S(1)} %pad_maximum_fusion.14), channel_id=1, source_target_pairs={{0,64},{64,0},{1,65},{65,1},{2,66},{66,2},{3,67},{67,3},{4,68},{68... | collective-permute-start | bytes 24584 | tf_op jit(solution)/shard_map/ppermute | solution.py:24
  24.0 4.2 %all-to-all-start = ((bf16[4,128,512]{2,1,0:T(8,128)(2,1)}), bf16[4,128,512]{2,1,0:T(8,128)(2,1)}, u32[]{:S(2)}, u32[]{:S(2)}) async-start(bf16[4,128,512]{2,1,0:T(8,128)(2,1)} %bitcast.107), calls=%async_computation | async-start | bytes 1048576 | tf_op jit(solution)/shard_map/all_to_all | solution.py:121
  29.6 5.9 %all-to-all-done = bf16[4,128,512]{2,1,0:T(8,128)(2,1)} async-done(((bf16[4,128,512]{2,1,0:T(8,128)(2,1)}), bf16[4,128,512]{2,1,0:T(8,128)(2,1)}, u32[]{:S(2)}, u32[]{:S(2)}) %all-to-all-start) | async-done | bytes 524320 | tf_op jit(solution)/shard_map/all_to_all | solution.py:121
  35.5 5.0 %collective-permute-done.7 = bf16[512,1024]{1,0:T(8,128)(2,1)S(1)} collective-permute-done((bf16[512,1024]{1,0:T(8,128)(2,1)}, bf16[512,1024]{1,0:T(8,128)(2,1)S(1)}, u32[]{:S(2)}, u32[]{:S(2)}) %collective-permute-start.7) | collective-permute-done | bytes 1048608 | tf_op jit(solution)/shard_map/ppermute | solution.py:16
  40.5 2.5 %collective-permute-done.6 = bf16[512,1024]{1,0:T(8,128)(2,1)} collective-permute-done((bf16[512,1024]{1,0:T(8,128)(2,1)}, bf16[512,1024]{1,0:T(8,128)(2,1)}, u32[]{:S(2)}, u32[]{:S(2)}) %collective-permute-start.6) | collective-permute-done | bytes 1048608 | tf_op jit(solution)/shard_map/ppermute | solution.py:16
  48.1 4.0 %all-to-all-start.1 = ((bf16[8,64,1536]{2,1,0:T(8,128)(2,1)}), bf16[8,64,1536]{2,1,0:T(8,128)(2,1)S(1)}, u32[]{:S(2)}, u32[]{:S(2)}) async-start(bf16[8,64,1536]{2,1,0:T(8,128)(2,1)} %pad_maximum_fusion.2), calls=%async_computation.1 | async-start | bytes 3145728 | tf_op jit(solution)/shard_map/all_to_all | solution.py:38
  54.1 2.4 %collective-permute-start.11 = (bf16[256,1024]{1,0:T(8,128)(2,1)S(1)}, bf16[256,1024]{1,0:T(8,128)(2,1)S(1)}, u32[]{:S(2)}, u32[]{:S(2)}) collective-permute-start(bf16[256,1024]{1,0:T(8,128)(2,1)S(1)} %slice.160), channel_id=1, source_target_pairs={{0,48},{16,0},{32,16},{48,32},{1,49},{17,1},{33,17},{49,33},{2,50}... | collective-permute-start | bytes 1572872 | tf_op jit(solution)/shard_map/ppermute | solution.py:16
  59.3 4.9 %collective-permute-done.10 = bf16[256,1024]{1,0:T(8,128)(2,1)S(1)} collective-permute-done((bf16[256,1024]{1,0:T(8,128)(2,1)S(1)}, bf16[256,1024]{1,0:T(8,128)(2,1)S(1)}, u32[]{:S(2)}, u32[]{:S(2)}) %collective-permute-start.10) | collective-permute-done | bytes 524320 | tf_op jit(solution)/shard_map/ppermute | solution.py:16
  65.3 2.3 %convolution_convert_fusion.1 = bf16[1024,512]{1,0:T(8,128)(2,1)} fusion(bf16[1024,1024]{1,0:T(8,128)(2,1)S(1)} %bitcast.103, bf16[256,1024]{1,0:T(8,128)(2,1)S(1)} %get-tuple-element.91, bf16[256,1024]{1,0:T(8,128)(2,1)S(1)} %get-tuple-element.90), kind=kOutput, calls=%fused_computation.36 | convolution fusion | flops 1076363264 | bytes 4194304 | tf_op jit(solution)/shard_map/dot_general | solution.py:33
  67.6 4.2 %all-to-all-done.1 = bf16[8,64,1536]{2,1,0:T(8,128)(2,1)S(1)} async-done(((bf16[8,64,1536]{2,1,0:T(8,128)(2,1)}), bf16[8,64,1536]{2,1,0:T(8,128)(2,1)S(1)}, u32[]{:S(2)}, u32[]{:S(2)}) %all-to-all-start.1) | async-done | bytes 1572896 | tf_op jit(solution)/shard_map/all_to_all | solution.py:38
  71.8 4.2 %all-to-all-start.2 = ((bf16[8,128,512]{2,1,0:T(8,128)(2,1)}), bf16[8,128,512]{2,1,0:T(8,128)(2,1)}, u32[]{:S(2)}, u32[]{:S(2)}) async-start(bf16[8,128,512]{2,1,0:T(8,128)(2,1)} %bitcast.105), calls=%async_computation.2 | async-start | bytes 2097152 | tf_op jit(solution)/shard_map/all_to_all | solution.py:38
  80.4 8.0 %all-to-all-done.2 = bf16[8,128,512]{2,1,0:T(8,128)(2,1)} async-done(((bf16[8,128,512]{2,1,0:T(8,128)(2,1)}), bf16[8,128,512]{2,1,0:T(8,128)(2,1)}, u32[]{:S(2)}, u32[]{:S(2)}) %all-to-all-start.2) | async-done | bytes 1048608 | tf_op jit(solution)/shard_map/all_to_all | solution.py:38
  94.4 2.3 %collective-permute-start.15 = (bf16[64,1024]{1,0:T(8,128)(2,1)S(1)}, bf16[64,1024]{1,0:T(8,128)(2,1)S(1)}, u32[]{:S(2)}, u32[]{:S(2)}) collective-permute-start(bf16[64,1024]{1,0:T(8,128)(2,1)S(1)} %pad_maximum_fusion.12), channel_id=1, source_target_pairs={{0,2},{2,0},{1,3},{3,1},{4,6},{6,4},{5,7},{7,5},{8,10},{10,8},{9,1... | collective-permute-start | bytes 393224 | tf_op jit(solution)/shard_map/ppermute | solution.py:16
  99.5 2.7 %collective-permute-start.26 = (bf16[2,64,1152]{2,1,0:T(8,128)(2,1)S(1)}, bf16[2,64,1152]{2,1,0:T(8,128)(2,1)S(1)}, u32[]{:S(2)}, u32[]{:S(2)}) collective-permute-start(bf16[2,64,1152]{2,1,0:T(8,128)(2,1)S(1)} %maximum_maximum_fusion), channel_id=1, source_target_pairs={{0,12},{4,0},{8,4},{12,8},{1,13},{5,1},{9,5},{13,9},{2,14},{6,2},{... | collective-permute-start | bytes 884744 | tf_op jit(solution)/shard_map/ppermute | solution.py:16
  106.4 2.7 %collective-permute-start.27 = (bf16[64,1152]{1,0:T(8,128)(2,1)S(1)}, bf16[64,1152]{1,0:T(8,128)(2,1)S(1)}, u32[]{:S(2)}, u32[]{:S(2)}) collective-permute-start(bf16[64,1152]{1,0:T(8,128)(2,1)S(1)} %slice_bitcast_fusion.2), channel_id=1, source_target_pairs={{0,12},{4,0},{8,4},{12,8},{1,13},{5,1},{9,5},{13,9},{2,14},{6,2},{... | collective-permute-start | bytes 442376 | tf_op jit(solution)/shard_map/ppermute | solution.py:16
  109.2 4.2 %collective-permute-done.17 = bf16[64,1152]{1,0:T(8,128)(2,1)S(1)} collective-permute-done((bf16[64,1152]{1,0:T(8,128)(2,1)S(1)}, bf16[64,1152]{1,0:T(8,128)(2,1)S(1)}, u32[]{:S(2)}, u32[]{:S(2)}) %collective-permute-start.17) | collective-permute-done | bytes 147488 | tf_op jit(solution)/shard_map/ppermute | solution.py:16
  113.4 2.7 %collective-permute-start.19 = (bf16[2,64,2048]{2,1,0:T(8,128)(2,1)S(1)}, bf16[2,64,2048]{2,1,0:T(8,128)(2,1)S(1)}, u32[]{:S(2)}, u32[]{:S(2)}) collective-permute-start(bf16[2,64,2048]{2,1,0:T(8,128)(2,1)S(1)} %pad_maximum_fusion.10), channel_id=1, source_target_pairs={{0,12},{4,0},{8,4},{12,8},{1,13},{5,1},{9,5},{13,9},{2,14},{6,2},{... | collective-permute-start | bytes 1572872 | tf_op jit(solution)/shard_map/ppermute | solution.py:16
  123.0 2.4 %collective-permute-start.31 = (bf16[512,1024]{1,0:T(8,128)(2,1)S(1)}, bf16[512,1024]{1,0:T(8,128)(2,1)S(1)}, u32[]{:S(2)}, u32[]{:S(2)}) collective-permute-start(bf16[512,1024]{1,0:T(8,128)(2,1)S(1)} %add_convert_fusion), channel_id=1, source_target_pairs={{0,64},{64,0},{1,65},{65,1},{2,66},{66,2},{3,67},{67,3},{4,68},{68... | collective-permute-start | bytes 3145736 | tf_op jit(solution)/shard_map/ppermute | solution.py:16
  125.6 2.7 %collective-permute-start.21 = (bf16[64,2048]{1,0:T(8,128)(2,1)S(1)}, bf16[64,2048]{1,0:T(8,128)(2,1)S(1)}, u32[]{:S(2)}, u32[]{:S(2)}) collective-permute-start(bf16[64,2048]{1,0:T(8,128)(2,1)S(1)} %slice_bitcast_fusion), channel_id=1, source_target_pairs={{0,12},{4,0},{8,4},{12,8},{1,13},{5,1},{9,5},{13,9},{2,14},{6,2},{... | collective-permute-start | bytes 786440 | tf_op jit(solution)/shard_map/ppermute | solution.py:16
  129.7 2.7 %collective-permute-done.30 = f32[8,128]{1,0:T(8,128)S(1)} collective-permute-done((f32[8,128]{1,0:T(8,128)S(1)}, f32[8,128]{1,0:T(8,128)S(1)}, u32[]{:S(2)}, u32[]{:S(2)}) %collective-permute-start.30) | collective-permute-done | bytes 4128 | tf_op jit(solution)/shard_map/ppermute | solution.py:24
  132.4 2.7 %collective-permute-done.20 = bf16[64,2048]{1,0:T(8,128)(2,1)S(1)} collective-permute-done((bf16[64,2048]{1,0:T(8,128)(2,1)S(1)}, bf16[64,2048]{1,0:T(8,128)(2,1)S(1)}, u32[]{:S(2)}, u32[]{:S(2)}) %collective-permute-start.20) | collective-permute-done | bytes 262176 | tf_op jit(solution)/shard_map/ppermute | solution.py:16
  140.2 3.3 %collective-permute-done.32 = f32[8,128]{1,0:T(8,128)S(1)} collective-permute-done((f32[8,128]{1,0:T(8,128)S(1)}, f32[8,128]{1,0:T(8,128)S(1)}, u32[]{:S(2)}, u32[]{:S(2)}) %collective-permute-start.32) | collective-permute-done | bytes 4128 | tf_op jit(solution)/shard_map/ppermute | solution.py:24
  144.6 10.3 %collective-permute-start.33 = (bf16[512,512]{1,0:T(8,128)(2,1)S(1)}, bf16[512,512]{1,0:T(8,128)(2,1)S(1)}, u32[]{:S(2)}, u32[]{:S(2)}) collective-permute-start(bf16[512,512]{1,0:T(8,128)(2,1)S(1)} %slice.174), channel_id=1, source_target_pairs={{0,1},{1,0},{2,3},{3,2},{4,5},{5,4},{6,7},{7,6},{8,9},{9,8},{10,11... | collective-permute-start | bytes 1572872 | tf_op jit(solution)/shard_map/ppermute | solution.py:16
  (177 shorter events, 65.2 us)
Async XLA Ops:
  17.6 22.9 %collective-permute-start.7 = (bf16[512,1024]{1,0:T(8,128)(2,1)}, bf16[512,1024]{1,0:T(8,128)(2,1)S(1)}, u32[]{:S(2)}, u32[]{:S(2)}) collective-permute-start(bf16[512,1024]{1,0:T(8,128)(2,1)} %pad_maximum_fusion.5), channel_id=1, source_target_pairs={{0,48},{16,0},{32,16},{48,32},{1,49},{17,1},{33,17},{49,33},{2,50}... | collective-permute-start | bytes 3145736 | tf_op jit(solution)/shard_map/ppermute | solution.py:16
  19.0 23.9 %collective-permute-start.6 = (bf16[512,1024]{1,0:T(8,128)(2,1)}, bf16[512,1024]{1,0:T(8,128)(2,1)}, u32[]{:S(2)}, u32[]{:S(2)}) collective-permute-start(bf16[512,1024]{1,0:T(8,128)(2,1)} %pad_maximum_fusion.5), channel_id=1, source_target_pairs={{0,64},{64,0},{1,65},{65,1},{2,66},{66,2},{3,67},{67,3},{4,68},{68... | collective-permute-start | bytes 3145736 | tf_op jit(solution)/shard_map/ppermute | solution.py:16
  24.0 11.5 %all-to-all-start = ((bf16[4,128,512]{2,1,0:T(8,128)(2,1)}), bf16[4,128,512]{2,1,0:T(8,128)(2,1)}, u32[]{:S(2)}, u32[]{:S(2)}) async-start(bf16[4,128,512]{2,1,0:T(8,128)(2,1)} %bitcast.107), calls=%async_computation | async-start | bytes 1048576 | tf_op jit(solution)/shard_map/all_to_all | solution.py:121
  28.9 23.5 %collective-permute-start.9 = (bf16[512,1024]{1,0:T(8,128)(2,1)}, bf16[512,1024]{1,0:T(8,128)(2,1)}, u32[]{:S(2)}, u32[]{:S(2)}) collective-permute-start(bf16[512,1024]{1,0:T(8,128)(2,1)} %pad_maximum_fusion.5), channel_id=1, source_target_pairs={{0,16},{16,32},{32,48},{48,0},{1,17},{17,33},{33,49},{49,1},{2,18}... | collective-permute-start | bytes 3145736 | tf_op jit(solution)/shard_map/ppermute | solution.py:16
  48.1 23.7 %all-to-all-start.1 = ((bf16[8,64,1536]{2,1,0:T(8,128)(2,1)}), bf16[8,64,1536]{2,1,0:T(8,128)(2,1)S(1)}, u32[]{:S(2)}, u32[]{:S(2)}) async-start(bf16[8,64,1536]{2,1,0:T(8,128)(2,1)} %pad_maximum_fusion.2), calls=%async_computation.1 | async-start | bytes 3145728 | tf_op jit(solution)/shard_map/all_to_all | solution.py:38
  53.6 10.7 %collective-permute-start.10 = (bf16[256,1024]{1,0:T(8,128)(2,1)S(1)}, bf16[256,1024]{1,0:T(8,128)(2,1)S(1)}, u32[]{:S(2)}, u32[]{:S(2)}) collective-permute-start(bf16[256,1024]{1,0:T(8,128)(2,1)S(1)} %slice.159), channel_id=1, source_target_pairs={{0,16},{16,32},{32,48},{48,0},{1,17},{17,33},{33,49},{49,1},{2,18}... | collective-permute-start | bytes 1572872 | tf_op jit(solution)/shard_map/ppermute | solution.py:16
  54.1 10.2 %collective-permute-start.11 = (bf16[256,1024]{1,0:T(8,128)(2,1)S(1)}, bf16[256,1024]{1,0:T(8,128)(2,1)S(1)}, u32[]{:S(2)}, u32[]{:S(2)}) collective-permute-start(bf16[256,1024]{1,0:T(8,128)(2,1)S(1)} %slice.160), channel_id=1, source_target_pairs={{0,48},{16,0},{32,16},{48,32},{1,49},{17,1},{33,17},{49,33},{2,50}... | collective-permute-start | bytes 1572872 | tf_op jit(solution)/shard_map/ppermute | solution.py:16
  57.6 18.4 %collective-permute-start.8 = (bf16[64,512]{1,0:T(8,128)(2,1)S(1)}, bf16[64,512]{1,0:T(8,128)(2,1)S(1)}, u32[]{:S(2)}, u32[]{:S(2)}) collective-permute-start(bf16[64,512]{1,0:T(8,128)(2,1)S(1)} %select_convert_fusion), channel_id=1, source_target_pairs={{0,2},{2,0},{1,3},{3,1},{4,6},{6,4},{5,7},{7,5},{8,10},{10,8},{9,1... | collective-permute-start | bytes 196616 | tf_op jit(solution)/shard_map/ppermute | solution.py:16
  71.8 16.6 %all-to-all-start.2 = ((bf16[8,128,512]{2,1,0:T(8,128)(2,1)}), bf16[8,128,512]{2,1,0:T(8,128)(2,1)}, u32[]{:S(2)}, u32[]{:S(2)}) async-start(bf16[8,128,512]{2,1,0:T(8,128)(2,1)} %bitcast.105), calls=%async_computation.2 | async-start | bytes 2097152 | tf_op jit(solution)/shard_map/all_to_all | solution.py:38
  77.4 17.0 %collective-permute-start.14 = (bf16[64,512]{1,0:T(8,128)(2,1)}, bf16[64,512]{1,0:T(8,128)(2,1)S(1)}, u32[]{:S(2)}, u32[]{:S(2)}) collective-permute-start(bf16[64,512]{1,0:T(8,128)(2,1)} %slice.163), channel_id=1, source_target_pairs={{0,80},{16,96},{32,112},{48,64},{64,16},{80,32},{96,48},{112,0},{1... | collective-permute-start | bytes 196616 | tf_op jit(solution)/shard_map/ppermute | solution.py:29
  78.9 18.5 %collective-permute-start.12 = (bf16[64,512]{1,0:T(8,128)(2,1)S(1)}, bf16[64,512]{1,0:T(8,128)(2,1)S(1)}, u32[]{:S(2)}, u32[]{:S(2)}) collective-permute-start(bf16[64,512]{1,0:T(8,128)(2,1)S(1)} %get-tuple-element.81), channel_id=1, source_target_pairs={{0,16},{16,32},{32,48},{48,0},{64,80},{80,96},{96,112},{112,64},{1... | collective-permute-start | bytes 196616 | tf_op jit(solution)/shard_map/ppermute | solution.py:29
  88.4 11.2 %collective-permute-start.22 = (bf16[64,1024]{1,0:T(8,128)(2,1)S(1)}, bf16[64,1024]{1,0:T(8,128)(2,1)S(1)}, u32[]{:S(2)}, u32[]{:S(2)}) collective-permute-start(bf16[64,1024]{1,0:T(8,128)(2,1)S(1)} %convert_element_type.148), channel_id=1, source_target_pairs={{0,4},{4,8},{8,12},{12,0},{1,5},{5,9},{9,13},{13,1},{2,6},{6,10},{... | collective-permute-start | bytes 393224 | tf_op jit(solution)/shard_map/ppermute | solution.py:16
  88.9 13.3 %collective-permute-start.23 = (bf16[64,1024]{1,0:T(8,128)(2,1)S(1)}, bf16[64,1024]{1,0:T(8,128)(2,1)S(1)}, u32[]{:S(2)}, u32[]{:S(2)}) collective-permute-start(bf16[64,1024]{1,0:T(8,128)(2,1)S(1)} %convert_element_type.148), channel_id=1, source_target_pairs={{0,8},{4,12},{8,0},{12,4},{1,9},{5,13},{9,1},{13,5},{2,10},{6,14},... | collective-permute-start | bytes 393224 | tf_op jit(solution)/shard_map/ppermute | solution.py:16
  90.9 11.4 %collective-permute-start.24 = (bf16[64,1024]{1,0:T(8,128)(2,1)S(1)}, bf16[64,1024]{1,0:T(8,128)(2,1)S(1)}, u32[]{:S(2)}, u32[]{:S(2)}) collective-permute-start(bf16[64,1024]{1,0:T(8,128)(2,1)S(1)} %convert_element_type.148), channel_id=1, source_target_pairs={{0,12},{4,0},{8,4},{12,8},{1,13},{5,1},{9,5},{13,9},{2,14},{6,2},{... | collective-permute-start | bytes 393224 | tf_op jit(solution)/shard_map/ppermute | solution.py:16
  97.4 7.0 %collective-permute-start.13 = (bf16[64,2048]{1,0:T(8,128)(2,1)S(1)}, bf16[64,2048]{1,0:T(8,128)(2,1)S(1)}, u32[]{:S(2)}, u32[]{:S(2)}) collective-permute-start(bf16[64,2048]{1,0:T(8,128)(2,1)S(1)} %pad_maximum_fusion.11), channel_id=1, source_target_pairs={{0,2},{2,0},{1,3},{3,1},{4,6},{6,4},{5,7},{7,5},{8,10},{10,8},{9,1... | collective-permute-start | bytes 786440 | tf_op jit(solution)/shard_map/ppermute | solution.py:16
  102.3 14.2 %collective-permute-start.25 = (bf16[4,64,1024]{2,1,0:T(8,128)(2,1)S(1)}, bf16[4,64,1024]{2,1,0:T(8,128)(2,1)S(1)}, u32[]{:S(2)}, u32[]{:S(2)}) collective-permute-start(bf16[4,64,1024]{2,1,0:T(8,128)(2,1)S(1)} %bitcast_dynamic-update-slice_fusion.6), channel_id=1, source_target_pairs={{0,2},{2,0},{1,3},{3,1},{4,6},{6,4},{5,7},{7,5},{8,10},{10,8},{9,1... | collective-permute-start | bytes 1572872 | tf_op jit(solution)/shard_map/ppermute | solution.py:16
  106.3 7.1 %collective-permute-start.17 = (bf16[64,1152]{1,0:T(8,128)(2,1)S(1)}, bf16[64,1152]{1,0:T(8,128)(2,1)S(1)}, u32[]{:S(2)}, u32[]{:S(2)}) collective-permute-start(bf16[64,1152]{1,0:T(8,128)(2,1)S(1)} %slice_bitcast_fusion.3), channel_id=1, source_target_pairs={{0,4},{4,8},{8,12},{12,0},{1,5},{5,9},{9,13},{13,1},{2,6},{6,10},{... | collective-permute-start | bytes 442376 | tf_op jit(solution)/shard_map/ppermute | solution.py:16
  106.4 9.7 %collective-permute-start.27 = (bf16[64,1152]{1,0:T(8,128)(2,1)S(1)}, bf16[64,1152]{1,0:T(8,128)(2,1)S(1)}, u32[]{:S(2)}, u32[]{:S(2)}) collective-permute-start(bf16[64,1152]{1,0:T(8,128)(2,1)S(1)} %slice_bitcast_fusion.2), channel_id=1, source_target_pairs={{0,12},{4,0},{8,4},{12,8},{1,13},{5,1},{9,5},{13,9},{2,14},{6,2},{... | collective-permute-start | bytes 442376 | tf_op jit(solution)/shard_map/ppermute | solution.py:16
  113.4 12.0 %collective-permute-start.18 = (bf16[2,64,2048]{2,1,0:T(8,128)(2,1)S(1)}, bf16[2,64,2048]{2,1,0:T(8,128)(2,1)S(1)}, u32[]{:S(2)}, u32[]{:S(2)}) collective-permute-start(bf16[2,64,2048]{2,1,0:T(8,128)(2,1)S(1)} %pad_maximum_fusion.10), channel_id=1, source_target_pairs={{0,4},{4,8},{8,12},{12,0},{1,5},{5,9},{9,13},{13,1},{2,6},{6,10},{... | collective-permute-start | bytes 1572872 | tf_op jit(solution)/shard_map/ppermute | solution.py:16
  113.4 12.1 %collective-permute-start.19 = (bf16[2,64,2048]{2,1,0:T(8,128)(2,1)S(1)}, bf16[2,64,2048]{2,1,0:T(8,128)(2,1)S(1)}, u32[]{:S(2)}, u32[]{:S(2)}) collective-permute-start(bf16[2,64,2048]{2,1,0:T(8,128)(2,1)S(1)} %pad_maximum_fusion.10), channel_id=1, source_target_pairs={{0,12},{4,0},{8,4},{12,8},{1,13},{5,1},{9,5},{13,9},{2,14},{6,2},{... | collective-permute-start | bytes 1572872 | tf_op jit(solution)/shard_map/ppermute | solution.py:16
  123.0 20.5 %collective-permute-start.31 = (bf16[512,1024]{1,0:T(8,128)(2,1)S(1)}, bf16[512,1024]{1,0:T(8,128)(2,1)S(1)}, u32[]{:S(2)}, u32[]{:S(2)}) collective-permute-start(bf16[512,1024]{1,0:T(8,128)(2,1)S(1)} %add_convert_fusion), channel_id=1, source_target_pairs={{0,64},{64,0},{1,65},{65,1},{2,66},{66,2},{3,67},{67,3},{4,68},{68... | collective-permute-start | bytes 3145736 | tf_op jit(solution)/shard_map/ppermute | solution.py:16
  125.5 9.7 %collective-permute-start.20 = (bf16[64,2048]{1,0:T(8,128)(2,1)S(1)}, bf16[64,2048]{1,0:T(8,128)(2,1)S(1)}, u32[]{:S(2)}, u32[]{:S(2)}) collective-permute-start(bf16[64,2048]{1,0:T(8,128)(2,1)S(1)} %slice_bitcast_fusion.1), channel_id=1, source_target_pairs={{0,4},{4,8},{8,12},{12,0},{1,5},{5,9},{9,13},{13,1},{2,6},{6,10},{... | collective-permute-start | bytes 786440 | tf_op jit(solution)/shard_map/ppermute | solution.py:16
  125.6 9.6 %collective-permute-start.21 = (bf16[64,2048]{1,0:T(8,128)(2,1)S(1)}, bf16[64,2048]{1,0:T(8,128)(2,1)S(1)}, u32[]{:S(2)}, u32[]{:S(2)}) collective-permute-start(bf16[64,2048]{1,0:T(8,128)(2,1)S(1)} %slice_bitcast_fusion), channel_id=1, source_target_pairs={{0,12},{4,0},{8,4},{12,8},{1,13},{5,1},{9,5},{13,9},{2,14},{6,2},{... | collective-permute-start | bytes 786440 | tf_op jit(solution)/shard_map/ppermute | solution.py:16
  144.6 12.5 %collective-permute-start.33 = (bf16[512,512]{1,0:T(8,128)(2,1)S(1)}, bf16[512,512]{1,0:T(8,128)(2,1)S(1)}, u32[]{:S(2)}, u32[]{:S(2)}) collective-permute-start(bf16[512,512]{1,0:T(8,128)(2,1)S(1)} %slice.174), channel_id=1, source_target_pairs={{0,1},{1,0},{2,3},{3,2},{4,5},{5,4},{6,7},{7,6},{8,9},{9,8},{10,11... | collective-permute-start | bytes 1572872 | tf_op jit(solution)/shard_map/ppermute | solution.py:16
  (32 other events, 180.4 us)

commit v8 on v6

--- a/solution.py
+++ b/solution.py
@@ -58,7 +58,7 @@
     rows = jnp.zeros((4, 2, 64, n), BF16)
     for step, block in ((0, both), (3, prev), (1, succ), (2, jnp.stack([far0, far1]))):
         rows = lax.dynamic_update_slice_in_dim(rows, block[None], (x + step) % 4, 0)
-    return rows.reshape(512, n), prev, far0
+    return rows.reshape(512, n), prev, far1
 
 
 def place(x, own, prev, opposite, succ):
@@ -140,7 +140,8 @@
     got_far, low_near = lax.optimization_barrier((got_far, low_near))
     x = lax.axis_index("x")
     first = lax.axis_index("yl") == 0
-    here = place(x, low_near, *[shift(low_near, "x", step) for step in (1, 2, 3)])
+    opposite, succ = shift(low_near, "x", 2), shift(low_near, "x", 3)
+    here = place(x, low_near, shift(low_near, "x", 1), opposite, succ)
     there = shift(here, "yl", 1)
     gram_near = jnp.stack([jnp.where(first, here, there), jnp.where(first, there, here)], axis=1)
     gram_near = gram_near.reshape(512, 1024)

time: 159 us -> 159 us (level)
  transfers between devices with their start and end apart: 38 -> 38, of which waited for: 16 -> 16; matrix products, arithmetic and copies ran while one was open for 20% -> 19% of each run, Pallas kernels for 0% -> 0%
where the time goes in v8:
time: 159 us; the launch traced here: 158 us
  starting transfers between devices  69.5 us (44%)
  waiting for transfers between devices  49.8 us (31%)
  other arithmetic  18 us (11%)
  matrix products  13.7 us (9%)
  local copies, waits for them, and re-layouts  5.77 us (4%)
    ppermute x27, starting transfers between devices, shift(): lax.ppermute(value, axis, [(i, (i + step) % size) for i in range(size)])  47.6 us
    ppermute x27, waiting for transfers between devices, shift(): lax.ppermute(value, axis, [(i, (i + step) % size) for i in range(size)])  24.2 us
    all_to_all x2, waiting for transfers between devices, send_gram(): return lax.all_to_all(pieces, ('x', 'yl'), 0, 0)  12.2 us
    all_to_all x2, starting transfers between devices, send_gram(): return lax.all_to_all(pieces, ('x', 'yl'), 0, 0)  8.26 us
    ppermute x6, waiting for transfers between devices, swap(): lax.ppermute(value, axis, [(i, i ^ mask) for i in range(COUNT[axis])])  7.52 us
    ppermute x6, starting transfers between devices, swap(): lax.ppermute(value, axis, [(i, i ^ mask) for i in range(COUNT[axis])])  6.76 us
    all_to_all x1, waiting for transfers between devices, body(): got_self = lax.all_to_all(part, 'x', 0, 0)  5.88 us
    dot_general x4, matrix products, nt(): lax.dot_general(lhs, rhs, (((1,), (1,)), ((), ())), preferred_element_typ...  5.87 us
  transfers between devices with their start and end apart: 38, of which 16 were waited for; matrix products, arithmetic and copies ran while one was open for 19% of the time, Pallas kernels for 0%

profile of v8, /device:TPU:1, one launch (start us, length us, event | category | flops | bytes accessed | tf_op | source)
XLA Modules:
  0.0 158.2 jit_solution(7424443909843922701)
XLA Ops:
  7.8 2.2 %collective-permute-start.3 = (f32[2,1024]{1,0:T(2,128)S(1)}, f32[2,1024]{1,0:T(2,128)S(1)}, u32[]{:S(2)}, u32[]{:S(2)}) collective-permute-start(f32[2,1024]{1,0:T(2,128)S(1)} %pad_maximum_fusion.13), channel_id=1, source_target_pairs={{0,48},{16,0},{32,16},{48,32},{1,49},{17,1},{33,17},{49,33},{2,50}... | collective-permute-start | bytes 24584 | tf_op jit(solution)/shard_map/ppermute | solution.py:16
  14.1 3.0 %collective-permute-start.5 = (f32[2,1024]{1,0:T(2,128)S(1)}, f32[2,1024]{1,0:T(2,128)S(1)}, u32[]{:S(2)}, u32[]{:S(2)}) collective-permute-start(f32[2,1024]{1,0:T(2,128)S(1)} %pad_maximum_fusion.14), channel_id=1, source_target_pairs={{0,64},{64,0},{1,65},{65,1},{2,66},{66,2},{3,67},{67,3},{4,68},{68... | collective-permute-start | bytes 24584 | tf_op jit(solution)/shard_map/ppermute | solution.py:24
  24.0 4.2 %all-to-all-start = ((bf16[4,128,512]{2,1,0:T(8,128)(2,1)}), bf16[4,128,512]{2,1,0:T(8,128)(2,1)}, u32[]{:S(2)}, u32[]{:S(2)}) async-start(bf16[4,128,512]{2,1,0:T(8,128)(2,1)} %bitcast.107), calls=%async_computation | async-start | bytes 1048576 | tf_op jit(solution)/shard_map/all_to_all | solution.py:121
  29.6 5.9 %all-to-all-done = bf16[4,128,512]{2,1,0:T(8,128)(2,1)} async-done(((bf16[4,128,512]{2,1,0:T(8,128)(2,1)}), bf16[4,128,512]{2,1,0:T(8,128)(2,1)}, u32[]{:S(2)}, u32[]{:S(2)}) %all-to-all-start) | async-done | bytes 524320 | tf_op jit(solution)/shard_map/all_to_all | solution.py:121
  35.5 5.0 %collective-permute-done.7 = bf16[512,1024]{1,0:T(8,128)(2,1)S(1)} collective-permute-done((bf16[512,1024]{1,0:T(8,128)(2,1)}, bf16[512,1024]{1,0:T(8,128)(2,1)S(1)}, u32[]{:S(2)}, u32[]{:S(2)}) %collective-permute-start.7) | collective-permute-done | bytes 1048608 | tf_op jit(solution)/shard_map/ppermute | solution.py:16
  40.5 2.5 %collective-permute-done.6 = bf16[512,1024]{1,0:T(8,128)(2,1)} collective-permute-done((bf16[512,1024]{1,0:T(8,128)(2,1)}, bf16[512,1024]{1,0:T(8,128)(2,1)}, u32[]{:S(2)}, u32[]{:S(2)}) %collective-permute-start.6) | collective-permute-done | bytes 1048608 | tf_op jit(solution)/shard_map/ppermute | solution.py:16
  48.1 4.0 %all-to-all-start.1 = ((bf16[8,64,1536]{2,1,0:T(8,128)(2,1)}), bf16[8,64,1536]{2,1,0:T(8,128)(2,1)S(1)}, u32[]{:S(2)}, u32[]{:S(2)}) async-start(bf16[8,64,1536]{2,1,0:T(8,128)(2,1)} %pad_maximum_fusion.2), calls=%async_computation.1 | async-start | bytes 3145728 | tf_op jit(solution)/shard_map/all_to_all | solution.py:38
  54.1 2.4 %collective-permute-start.11 = (bf16[256,1024]{1,0:T(8,128)(2,1)S(1)}, bf16[256,1024]{1,0:T(8,128)(2,1)S(1)}, u32[]{:S(2)}, u32[]{:S(2)}) collective-permute-start(bf16[256,1024]{1,0:T(8,128)(2,1)S(1)} %slice.160), channel_id=1, source_target_pairs={{0,48},{16,0},{32,16},{48,32},{1,49},{17,1},{33,17},{49,33},{2,50}... | collective-permute-start | bytes 1572872 | tf_op jit(solution)/shard_map/ppermute | solution.py:16
  59.3 4.9 %collective-permute-done.10 = bf16[256,1024]{1,0:T(8,128)(2,1)S(1)} collective-permute-done((bf16[256,1024]{1,0:T(8,128)(2,1)S(1)}, bf16[256,1024]{1,0:T(8,128)(2,1)S(1)}, u32[]{:S(2)}, u32[]{:S(2)}) %collective-permute-start.10) | collective-permute-done | bytes 524320 | tf_op jit(solution)/shard_map/ppermute | solution.py:16
  65.3 2.3 %convolution_convert_fusion.1 = bf16[1024,512]{1,0:T(8,128)(2,1)} fusion(bf16[1024,1024]{1,0:T(8,128)(2,1)S(1)} %bitcast.103, bf16[256,1024]{1,0:T(8,128)(2,1)S(1)} %get-tuple-element.91, bf16[256,1024]{1,0:T(8,128)(2,1)S(1)} %get-tuple-element.90), kind=kOutput, calls=%fused_computation.36 | convolution fusion | flops 1076363264 | bytes 4194304 | tf_op jit(solution)/shard_map/dot_general | solution.py:33
  67.6 4.2 %all-to-all-done.1 = bf16[8,64,1536]{2,1,0:T(8,128)(2,1)S(1)} async-done(((bf16[8,64,1536]{2,1,0:T(8,128)(2,1)}), bf16[8,64,1536]{2,1,0:T(8,128)(2,1)S(1)}, u32[]{:S(2)}, u32[]{:S(2)}) %all-to-all-start.1) | async-done | bytes 1572896 | tf_op jit(solution)/shard_map/all_to_all | solution.py:38
  71.8 4.2 %all-to-all-start.2 = ((bf16[8,128,512]{2,1,0:T(8,128)(2,1)}), bf16[8,128,512]{2,1,0:T(8,128)(2,1)}, u32[]{:S(2)}, u32[]{:S(2)}) async-start(bf16[8,128,512]{2,1,0:T(8,128)(2,1)} %bitcast.105), calls=%async_computation.2 | async-start | bytes 2097152 | tf_op jit(solution)/shard_map/all_to_all | solution.py:38
  80.4 8.0 %all-to-all-done.2 = bf16[8,128,512]{2,1,0:T(8,128)(2,1)} async-done(((bf16[8,128,512]{2,1,0:T(8,128)(2,1)}), bf16[8,128,512]{2,1,0:T(8,128)(2,1)}, u32[]{:S(2)}, u32[]{:S(2)}) %all-to-all-start.2) | async-done | bytes 1048608 | tf_op jit(solution)/shard_map/all_to_all | solution.py:38
  94.4 2.3 %collective-permute-start.15 = (bf16[64,1024]{1,0:T(8,128)(2,1)S(1)}, bf16[64,1024]{1,0:T(8,128)(2,1)S(1)}, u32[]{:S(2)}, u32[]{:S(2)}) collective-permute-start(bf16[64,1024]{1,0:T(8,128)(2,1)S(1)} %pad_maximum_fusion.12), channel_id=1, source_target_pairs={{0,2},{2,0},{1,3},{3,1},{4,6},{6,4},{5,7},{7,5},{8,10},{10,8},{9,1... | collective-permute-start | bytes 393224 | tf_op jit(solution)/shard_map/ppermute | solution.py:16
  99.5 2.7 %collective-permute-start.16 = (bf16[2,64,1152]{2,1,0:T(8,128)(2,1)S(1)}, bf16[2,64,1152]{2,1,0:T(8,128)(2,1)S(1)}, u32[]{:S(2)}, u32[]{:S(2)}) collective-permute-start(bf16[2,64,1152]{2,1,0:T(8,128)(2,1)S(1)} %maximum_maximum_fusion), channel_id=1, source_target_pairs={{0,12},{4,0},{8,4},{12,8},{1,13},{5,1},{9,5},{13,9},{2,14},{6,2},{... | collective-permute-start | bytes 884744 | tf_op jit(solution)/shard_map/ppermute | solution.py:16
  106.4 2.7 %collective-permute-start.17 = (bf16[64,1152]{1,0:T(8,128)(2,1)S(1)}, bf16[64,1152]{1,0:T(8,128)(2,1)S(1)}, u32[]{:S(2)}, u32[]{:S(2)}) collective-permute-start(bf16[64,1152]{1,0:T(8,128)(2,1)S(1)} %slice_bitcast_fusion.3), channel_id=1, source_target_pairs={{0,12},{4,0},{8,4},{12,8},{1,13},{5,1},{9,5},{13,9},{2,14},{6,2},{... | collective-permute-start | bytes 442376 | tf_op jit(solution)/shard_map/ppermute | solution.py:16
  109.2 3.5 %collective-permute-done.17 = bf16[64,1152]{1,0:T(8,128)(2,1)S(1)} collective-permute-done((bf16[64,1152]{1,0:T(8,128)(2,1)S(1)}, bf16[64,1152]{1,0:T(8,128)(2,1)S(1)}, u32[]{:S(2)}, u32[]{:S(2)}) %collective-permute-start.17) | collective-permute-done | bytes 147488 | tf_op jit(solution)/shard_map/ppermute | solution.py:16
  112.8 3.4 %collective-permute-start.19 = (bf16[2,64,2048]{2,1,0:T(8,128)(2,1)S(1)}, bf16[2,64,2048]{2,1,0:T(8,128)(2,1)S(1)}, u32[]{:S(2)}, u32[]{:S(2)}) collective-permute-start(bf16[2,64,2048]{2,1,0:T(8,128)(2,1)S(1)} %pad_maximum_fusion.10), channel_id=1, source_target_pairs={{0,12},{4,0},{8,4},{12,8},{1,13},{5,1},{9,5},{13,9},{2,14},{6,2},{... | collective-permute-start | bytes 1572872 | tf_op jit(solution)/shard_map/ppermute | solution.py:16
  123.4 2.5 %collective-permute-start.31 = (bf16[512,1024]{1,0:T(8,128)(2,1)S(1)}, bf16[512,1024]{1,0:T(8,128)(2,1)S(1)}, u32[]{:S(2)}, u32[]{:S(2)}) collective-permute-start(bf16[512,1024]{1,0:T(8,128)(2,1)S(1)} %add_convert_fusion), channel_id=1, source_target_pairs={{0,64},{64,0},{1,65},{65,1},{2,66},{66,2},{3,67},{67,3},{4,68},{68... | collective-permute-start | bytes 3145736 | tf_op jit(solution)/shard_map/ppermute | solution.py:16
  126.0 2.7 %collective-permute-start.21 = (bf16[64,2048]{1,0:T(8,128)(2,1)S(1)}, bf16[64,2048]{1,0:T(8,128)(2,1)S(1)}, u32[]{:S(2)}, u32[]{:S(2)}) collective-permute-start(bf16[64,2048]{1,0:T(8,128)(2,1)S(1)} %slice_bitcast_fusion), channel_id=1, source_target_pairs={{0,12},{4,0},{8,4},{12,8},{1,13},{5,1},{9,5},{13,9},{2,14},{6,2},{... | collective-permute-start | bytes 786440 | tf_op jit(solution)/shard_map/ppermute | solution.py:16
  130.2 2.7 %collective-permute-done.30 = f32[8,128]{1,0:T(8,128)S(1)} collective-permute-done((f32[8,128]{1,0:T(8,128)S(1)}, f32[8,128]{1,0:T(8,128)S(1)}, u32[]{:S(2)}, u32[]{:S(2)}) %collective-permute-start.30) | collective-permute-done | bytes 4128 | tf_op jit(solution)/shard_map/ppermute | solution.py:24
  132.9 2.5 %collective-permute-done.20 = bf16[64,2048]{1,0:T(8,128)(2,1)S(1)} collective-permute-done((bf16[64,2048]{1,0:T(8,128)(2,1)S(1)}, bf16[64,2048]{1,0:T(8,128)(2,1)S(1)}, u32[]{:S(2)}, u32[]{:S(2)}) %collective-permute-start.20) | collective-permute-done | bytes 262176 | tf_op jit(solution)/shard_map/ppermute | solution.py:16
  140.4 3.4 %collective-permute-done.32 = f32[8,128]{1,0:T(8,128)S(1)} collective-permute-done((f32[8,128]{1,0:T(8,128)S(1)}, f32[8,128]{1,0:T(8,128)S(1)}, u32[]{:S(2)}, u32[]{:S(2)}) %collective-permute-start.32) | collective-permute-done | bytes 4128 | tf_op jit(solution)/shard_map/ppermute | solution.py:24
  144.8 10.2 %collective-permute-start.33 = (bf16[512,512]{1,0:T(8,128)(2,1)S(1)}, bf16[512,512]{1,0:T(8,128)(2,1)S(1)}, u32[]{:S(2)}, u32[]{:S(2)}) collective-permute-start(bf16[512,512]{1,0:T(8,128)(2,1)S(1)} %slice.174), channel_id=1, source_target_pairs={{0,1},{1,0},{2,3},{3,2},{4,5},{5,4},{6,7},{7,6},{8,9},{9,8},{10,11... | collective-permute-start | bytes 1572872 | tf_op jit(solution)/shard_map/ppermute | solution.py:16
  (177 shorter events, 65.5 us)
Async XLA Ops:
  17.6 22.9 %collective-permute-start.7 = (bf16[512,1024]{1,0:T(8,128)(2,1)}, bf16[512,1024]{1,0:T(8,128)(2,1)S(1)}, u32[]{:S(2)}, u32[]{:S(2)}) collective-permute-start(bf16[512,1024]{1,0:T(8,128)(2,1)} %pad_maximum_fusion.5), channel_id=1, source_target_pairs={{0,48},{16,0},{32,16},{48,32},{1,49},{17,1},{33,17},{49,33},{2,50}... | collective-permute-start | bytes 3145736 | tf_op jit(solution)/shard_map/ppermute | solution.py:16
  19.0 23.9 %collective-permute-start.6 = (bf16[512,1024]{1,0:T(8,128)(2,1)}, bf16[512,1024]{1,0:T(8,128)(2,1)}, u32[]{:S(2)}, u32[]{:S(2)}) collective-permute-start(bf16[512,1024]{1,0:T(8,128)(2,1)} %pad_maximum_fusion.5), channel_id=1, source_target_pairs={{0,64},{64,0},{1,65},{65,1},{2,66},{66,2},{3,67},{67,3},{4,68},{68... | collective-permute-start | bytes 3145736 | tf_op jit(solution)/shard_map/ppermute | solution.py:16
  24.0 11.5 %all-to-all-start = ((bf16[4,128,512]{2,1,0:T(8,128)(2,1)}), bf16[4,128,512]{2,1,0:T(8,128)(2,1)}, u32[]{:S(2)}, u32[]{:S(2)}) async-start(bf16[4,128,512]{2,1,0:T(8,128)(2,1)} %bitcast.107), calls=%async_computation | async-start | bytes 1048576 | tf_op jit(solution)/shard_map/all_to_all | solution.py:121
  28.9 23.5 %collective-permute-start.9 = (bf16[512,1024]{1,0:T(8,128)(2,1)}, bf16[512,1024]{1,0:T(8,128)(2,1)}, u32[]{:S(2)}, u32[]{:S(2)}) collective-permute-start(bf16[512,1024]{1,0:T(8,128)(2,1)} %pad_maximum_fusion.5), channel_id=1, source_target_pairs={{0,16},{16,32},{32,48},{48,0},{1,17},{17,33},{33,49},{49,1},{2,18}... | collective-permute-start | bytes 3145736 | tf_op jit(solution)/shard_map/ppermute | solution.py:16
  48.1 23.7 %all-to-all-start.1 = ((bf16[8,64,1536]{2,1,0:T(8,128)(2,1)}), bf16[8,64,1536]{2,1,0:T(8,128)(2,1)S(1)}, u32[]{:S(2)}, u32[]{:S(2)}) async-start(bf16[8,64,1536]{2,1,0:T(8,128)(2,1)} %pad_maximum_fusion.2), calls=%async_computation.1 | async-start | bytes 3145728 | tf_op jit(solution)/shard_map/all_to_all | solution.py:38
  53.6 10.7 %collective-permute-start.10 = (bf16[256,1024]{1,0:T(8,128)(2,1)S(1)}, bf16[256,1024]{1,0:T(8,128)(2,1)S(1)}, u32[]{:S(2)}, u32[]{:S(2)}) collective-permute-start(bf16[256,1024]{1,0:T(8,128)(2,1)S(1)} %slice.159), channel_id=1, source_target_pairs={{0,16},{16,32},{32,48},{48,0},{1,17},{17,33},{33,49},{49,1},{2,18}... | collective-permute-start | bytes 1572872 | tf_op jit(solution)/shard_map/ppermute | solution.py:16
  54.1 10.2 %collective-permute-start.11 = (bf16[256,1024]{1,0:T(8,128)(2,1)S(1)}, bf16[256,1024]{1,0:T(8,128)(2,1)S(1)}, u32[]{:S(2)}, u32[]{:S(2)}) collective-permute-start(bf16[256,1024]{1,0:T(8,128)(2,1)S(1)} %slice.160), channel_id=1, source_target_pairs={{0,48},{16,0},{32,16},{48,32},{1,49},{17,1},{33,17},{49,33},{2,50}... | collective-permute-start | bytes 1572872 | tf_op jit(solution)/shard_map/ppermute | solution.py:16
  57.6 18.4 %collective-permute-start.8 = (bf16[64,512]{1,0:T(8,128)(2,1)S(1)}, bf16[64,512]{1,0:T(8,128)(2,1)S(1)}, u32[]{:S(2)}, u32[]{:S(2)}) collective-permute-start(bf16[64,512]{1,0:T(8,128)(2,1)S(1)} %select_convert_fusion), channel_id=1, source_target_pairs={{0,2},{2,0},{1,3},{3,1},{4,6},{6,4},{5,7},{7,5},{8,10},{10,8},{9,1... | collective-permute-start | bytes 196616 | tf_op jit(solution)/shard_map/ppermute | solution.py:16
  71.8 16.6 %all-to-all-start.2 = ((bf16[8,128,512]{2,1,0:T(8,128)(2,1)}), bf16[8,128,512]{2,1,0:T(8,128)(2,1)}, u32[]{:S(2)}, u32[]{:S(2)}) async-start(bf16[8,128,512]{2,1,0:T(8,128)(2,1)} %bitcast.105), calls=%async_computation.2 | async-start | bytes 2097152 | tf_op jit(solution)/shard_map/all_to_all | solution.py:38
  77.4 17.0 %collective-permute-start.14 = (bf16[64,512]{1,0:T(8,128)(2,1)}, bf16[64,512]{1,0:T(8,128)(2,1)S(1)}, u32[]{:S(2)}, u32[]{:S(2)}) collective-permute-start(bf16[64,512]{1,0:T(8,128)(2,1)} %slice.163), channel_id=1, source_target_pairs={{0,80},{16,96},{32,112},{48,64},{64,16},{80,32},{96,48},{112,0},{1... | collective-permute-start | bytes 196616 | tf_op jit(solution)/shard_map/ppermute | solution.py:29
  78.9 18.5 %collective-permute-start.12 = (bf16[64,512]{1,0:T(8,128)(2,1)S(1)}, bf16[64,512]{1,0:T(8,128)(2,1)S(1)}, u32[]{:S(2)}, u32[]{:S(2)}) collective-permute-start(bf16[64,512]{1,0:T(8,128)(2,1)S(1)} %get-tuple-element.81), channel_id=1, source_target_pairs={{0,16},{16,32},{32,48},{48,0},{64,80},{80,96},{96,112},{112,64},{1... | collective-permute-start | bytes 196616 | tf_op jit(solution)/shard_map/ppermute | solution.py:29
  88.4 11.2 %collective-permute-start.22 = (bf16[64,1024]{1,0:T(8,128)(2,1)S(1)}, bf16[64,1024]{1,0:T(8,128)(2,1)S(1)}, u32[]{:S(2)}, u32[]{:S(2)}) collective-permute-start(bf16[64,1024]{1,0:T(8,128)(2,1)S(1)} %convert_element_type.148), channel_id=1, source_target_pairs={{0,4},{4,8},{8,12},{12,0},{1,5},{5,9},{9,13},{13,1},{2,6},{6,10},{... | collective-permute-start | bytes 393224 | tf_op jit(solution)/shard_map/ppermute | solution.py:16
  88.9 13.3 %collective-permute-start.23 = (bf16[64,1024]{1,0:T(8,128)(2,1)S(1)}, bf16[64,1024]{1,0:T(8,128)(2,1)S(1)}, u32[]{:S(2)}, u32[]{:S(2)}) collective-permute-start(bf16[64,1024]{1,0:T(8,128)(2,1)S(1)} %convert_element_type.148), channel_id=1, source_target_pairs={{0,8},{4,12},{8,0},{12,4},{1,9},{5,13},{9,1},{13,5},{2,10},{6,14},... | collective-permute-start | bytes 393224 | tf_op jit(solution)/shard_map/ppermute | solution.py:16
  90.9 11.4 %collective-permute-start.24 = (bf16[64,1024]{1,0:T(8,128)(2,1)S(1)}, bf16[64,1024]{1,0:T(8,128)(2,1)S(1)}, u32[]{:S(2)}, u32[]{:S(2)}) collective-permute-start(bf16[64,1024]{1,0:T(8,128)(2,1)S(1)} %convert_element_type.148), channel_id=1, source_target_pairs={{0,12},{4,0},{8,4},{12,8},{1,13},{5,1},{9,5},{13,9},{2,14},{6,2},{... | collective-permute-start | bytes 393224 | tf_op jit(solution)/shard_map/ppermute | solution.py:16
  97.4 7.0 %collective-permute-start.13 = (bf16[64,2048]{1,0:T(8,128)(2,1)S(1)}, bf16[64,2048]{1,0:T(8,128)(2,1)S(1)}, u32[]{:S(2)}, u32[]{:S(2)}) collective-permute-start(bf16[64,2048]{1,0:T(8,128)(2,1)S(1)} %pad_maximum_fusion.11), channel_id=1, source_target_pairs={{0,2},{2,0},{1,3},{3,1},{4,6},{6,4},{5,7},{7,5},{8,10},{10,8},{9,1... | collective-permute-start | bytes 786440 | tf_op jit(solution)/shard_map/ppermute | solution.py:16
  99.5 6.9 %collective-permute-start.16 = (bf16[2,64,1152]{2,1,0:T(8,128)(2,1)S(1)}, bf16[2,64,1152]{2,1,0:T(8,128)(2,1)S(1)}, u32[]{:S(2)}, u32[]{:S(2)}) collective-permute-start(bf16[2,64,1152]{2,1,0:T(8,128)(2,1)S(1)} %maximum_maximum_fusion), channel_id=1, source_target_pairs={{0,12},{4,0},{8,4},{12,8},{1,13},{5,1},{9,5},{13,9},{2,14},{6,2},{... | collective-permute-start | bytes 884744 | tf_op jit(solution)/shard_map/ppermute | solution.py:16
  102.3 14.3 %collective-permute-start.25 = (bf16[4,64,1024]{2,1,0:T(8,128)(2,1)S(1)}, bf16[4,64,1024]{2,1,0:T(8,128)(2,1)S(1)}, u32[]{:S(2)}, u32[]{:S(2)}) collective-permute-start(bf16[4,64,1024]{2,1,0:T(8,128)(2,1)S(1)} %bitcast_dynamic-update-slice_fusion.6), channel_id=1, source_target_pairs={{0,2},{2,0},{1,3},{3,1},{4,6},{6,4},{5,7},{7,5},{8,10},{10,8},{9,1... | collective-permute-start | bytes 1572872 | tf_op jit(solution)/shard_map/ppermute | solution.py:16
  106.3 9.9 %collective-permute-start.27 = (bf16[64,1152]{1,0:T(8,128)(2,1)S(1)}, bf16[64,1152]{1,0:T(8,128)(2,1)S(1)}, u32[]{:S(2)}, u32[]{:S(2)}) collective-permute-start(bf16[64,1152]{1,0:T(8,128)(2,1)S(1)} %slice_bitcast_fusion.2), channel_id=1, source_target_pairs={{0,4},{4,8},{8,12},{12,0},{1,5},{5,9},{9,13},{13,1},{2,6},{6,10},{... | collective-permute-start | bytes 442376 | tf_op jit(solution)/shard_map/ppermute | solution.py:16
  112.8 13.1 %collective-permute-start.18 = (bf16[2,64,2048]{2,1,0:T(8,128)(2,1)S(1)}, bf16[2,64,2048]{2,1,0:T(8,128)(2,1)S(1)}, u32[]{:S(2)}, u32[]{:S(2)}) collective-permute-start(bf16[2,64,2048]{2,1,0:T(8,128)(2,1)S(1)} %pad_maximum_fusion.10), channel_id=1, source_target_pairs={{0,4},{4,8},{8,12},{12,0},{1,5},{5,9},{9,13},{13,1},{2,6},{6,10},{... | collective-permute-start | bytes 1572872 | tf_op jit(solution)/shard_map/ppermute | solution.py:16
  112.8 13.2 %collective-permute-start.19 = (bf16[2,64,2048]{2,1,0:T(8,128)(2,1)S(1)}, bf16[2,64,2048]{2,1,0:T(8,128)(2,1)S(1)}, u32[]{:S(2)}, u32[]{:S(2)}) collective-permute-start(bf16[2,64,2048]{2,1,0:T(8,128)(2,1)S(1)} %pad_maximum_fusion.10), channel_id=1, source_target_pairs={{0,12},{4,0},{8,4},{12,8},{1,13},{5,1},{9,5},{13,9},{2,14},{6,2},{... | collective-permute-start | bytes 1572872 | tf_op jit(solution)/shard_map/ppermute | solution.py:16
  123.4 20.3 %collective-permute-start.31 = (bf16[512,1024]{1,0:T(8,128)(2,1)S(1)}, bf16[512,1024]{1,0:T(8,128)(2,1)S(1)}, u32[]{:S(2)}, u32[]{:S(2)}) collective-permute-start(bf16[512,1024]{1,0:T(8,128)(2,1)S(1)} %add_convert_fusion), channel_id=1, source_target_pairs={{0,64},{64,0},{1,65},{65,1},{2,66},{66,2},{3,67},{67,3},{4,68},{68... | collective-permute-start | bytes 3145736 | tf_op jit(solution)/shard_map/ppermute | solution.py:16
  125.9 9.5 %collective-permute-start.20 = (bf16[64,2048]{1,0:T(8,128)(2,1)S(1)}, bf16[64,2048]{1,0:T(8,128)(2,1)S(1)}, u32[]{:S(2)}, u32[]{:S(2)}) collective-permute-start(bf16[64,2048]{1,0:T(8,128)(2,1)S(1)} %slice_bitcast_fusion.1), channel_id=1, source_target_pairs={{0,4},{4,8},{8,12},{12,0},{1,5},{5,9},{9,13},{13,1},{2,6},{6,10},{... | collective-permute-start | bytes 786440 | tf_op jit(solution)/shard_map/ppermute | solution.py:16
  126.0 9.4 %collective-permute-start.21 = (bf16[64,2048]{1,0:T(8,128)(2,1)S(1)}, bf16[64,2048]{1,0:T(8,128)(2,1)S(1)}, u32[]{:S(2)}, u32[]{:S(2)}) collective-permute-start(bf16[64,2048]{1,0:T(8,128)(2,1)S(1)} %slice_bitcast_fusion), channel_id=1, source_target_pairs={{0,12},{4,0},{8,4},{12,8},{1,13},{5,1},{9,5},{13,9},{2,14},{6,2},{... | collective-permute-start | bytes 786440 | tf_op jit(solution)/shard_map/ppermute | solution.py:16
  144.8 12.3 %collective-permute-start.33 = (bf16[512,512]{1,0:T(8,128)(2,1)S(1)}, bf16[512,512]{1,0:T(8,128)(2,1)S(1)}, u32[]{:S(2)}, u32[]{:S(2)}) collective-permute-start(bf16[512,512]{1,0:T(8,128)(2,1)S(1)} %slice.174), channel_id=1, source_target_pairs={{0,1},{1,0},{2,3},{3,2},{4,5},{5,4},{6,7},{7,6},{8,9},{9,8},{10,11... | collective-permute-start | bytes 1572872 | tf_op jit(solution)/shard_map/ppermute | solution.py:16
  (32 other events, 180.3 us)
